TPU v7x, 32 devices: a whole 2x2x4 slice. The times are simulated.
32 devices in a mesh: tok: 4 (over z), exp: 8 (over y, x, core).
Axes of the slice: x: 2, y: 2, z: 4, core: 2. Of those that a mesh axis runs over, the one named last changes fastest.
Arguments:
- x_rows: bfloat16 [768, 4096], P(('tok', 'exp')), may hold values from -6 to 6
- routes: int32 [768, 8], P(('tok', 'exp')), may hold values from 0 to 31, all different within a row; in each aligned block of 24 rows (0 to 23, 24 to 47, ...) at most 7 rows name the same one
- base_weight: bfloat16 [32, 1536, 4096], P('exp', 'tok'), may hold values from -6 to 6
- keep_mask: int32 [32, 24, 64], P('exp', 'tok'), may hold values 0 or 1
- dual_start: float32 [32, 1536, 4096], P('exp', 'tok'), may hold values from -4 to 4
Outputs:
- weight: float32 [32, 1536, 4096], P('exp', 'tok')
- dual: float32 [32, 1536, 4096], P('exp', 'tok')
Inputs may be any that keep to these rules, and one draw needn't show every extreme that they name: `routes`: each row names 8 different experts; among the rows of one device no expert is named more than 7 times, a bound that some block reaches; every expert is named by at least one token.
All inputs are finite; a program needn't handle non-finite values. No bound on the sum of `keep_mask` on one device may be relied on, other than what follows from the above.
Results may differ from a plain program's by a relative error of at most 0.0027.
Values may be sent and summed in bfloat16 or wider, within the bound.
No kernel may reach another device: no remote copies, remote signals or barrier semaphores. Data moves between devices by JAX's collectives and lax.ppermute only.
A program may use at most 192 MiB of HBM per device.

v0:
```python
import functools

import jax
import jax.numpy as jnp
from jax import lax
from jax.experimental import pallas as pl
from jax.experimental.pallas import tpu as pltpu
from jax.sharding import PartitionSpec as P

EXPERTS = 32
BLOCK = 64
ROWS_BLOCK = 24
MOST = 7
LANES = 128

step_rate = 0.2

F32 = jnp.float32
BF16 = jnp.bfloat16


def dot_nn(a, b):
    return jnp.dot(a, b, preferred_element_type=F32)


def dot_nt(a, b):
    return lax.dot_general(a, b, (((1,), (1,)), ((), ())), preferred_element_type=F32)


def kernel(
    chunk, width, topk, first_ref, x_ref, base_ref, dual_ref, mask_ref,
    weight_out, dual_out, rows, rank, hits, scale,
):
    expert, tile = pl.program_id(0), pl.program_id(1)
    tokens = x_ref.shape[0]
    slots = rows.shape[0]
    count_here = hits.shape[0]
    tall = base_ref.shape[1]
    cuts = [pl.ds(start, chunk) for start in range(0, width, chunk)]

    @pl.when((expert == 0) & (tile == 0))
    def _():
        named = x_ref[:, pl.ds(width, LANES)].astype(F32).T[:topk, :]
        for own in range(count_here):
            label = (first_ref[0] + own).astype(F32)
            hit = jnp.max(jnp.where(named == label, 1.0, 0.0), axis=0, keepdims=True)
            hits[own : own + 1, :] = hit
        earlier = lax.broadcasted_iota(jnp.int32, (tokens, tokens), 0)
        later = lax.broadcasted_iota(jnp.int32, (tokens, tokens), 1)
        ahead = jnp.where(earlier < later, 1.0, 0.0).astype(BF16)
        rank[...] = dot_nn(hits[...].astype(BF16), ahead)

    @pl.when(tile == 0)
    def _():
        hit = hits[pl.ds(expert, 1), :]
        place = rank[pl.ds(expert, 1), :]
        slot = lax.broadcasted_iota(jnp.int32, (slots, tokens), 0).astype(F32)
        taken = jnp.where((slot == place) & (hit > 0.5), 1.0, 0.0).astype(BF16)
        for cut in cuts:
            rows[:, cut] = dot_nn(taken, x_ref[:, cut]).astype(BF16)
        total = jnp.sum(hit, axis=1, keepdims=True)
        scale[...] = jnp.broadcast_to(step_rate / total, scale.shape)

    rate = scale[0:1, 0:1]
    parts = [slice(start, start + BLOCK) for start in range(0, tall, BLOCK)]

    resid = jnp.zeros((tall, slots), F32)
    for cut in cuts:
        delta = jnp.concatenate(
            [base_ref[0, part, cut] * (mask_ref[0, 0, i : i + 1, cut] - 1.0).astype(BF16) for i, part in enumerate(parts)],
            axis=0,
        )
        resid = resid + dot_nt(delta, rows[:, cut])
    resid = resid.astype(BF16)

    after = jnp.zeros((tall, slots), F32)
    for cut in cuts:
        grad = dot_nn(resid, rows[:, cut])
        deltas = []
        for i, part in enumerate(parts):
            keep = mask_ref[0, 0, i : i + 1, cut]
            base = base_ref[0, part, cut].astype(F32)
            weight = keep * base - step_rate * dual_ref[0, part, cut] - rate * grad[part, :]
            weight_out[0, part, cut] = weight
            deltas.append((weight - base).astype(BF16))
        after = after + dot_nt(jnp.concatenate(deltas, axis=0), rows[:, cut])
    resid = after.astype(BF16)

    for cut in cuts:
        grad = dot_nn(resid, rows[:, cut])
        for i, part in enumerate(parts):
            keep = mask_ref[0, 0, i : i + 1, cut]
            weight = weight_out[0, part, cut]
            both = weight + dual_ref[0, part, cut]
            weight = (1.0 - step_rate) * weight - (step_rate - 2.0 * step_rate * keep) * both - rate * grad[part, :]
            weight_out[0, part, cut] = weight
            dual_out[0, part, cut] = (1.0 - keep) * (both + weight)


def fused(first, gathered, base_weight, mask, dual_start, topk, tall):
    local, hidden, width = base_weight.shape
    tokens = gathered.shape[0]
    slots = -(-tokens // ROWS_BLOCK) * MOST
    slots = -(-min(slots, tokens) // 16) * 16
    tiles = hidden // tall
    block = pl.BlockSpec((1, tall, width), lambda e, t: (e, t, 0))
    out = jax.ShapeDtypeStruct(dual_start.shape, F32)
    macs = local * slots * width * (4 * hidden + tokens)
    return pl.pallas_call(
        functools.partial(kernel, 512, width, topk),
        grid=(local, tiles),
        in_specs=[
            pl.BlockSpec(memory_space=pltpu.SMEM),
            pl.BlockSpec(gathered.shape, lambda e, t: (0, 0), pipeline_mode=pl.Buffered(1)),
            block,
            block,
            pl.BlockSpec((1, 1, tall // BLOCK, width), lambda e, t: (e, t, 0, 0)),
        ],
        out_specs=[block, block],
        out_shape=[out, out],
        scratch_shapes=[
            pltpu.VMEM((slots, width), BF16),
            pltpu.VMEM((local, tokens), F32),
            pltpu.VMEM((local, tokens), F32),
            pltpu.VMEM((8, LANES), F32),
        ],
        compiler_params=pltpu.CompilerParams(
            vmem_limit_bytes=60 * 1024 * 1024,
            dimension_semantics=("arbitrary", "arbitrary"),
        ),
        cost_estimate=pl.CostEstimate(flops=2 * macs, bytes_accessed=14 * base_weight.size + 2 * gathered.size, transcendentals=0),
    )(first, gathered, base_weight, dual_start, mask)


def on_device(x_rows, routes, base_weight, keep_mask, dual_start):
    local, hidden, width = base_weight.shape
    topk = routes.shape[1]
    tall = 3 * BLOCK
    with jax.named_scope("gather_rows"):
        named = jnp.pad(routes.astype(BF16), ((0, 0), (0, LANES - topk)))
        own = jnp.concatenate([x_rows, named], axis=1)
        gathered = lax.all_gather(own, ("tok", "exp"), axis=0, tiled=True)
    mask = jnp.repeat(keep_mask.astype(F32), BLOCK, 2)
    mask = mask.reshape(local, hidden // tall, tall // BLOCK, width)
    first = (lax.axis_index("exp") * local).astype(jnp.int32).reshape(1)
    with jax.named_scope("fused_iterations"):
        return fused(first, gathered, base_weight, mask, dual_start, topk, tall)


def solution(mesh):
    return jax.shard_map(
        on_device,
        mesh=mesh,
        in_specs=(
            P(("tok", "exp"), None),
            P(("tok", "exp"), None),
            P("exp", "tok", None),
            P("exp", "tok", None),
            P("exp", "tok", None),
        ),
        out_specs=(P("exp", "tok", None), P("exp", "tok", None)),
        check_vma=False,
    )
```

profile of v0, /device:TPU:0, one launch (start us, length us, event | category | flops | bytes accessed | tf_op | source)
XLA Modules:
  0.0 138.4 jit_solution(430852748621725687)
XLA Ops:
  7.2 0.0 all-gather.2.cloned.1.call-start
  7.2 0.7 convert_element_type.8
  7.9 0.1 copy.11
  8.0 1.6 %fusion.1 = bf16[24,4224]{1,0:T(8,128)(2,1)} fusion(bf16[24,8]{1,0:T(8,128)(2,1)S(1)} %copy.11, bf16[24,4096]{1,0:T(8,128)(2,1)} %param.5), kind=kLoop, calls=%fused_computation.2 | loop fusion | flops 608256 | bytes 399744 | tf_op jit(solution)/shard_map/gather_rows/concatenate | solution.py:141
  9.6 0.0 all-gather.2.cloned.1.call-update
  9.6 0.7 convert_element_type.9
  10.4 0.3 broadcast_in_dim.3
  10.6 0.3 reshape_reshape.3
  10.9 1.1 copy.12.mask_ref
  12.0 72.5 %all-gather.2.cloned.1.call-done.x_ref = bf16[768,4224]{1,0:T(8,128)(2,1)} async-done(((bf16[24,4224]{1,0:T(8,128)(2,1)}), bf16[768,4224]{1,0:T(8,128)(2,1)}) %all-gather.2.cloned.1.call-update) | async-done | bytes 6488080 | tf_op jit(solution)/shard_map/gather_rows/all_gather | solution.py:142
  84.5 47.1 %fused_iterations.1 = (f32[4,384,4096]{2,1,0:T(8,128)}, f32[4,384,4096]{2,1,0:T(8,128)}) custom-call(s32[1]{0:T(128)} %bitcast.first_ref, bf16[768,4224]{1,0:T(8,128)(2,1)} %all-gather.2.cloned.1.call-done.x_ref, bf16[4,384,4096]{2,1,0:T(8,128)(2,1)} %base_ref.1, f32[4,384,4096]{2,1,0:T(8,128)} %dual_ref.1, f32[4,2,3,4096]{3,2,1,0:T(4,128)} %copy.12.mask_ref), custom_call_target="tpu_custom_call" | custom-call | flops 16911433728 | bytes 94568448 | tf_op jit(solution)/shard_map/fused_iterations/pallas_call | solution.py:109
Async XLA Ops:
  7.2 77.3 %all-gather.2.cloned.1.call-start = ((), (), s32[]{:S(2)}) async-start(), calls=%async_computation | async-start | bytes 6690816 | tf_op jit(solution)/shard_map/gather_rows/all_gather | solution.py:142
Sparse Core Ops, SparseCore 0:
  11.4 73.0 all-gather.1
where the time goes:
time: 139 us; the launch traced here: 138 us
  waiting for transfers between devices  72.5 us (52%)
  Pallas kernels  47.1 us (34%)
  between operations  14 us (10%)
  other arithmetic  3.02 us (2%)
  local copies, waits for them, and re-layouts  1.74 us (1%)
    all_gather x1, waiting for transfers between devices, on_device(): gathered = lax.all_gather(own, ('tok', 'exp'), axis=0, tiled=True)  72.5 us
    pallas_call x1, Pallas kernels, fused(): pl.pallas_call(functools.partial(kernel, 512, width, topk), grid=(local,...  47.1 us
  transfers between devices with their start and end apart: 1, of which 1 were waited for; matrix products, arithmetic and copies ran while one was open for 2% of the time, Pallas kernels for 0%

commit v1 on v0

v1 whole, which is shorter than its diff:
```python
import functools

import jax
import jax.numpy as jnp
from jax import lax
from jax.experimental import pallas as pl
from jax.experimental.pallas import tpu as pltpu
from jax.sharding import PartitionSpec as P

EXPERTS = 32
BLOCK = 64
ROWS_BLOCK = 24
MOST = 7
LANES = 128
MIB = 1024 * 1024

step_rate = 0.2

F32 = jnp.float32
BF16 = jnp.bfloat16


def dot_nn(a, b):
    return jnp.dot(a, b, preferred_element_type=F32)


def dot_nt(a, b):
    return lax.dot_general(a, b, (((1,), (1,)), ((), ())), preferred_element_type=F32)


def cuts_of(width, chunk):
    return [pl.ds(start, chunk) for start in range(0, width, chunk)]


def pack_kernel(n_pieces, half, topk, chunk, *refs):
    pieces, refs = refs[:n_pieces], refs[n_pieces:]
    if half == 0:
        first_ref, base_ref, mask_ref, rows_out, resid_out, hits, rank, rate_out, gathered, sems = refs
    else:
        hits, rank, part_ref, base_ref, mask_ref, rows_out, resid_out, gathered, sems = refs
    expert = pl.program_id(0)
    tokens = gathered.shape[0]
    slots, width = rows_out.shape[1], rows_out.shape[2]
    local = hits.shape[0]
    tall = base_ref.shape[1]
    piece_rows = tokens // n_pieces

    @pl.when(expert == 0)
    def _():
        copies = [
            pltpu.make_async_copy(piece, gathered.at[pl.ds(i * piece_rows, piece_rows), :], sems.at[i])
            for i, piece in enumerate(pieces)
        ]
        for copy in copies:
            copy.start()
        for copy in copies:
            copy.wait()
        if half == 0:
            named = gathered[:, pl.ds(width, LANES)].astype(F32).T[:topk, :]
            for own in range(local):
                label = (first_ref[0] + own).astype(F32)
                hit = jnp.max(jnp.where(named == label, 1.0, 0.0), axis=0, keepdims=True)
                hits[own : own + 1, :] = hit
                total = jnp.sum(hit, axis=1, keepdims=True)
                rate_out[own : own + 1, :] = jnp.broadcast_to(step_rate / total, (1, LANES))
            earlier = lax.broadcasted_iota(jnp.int32, (tokens, tokens), 0)
            later = lax.broadcasted_iota(jnp.int32, (tokens, tokens), 1)
            ahead = jnp.where(earlier < later, 1.0, 0.0).astype(BF16)
            rank[...] = dot_nn(hits[...].astype(BF16), ahead)

    hit = hits[pl.ds(expert, 1), :]
    place = rank[pl.ds(expert, 1), :]
    slot = lax.broadcasted_iota(jnp.int32, (slots, tokens), 0).astype(F32)
    taken = jnp.where((slot == place) & (hit > 0.5), 1.0, 0.0).astype(BF16)
    resid = jnp.zeros((tall, slots), F32) if half == 0 else part_ref[0]
    for cut in cuts_of(width, chunk):
        rows = dot_nn(taken, gathered[:, cut]).astype(BF16)
        rows_out[0, :, cut] = rows
        delta = jnp.concatenate(
            [
                base_ref[0, start : start + BLOCK, cut] * (mask_ref[0, i : i + 1, cut] - 1.0).astype(BF16)
                for i, start in enumerate(range(0, tall, BLOCK))
            ],
            axis=0,
        )
        resid = resid + dot_nt(delta, rows)
    resid_out[0] = resid.astype(resid_out.dtype)


def pack(half, halves, pieces, extra, base_weight, mask, slots, topk):
    local, hidden, width = base_weight.shape
    part = width // halves
    n_pieces = len(pieces)
    piece_rows, piece_width = pieces[0].shape
    tokens = n_pieces * piece_rows
    last = half == halves - 1
    small = pl.BlockSpec((local, tokens), lambda e: (0, 0))
    resid = pl.BlockSpec((1, hidden, slots), lambda e: (e, 0, 0))
    in_specs = [pl.BlockSpec(memory_space=pl.ANY)] * n_pieces
    if half == 0:
        in_specs += [pl.BlockSpec(memory_space=pltpu.SMEM)]
    else:
        in_specs += [small, small, resid]
    in_specs += [
        pl.BlockSpec((1, hidden, part), lambda e: (e, 0, half)),
        pl.BlockSpec((1, hidden // BLOCK, part), lambda e: (e, 0, half)),
    ]
    out_specs = [pl.BlockSpec((1, slots, part), lambda e: (e, 0, 0)), resid]
    out_shape = [
        jax.ShapeDtypeStruct((local, slots, part), BF16),
        jax.ShapeDtypeStruct((local, hidden, slots), BF16 if last else F32),
    ]
    if half == 0:
        out_specs += [small, small, pl.BlockSpec((local, LANES), lambda e: (0, 0))]
        out_shape += [jax.ShapeDtypeStruct((local, tokens), F32)] * 2
        out_shape += [jax.ShapeDtypeStruct((local, LANES), F32)]
    macs = local * slots * part * (hidden + tokens)
    return pl.pallas_call(
        functools.partial(pack_kernel, n_pieces, half, topk, 512),
        grid=(local,),
        in_specs=in_specs,
        out_specs=out_specs,
        out_shape=out_shape,
        scratch_shapes=[pltpu.VMEM((tokens, piece_width), BF16), pltpu.SemaphoreType.DMA((n_pieces,))],
        compiler_params=pltpu.CompilerParams(vmem_limit_bytes=48 * MIB, dimension_semantics=("arbitrary",)),
        cost_estimate=pl.CostEstimate(
            flops=2 * macs, bytes_accessed=2 * (tokens + local * (slots + hidden)) * part, transcendentals=0
        ),
    )(*pieces, *extra, base_weight, mask)


def main_kernel(halves, chunk, rate_ref, resid_ref, *refs):
    rows_refs, (base_ref, dual_ref, mask_ref, weight_out, dual_out) = refs[:halves], refs[halves:]
    tall = base_ref.shape[1]
    slots, part_width = rows_refs[0].shape[1:]
    rate = rate_ref[pl.ds(pl.program_id(0), 1), 0:1]
    parts = [slice(start, start + BLOCK) for start in range(0, tall, BLOCK)]
    cuts = [
        (rows_refs[h], cut, pl.ds(h * part_width + cut.start, chunk))
        for h in range(halves)
        for cut in cuts_of(part_width, chunk)
    ]

    resid = resid_ref[0]
    after = jnp.zeros((tall, slots), F32)
    for rows, here, cut in cuts:
        grad = dot_nn(resid, rows[0, :, here])
        deltas = []
        for i, part in enumerate(parts):
            keep = mask_ref[0, 0, i : i + 1, cut]
            base = base_ref[0, part, cut].astype(F32)
            weight = keep * base - step_rate * dual_ref[0, part, cut] - rate * grad[part, :]
            weight_out[0, part, cut] = weight
            deltas.append((weight - base).astype(BF16))
        after = after + dot_nt(jnp.concatenate(deltas, axis=0), rows[0, :, here])
    resid = after.astype(BF16)

    for rows, here, cut in cuts:
        grad = dot_nn(resid, rows[0, :, here])
        for i, part in enumerate(parts):
            keep = mask_ref[0, 0, i : i + 1, cut]
            weight = weight_out[0, part, cut]
            both = weight + dual_ref[0, part, cut]
            weight = (1.0 - step_rate) * weight - (step_rate - 2.0 * step_rate * keep) * both - rate * grad[part, :]
            weight_out[0, part, cut] = weight
            dual_out[0, part, cut] = (1.0 - keep) * (both + weight)


def iterate(rate, resid, rows, base_weight, mask, dual_start, tall):
    local, hidden, width = base_weight.shape
    slots, part = rows[0].shape[1:]
    tiles = hidden // tall
    block = pl.BlockSpec((1, tall, width), lambda e, t: (e, t, 0))
    out = jax.ShapeDtypeStruct(dual_start.shape, F32)
    macs = local * slots * width * 3 * hidden
    mask = mask.reshape(local, tiles, tall // BLOCK, width)
    return pl.pallas_call(
        functools.partial(main_kernel, len(rows), 512),
        grid=(local, tiles),
        in_specs=[pl.BlockSpec(rate.shape, lambda e, t: (0, 0)), pl.BlockSpec((1, tall, slots), lambda e, t: (e, t, 0))]
        + [pl.BlockSpec((1, slots, part), lambda e, t: (e, 0, 0)) for _ in rows]
        + [block, block, pl.BlockSpec((1, 1, tall // BLOCK, width), lambda e, t: (e, t, 0, 0))],
        out_specs=[block, block],
        out_shape=[out, out],
        compiler_params=pltpu.CompilerParams(
            vmem_limit_bytes=56 * MIB, dimension_semantics=("arbitrary", "arbitrary")
        ),
        cost_estimate=pl.CostEstimate(flops=2 * macs, bytes_accessed=14 * base_weight.size, transcendentals=0),
    )(rate, resid, *rows, base_weight, dual_start, mask)


def spread(own, bits):
    n_tok, n_exp = lax.axis_size("tok"), lax.axis_size("exp")
    column = [own]
    for shift in range(1, n_tok):
        column.append(lax.ppermute(own, "tok", [(i, (i + shift) % n_tok) for i in range(n_tok)]))
    pieces = {0: jnp.concatenate(column, axis=0)}
    for bit in bits:
        swap = [(i, i ^ (1 << bit)) for i in range(n_exp)]
        pieces.update({at ^ (1 << bit): lax.ppermute(piece, "exp", swap) for at, piece in pieces.items()})
    return [pieces[i] for i in range(n_exp)]


def on_device(x_rows, routes, base_weight, keep_mask, dual_start):
    local, hidden, width = base_weight.shape
    topk = routes.shape[1]
    n_tok, n_exp = lax.axis_size("tok"), lax.axis_size("exp")
    tokens = n_tok * n_exp * x_rows.shape[0]
    slots = -(-tokens // ROWS_BLOCK) * MOST
    slots = -(-min(slots, tokens) // 16) * 16
    halves = 2
    part = width // halves
    top = n_exp.bit_length() - 1
    assert 1 << top == n_exp
    named = jnp.pad(routes.astype(BF16), ((0, 0), (0, LANES - topk)))
    sent = [x_rows[:, h * part : (h + 1) * part] for h in range(halves)]
    sent[0] = jnp.concatenate([sent[0], named], axis=1)
    orders = [list(range(1, top)) + [0], list(range(1, top))[::-1] + [0]]
    with jax.named_scope("exchange_rows"):
        pieces = [spread(own, orders[h % 2]) for h, own in enumerate(sent)]
    mask = jnp.repeat(keep_mask.astype(F32), BLOCK, 2)
    first = (lax.axis_index("exp") * local).astype(jnp.int32).reshape(1)
    rows = []
    with jax.named_scope("pack_rows"):
        part_rows, resid, hits, rank, rate = pack(0, halves, pieces[0], [first], base_weight, mask, slots, topk)
        rows.append(part_rows)
        for h in range(1, halves):
            part_rows, resid = pack(h, halves, pieces[h], [hits, rank, resid], base_weight, mask, slots, topk)
            rows.append(part_rows)
    with jax.named_scope("iterations"):
        return iterate(rate, resid, rows, base_weight, mask, dual_start, 3 * BLOCK)


def solution(mesh):
    return jax.shard_map(
        on_device,
        mesh=mesh,
        in_specs=(
            P(("tok", "exp"), None),
            P(("tok", "exp"), None),
            P("exp", "tok", None),
            P("exp", "tok", None),
            P("exp", "tok", None),
        ),
        out_specs=(P("exp", "tok", None), P("exp", "tok", None)),
        check_vma=False,
    )
```

time: 139 us -> 126 us (0.906)
  waiting for transfers between devices: 72.5 us -> 31.4 us
  starting transfers between devices: 0.04 us -> 18.8 us
  Pallas kernels: 47.1 us -> 61.2 us
  between operations: 14 us -> 0.77 us
  local copies, waits for them, and re-layouts: 1.74 us -> 11.7 us
  other arithmetic: 3.02 us -> 1.47 us
    all_gather x1 -> x0, waiting for transfers between devices: 72.5 us -> none  [on_device(): gathered = lax.all_gather(own, ('tok', 'exp'), axis=0, tiled=True)]
    ppermute x0 -> x20, waiting for transfers between devices: none -> 31.4 us  [the longest x14 23.2 us: spread(): lax.ppermute(piece, 'exp', swap)]
    ppermute x0 -> x20, starting transfers between devices: none -> 18.8 us  [the longest x6 10.5 us: spread(): lax.ppermute(own, 'tok', [(i, (i + shift) % n_tok) for i in range(n_tok)])]
    pallas_call x1 -> x3, Pallas kernels: 47.1 us -> 61.2 us  [the longest x1 39.2 us: iterate(): pl.pallas_call(functools.partial(main_kernel, len(rows), 512), grid=(loca...]
    reshape x0 -> x2, local copies, waits for them, and re-layouts: none -> 3.43 us  [on_device(): mask = jnp.repeat(keep_mask.astype(F32), BLOCK, 2)]
    another operation x2, local copies, waits for them, and re-layouts: 1.4 us -> 4.33 us  [iterate(): mask = mask.reshape(local, tiles, tall // BLOCK, width)]
    unnamed x0 -> x8, local copies, waits for them, and re-layouts: none -> 1.7 us
    concatenate x1 -> x3, other arithmetic: 1.62 us -> 0.07 us  [the longest x2 0.06 us: spread(): pieces = {0: jnp.concatenate(column, axis=0)}]
  transfers between devices with their start and end apart: 1 -> 20, of which waited for: 1 -> 6; matrix products, arithmetic and copies ran while one was open for 2% -> 8% of each run, Pallas kernels for 0% -> 9%
where the time goes in v1:
time: 126 us; the launch traced here: 125 us
  Pallas kernels  61.2 us (49%)
  waiting for transfers between devices  31.4 us (25%)
  starting transfers between devices  18.8 us (15%)
  local copies, waits for them, and re-layouts  11.7 us (9%)
  other arithmetic  1.47 us (1%)
    pallas_call x1, Pallas kernels, iterate(): pl.pallas_call(functools.partial(main_kernel, len(rows), 512), grid=(loca...  39.2 us
    ppermute x14, waiting for transfers between devices, spread(): lax.ppermute(piece, 'exp', swap)  23.2 us
    pallas_call x2, Pallas kernels, pack(): pl.pallas_call(functools.partial(pack_kernel, n_pieces, half, topk, 512),...  22 us
    ppermute x6, starting transfers between devices, spread(): lax.ppermute(own, 'tok', [(i, (i + shift) % n_tok) for i in range(n_tok)])  10.5 us
    ppermute x14, starting transfers between devices, spread(): lax.ppermute(piece, 'exp', swap)  8.29 us
    ppermute x6, waiting for transfers between devices, spread(): lax.ppermute(own, 'tok', [(i, (i + shift) % n_tok) for i in range(n_tok)])  8.2 us
    another operation x2, local copies, waits for them, and re-layouts, iterate(): mask = mask.reshape(local, tiles, tall // BLOCK, width)  4.33 us
    reshape x2, local copies, waits for them, and re-layouts, on_device(): mask = jnp.repeat(keep_mask.astype(F32), BLOCK, 2)  3.43 us
  transfers between devices with their start and end apart: 20, of which 6 were waited for; matrix products, arithmetic and copies ran while one was open for 8% of the time, Pallas kernels for 9%

profile of v1, /device:TPU:0, one launch (start us, length us, event | category | flops | bytes accessed | tf_op | source)
XLA Modules:
  0.0 125.2 jit_solution(11776507086697222375)
XLA Ops:
  1.4 1.0 fusion
  2.4 5.1 %collective-permute-start.2 = (bf16[24,2176]{1,0:T(8,128)(2,1)S(1)}, bf16[24,2176]{1,0:T(8,128)(2,1)S(1)}, u32[]{:S(2)}, u32[]{:S(2)}) collective-permute-start(bf16[24,2176]{1,0:T(8,128)(2,1)S(1)} %pad_maximum_fusion.2), channel_id=1, source_target_pairs={{0,24},{8,0},{16,8},{24,16},{1,25},{9,1},{17,9},{25,17},{2,26},{10... | collective-permute-start | bytes 313352 | tf_op jit(solution)/shard_map/exchange_rows/ppermute | solution.py:196
  7.5 1.0 collective-permute-start
  8.5 2.3 %collective-permute-done.2 = bf16[24,2176]{1,0:T(8,128)(2,1)S(1)} collective-permute-done((bf16[24,2176]{1,0:T(8,128)(2,1)S(1)}, bf16[24,2176]{1,0:T(8,128)(2,1)S(1)}, u32[]{:S(2)}, u32[]{:S(2)}) %collective-permute-start.2) | collective-permute-done | bytes 104480 | tf_op jit(solution)/shard_map/exchange_rows/ppermute | solution.py:196
  10.8 5.9 %collective-permute-done.1 = bf16[24,2176]{1,0:T(8,128)(2,1)S(1)} collective-permute-done((bf16[24,2176]{1,0:T(8,128)(2,1)S(1)}, bf16[24,2176]{1,0:T(8,128)(2,1)S(1)}, u32[]{:S(2)}, u32[]{:S(2)}) %collective-permute-start.1) | collective-permute-done | bytes 104480 | tf_op jit(solution)/shard_map/exchange_rows/ppermute | solution.py:196
  16.7 1.6 %collective-permute-start.4 = (bf16[96,2176]{1,0:T(8,128)(2,1)S(1)}, bf16[96,2176]{1,0:T(8,128)(2,1)S(1)}, u32[]{:S(2)}, u32[]{:S(2)}) collective-permute-start(bf16[96,2176]{1,0:T(8,128)(2,1)S(1)} %pad_maximum_fusion.refs_0_), channel_id=1, source_target_pairs={{0,2},{1,3},{2,0},{3,1},{4,6},{5,7},{6,4},{7,5},{8,10},{9,11},{10,... | collective-permute-start | bytes 1253384 | tf_op jit(solution)/shard_map/exchange_rows/ppermute | solution.py:200
  18.3 1.9 %collective-permute-start.12 = (bf16[24,2048]{1,0:T(8,128)(2,1)S(1)}, bf16[24,2048]{1,0:T(8,128)(2,1)S(1)}, u32[]{:S(2)}, u32[]{:S(2)}) collective-permute-start(bf16[24,2048]{1,0:T(8,128)(2,1)S(1)} %get-tuple-element.16), channel_id=1, source_target_pairs={{0,24},{8,0},{16,8},{24,16},{1,25},{9,1},{17,9},{25,17},{2,26},{10... | collective-permute-start | bytes 294920 | tf_op jit(solution)/shard_map/exchange_rows/ppermute | solution.py:196
  20.6 2.0 %collective-permute-start.10 = (bf16[24,2048]{1,0:T(8,128)(2,1)S(1)}, bf16[24,2048]{1,0:T(8,128)(2,1)S(1)}, u32[]{:S(2)}, u32[]{:S(2)}) collective-permute-start(bf16[24,2048]{1,0:T(8,128)(2,1)S(1)} %get-tuple-element.16), channel_id=1, source_target_pairs={{0,8},{8,16},{16,24},{24,0},{1,9},{9,17},{17,25},{25,1},{2,10},{10... | collective-permute-start | bytes 294920 | tf_op jit(solution)/shard_map/exchange_rows/ppermute | solution.py:196
  22.7 1.5 %collective-permute-start.6 = (bf16[96,2176]{1,0:T(8,128)(2,1)S(1)}, bf16[96,2176]{1,0:T(8,128)(2,1)S(1)}, u32[]{:S(2)}, u32[]{:S(2)}) collective-permute-start(bf16[96,2176]{1,0:T(8,128)(2,1)S(1)} %pad_maximum_fusion.refs_0_), channel_id=1, source_target_pairs={{0,4},{1,5},{2,6},{3,7},{4,0},{5,1},{6,2},{7,3},{8,12},{9,13},{10,... | collective-permute-start | bytes 1253384 | tf_op jit(solution)/shard_map/exchange_rows/ppermute | solution.py:200
  24.2 3.6 %collective-permute-done.4.refs_2_ = bf16[96,2176]{1,0:T(8,128)(2,1)S(1)} collective-permute-done((bf16[96,2176]{1,0:T(8,128)(2,1)S(1)}, bf16[96,2176]{1,0:T(8,128)(2,1)S(1)}, u32[]{:S(2)}, u32[]{:S(2)}) %collective-permute-start.4) | collective-permute-done | bytes 417824 | tf_op jit(solution)/shard_map/exchange_rows/ppermute | solution.py:200
  27.8 1.5 %collective-permute-start.8 = (bf16[96,2176]{1,0:T(8,128)(2,1)S(1)}, bf16[96,2176]{1,0:T(8,128)(2,1)S(1)}, u32[]{:S(2)}, u32[]{:S(2)}) collective-permute-start(bf16[96,2176]{1,0:T(8,128)(2,1)S(1)} %collective-permute-done.4.refs_2_), channel_id=1, source_target_pairs={{0,4},{1,5},{2,6},{3,7},{4,0},{5,1},{6,2},{7,3},{8,12},{9,13},{10,... | collective-permute-start | bytes 1253384 | tf_op jit(solution)/shard_map/exchange_rows/ppermute | solution.py:200
  29.4 1.1 collective-permute-start.16
  30.5 1.0 collective-permute-start.14
  31.5 3.8 %collective-permute-done.6.refs_4_ = bf16[96,2176]{1,0:T(8,128)(2,1)S(1)} collective-permute-done((bf16[96,2176]{1,0:T(8,128)(2,1)S(1)}, bf16[96,2176]{1,0:T(8,128)(2,1)S(1)}, u32[]{:S(2)}, u32[]{:S(2)}) %collective-permute-start.6) | collective-permute-done | bytes 417824 | tf_op jit(solution)/shard_map/exchange_rows/ppermute | solution.py:200
  35.3 14.6 %collective-permute-done.16.refs_4_ = bf16[96,2048]{1,0:T(8,128)(2,1)} collective-permute-done((bf16[96,2048]{1,0:T(8,128)(2,1)S(1)}, bf16[96,2048]{1,0:T(8,128)(2,1)}, u32[]{:S(2)}, u32[]{:S(2)}) %collective-permute-start.16) | collective-permute-done | bytes 393248 | tf_op jit(solution)/shard_map/exchange_rows/ppermute | solution.py:200
  52.3 1.1 broadcast_in_dim.3
  53.5 2.2 %reshape_reshape.3 = f32[4,2,3,4096]{3,0,2,1:T(4,128)} reshape(f32[4,6,64,64]{3,2,0,1:T(8,128)} %broadcast_in_dim.3) | data formatting | bytes 786432 | tf_op jit(solution)/shard_map/iterations/reshape;reshape | solution.py:176
  55.7 2.2 %reshape.11 = f32[4,6,4096]{2,0,1:T(4,128)} reshape(f32[4,6,64,64]{3,2,0,1:T(8,128)} %broadcast_in_dim.3) | data formatting | bytes 786432 | tf_op jit(solution)/shard_map/reshape | solution.py:221
  57.9 1.2 copy.14.refs_10_.refs_12_
  59.1 2.1 %copy.16.refs_4_ = f32[4,2,3,4096]{3,2,1,0:T(4,128)} copy(f32[4,2,3,4096]{3,0,2,1:T(4,128)} %reshape_reshape.3) | data formatting | bytes 786432 | tf_op jit(solution)/shard_map/iterations/reshape;reshape | solution.py:176
  61.3 1.2 collective-permute-done.18.refs_6_
  63.0 10.9 %pack_rows.2 = (bf16[4,224,2048]{2,1,0:T(8,128)(2,1)}, f32[4,384,224]{2,1,0:T(8,128)S(1)}, f32[4,768]{1,0:T(4,128)S(1)}, f32[4,768]{1,0:T(4,128)S(1)}, f32[4,128]{1,0:T(4,128)S(1)}) custom-call(bf16[96,2176]{1,0:T(8,128)(2,1)S(1)} %pad_maximum_fusion.refs_0_, bf16[96,2176]{1,0:T(8,128)(2,1)S(1)} %collective-permute-done.3.refs_1_, ...), custom_call_target="tpu_custom_call" | custom-call | flops 4227858432 | bytes 13107200 | tf_op jit(solution)/shard_map/pack_rows/pallas_call | solution.py:118
  74.0 11.0 %pack_rows.3 = (bf16[4,224,2048]{2,1,0:T(8,128)(2,1)}, bf16[4,384,224]{2,1,0:T(8,128)(2,1)S(1)}) custom-call(bf16[96,2048]{1,0:T(8,128)(2,1)S(1)} %pad_maximum_fusion.1.refs_0_, bf16[96,2048]{1,0:T(8,128)(2,1)S(1)} %collective-permute-done.13.refs_1_, bf16[96,2048]{1,0:T(8,128)(2,1)S(1)} %copy-done.2, bf16[96,2048]{1,0:T(8,128)(2,1)S(1)} %collective-permute-done.15.refs_3_, ...), custom_call_target="tpu_custom_call" | custom-call | flops 4227858432 | bytes 13107200 | tf_op jit(solution)/shard_map/pack_rows/pallas_call | solution.py:118
  86.0 39.2 %iterations.1 = (f32[4,384,4096]{2,1,0:T(8,128)}, f32[4,384,4096]{2,1,0:T(8,128)}) custom-call(f32[4,128]{1,0:T(4,128)} %copy-done.3, bf16[4,384,224]{2,1,0:T(8,128)(2,1)} %copy-done, bf16[4,224,2048]{2,1,0:T(8,128)(2,1)} %get-tuple-element.14.refs_0_, bf16[4,224,2048]{2,1,0:T(8,128)(2,1)} %get-tuple-element.15.refs_1_, bf16[4,384,4096]{2,1,0:T(8,128)(2,1)} %refs_2_.1, ...), custom_call_target="tpu_custom_call" | custom-call | flops 8455716864 | bytes 88080384 | tf_op jit(solution)/shard_map/iterations/pallas_call | solution.py:177
  (40 shorter events, 5.4 us)
Async XLA Ops:
  2.4 8.4 %collective-permute-start.2 = (bf16[24,2176]{1,0:T(8,128)(2,1)S(1)}, bf16[24,2176]{1,0:T(8,128)(2,1)S(1)}, u32[]{:S(2)}, u32[]{:S(2)}) collective-permute-start(bf16[24,2176]{1,0:T(8,128)(2,1)S(1)} %pad_maximum_fusion.2), channel_id=1, source_target_pairs={{0,24},{8,0},{16,8},{24,16},{1,25},{9,1},{17,9},{25,17},{2,26},{10... | collective-permute-start | bytes 313352 | tf_op jit(solution)/shard_map/exchange_rows/ppermute | solution.py:196
  7.5 9.2 %collective-permute-start.1 = (bf16[24,2176]{1,0:T(8,128)(2,1)S(1)}, bf16[24,2176]{1,0:T(8,128)(2,1)S(1)}, u32[]{:S(2)}, u32[]{:S(2)}) collective-permute-start(bf16[24,2176]{1,0:T(8,128)(2,1)S(1)} %pad_maximum_fusion.2), channel_id=1, source_target_pairs={{0,16},{8,24},{16,0},{24,8},{1,17},{9,25},{17,1},{25,9},{2,18},{10... | collective-permute-start | bytes 313352 | tf_op jit(solution)/shard_map/exchange_rows/ppermute | solution.py:196
  7.5 9.2 %collective-permute-start = (bf16[24,2176]{1,0:T(8,128)(2,1)S(1)}, bf16[24,2176]{1,0:T(8,128)(2,1)S(1)}, u32[]{:S(2)}, u32[]{:S(2)}) collective-permute-start(bf16[24,2176]{1,0:T(8,128)(2,1)S(1)} %pad_maximum_fusion.2), channel_id=1, source_target_pairs={{0,8},{8,16},{16,24},{24,0},{1,9},{9,17},{17,25},{25,1},{2,10},{10... | collective-permute-start | bytes 313352 | tf_op jit(solution)/shard_map/exchange_rows/ppermute | solution.py:196
  16.7 11.1 %collective-permute-start.4 = (bf16[96,2176]{1,0:T(8,128)(2,1)S(1)}, bf16[96,2176]{1,0:T(8,128)(2,1)S(1)}, u32[]{:S(2)}, u32[]{:S(2)}) collective-permute-start(bf16[96,2176]{1,0:T(8,128)(2,1)S(1)} %pad_maximum_fusion.refs_0_), channel_id=1, source_target_pairs={{0,2},{1,3},{2,0},{3,1},{4,6},{5,7},{6,4},{7,5},{8,10},{9,11},{10,... | collective-permute-start | bytes 1253384 | tf_op jit(solution)/shard_map/exchange_rows/ppermute | solution.py:200
  18.3 11.0 %collective-permute-start.12 = (bf16[24,2048]{1,0:T(8,128)(2,1)S(1)}, bf16[24,2048]{1,0:T(8,128)(2,1)S(1)}, u32[]{:S(2)}, u32[]{:S(2)}) collective-permute-start(bf16[24,2048]{1,0:T(8,128)(2,1)S(1)} %get-tuple-element.16), channel_id=1, source_target_pairs={{0,24},{8,0},{16,8},{24,16},{1,25},{9,1},{17,9},{25,17},{2,26},{10... | collective-permute-start | bytes 294920 | tf_op jit(solution)/shard_map/exchange_rows/ppermute | solution.py:196
  20.2 9.2 %collective-permute-start.11 = (bf16[24,2048]{1,0:T(8,128)(2,1)S(1)}, bf16[24,2048]{1,0:T(8,128)(2,1)S(1)}, u32[]{:S(2)}, u32[]{:S(2)}) collective-permute-start(bf16[24,2048]{1,0:T(8,128)(2,1)S(1)} %get-tuple-element.16), channel_id=1, source_target_pairs={{0,16},{8,24},{16,0},{24,8},{1,17},{9,25},{17,1},{25,9},{2,18},{10... | collective-permute-start | bytes 294920 | tf_op jit(solution)/shard_map/exchange_rows/ppermute | solution.py:196
  20.6 8.7 %collective-permute-start.10 = (bf16[24,2048]{1,0:T(8,128)(2,1)S(1)}, bf16[24,2048]{1,0:T(8,128)(2,1)S(1)}, u32[]{:S(2)}, u32[]{:S(2)}) collective-permute-start(bf16[24,2048]{1,0:T(8,128)(2,1)S(1)} %get-tuple-element.16), channel_id=1, source_target_pairs={{0,8},{8,16},{16,24},{24,0},{1,9},{9,17},{17,25},{25,1},{2,10},{10... | collective-permute-start | bytes 294920 | tf_op jit(solution)/shard_map/exchange_rows/ppermute | solution.py:196
  22.7 12.6 %collective-permute-start.6 = (bf16[96,2176]{1,0:T(8,128)(2,1)S(1)}, bf16[96,2176]{1,0:T(8,128)(2,1)S(1)}, u32[]{:S(2)}, u32[]{:S(2)}) collective-permute-start(bf16[96,2176]{1,0:T(8,128)(2,1)S(1)} %pad_maximum_fusion.refs_0_), channel_id=1, source_target_pairs={{0,4},{1,5},{2,6},{3,7},{4,0},{5,1},{6,2},{7,3},{8,12},{9,13},{10,... | collective-permute-start | bytes 1253384 | tf_op jit(solution)/shard_map/exchange_rows/ppermute | solution.py:200
  27.8 22.0 %collective-permute-start.8 = (bf16[96,2176]{1,0:T(8,128)(2,1)S(1)}, bf16[96,2176]{1,0:T(8,128)(2,1)S(1)}, u32[]{:S(2)}, u32[]{:S(2)}) collective-permute-start(bf16[96,2176]{1,0:T(8,128)(2,1)S(1)} %collective-permute-done.4.refs_2_), channel_id=1, source_target_pairs={{0,4},{1,5},{2,6},{3,7},{4,0},{5,1},{6,2},{7,3},{8,12},{9,13},{10,... | collective-permute-start | bytes 1253384 | tf_op jit(solution)/shard_map/exchange_rows/ppermute | solution.py:200
  29.4 20.4 %collective-permute-start.16 = (bf16[96,2048]{1,0:T(8,128)(2,1)S(1)}, bf16[96,2048]{1,0:T(8,128)(2,1)}, u32[]{:S(2)}, u32[]{:S(2)}) collective-permute-start(bf16[96,2048]{1,0:T(8,128)(2,1)S(1)} %pad_maximum_fusion.1.refs_0_), channel_id=1, source_target_pairs={{0,4},{1,5},{2,6},{3,7},{4,0},{5,1},{6,2},{7,3},{8,12},{9,13},{10,... | collective-permute-start | bytes 1179656 | tf_op jit(solution)/shard_map/exchange_rows/ppermute | solution.py:200
  30.5 19.8 %collective-permute-start.14 = (bf16[96,2048]{1,0:T(8,128)(2,1)S(1)}, bf16[96,2048]{1,0:T(8,128)(2,1)S(1)}, u32[]{:S(2)}, u32[]{:S(2)}) collective-permute-start(bf16[96,2048]{1,0:T(8,128)(2,1)S(1)} %pad_maximum_fusion.1.refs_0_), channel_id=1, source_target_pairs={{0,2},{1,3},{2,0},{3,1},{4,6},{5,7},{6,4},{7,5},{8,10},{9,11},{10,... | collective-permute-start | bytes 1179656 | tf_op jit(solution)/shard_map/exchange_rows/ppermute | solution.py:200
  31.5 29.8 %collective-permute-start.3 = (bf16[96,2176]{1,0:T(8,128)(2,1)S(1)}, bf16[96,2176]{1,0:T(8,128)(2,1)S(1)}, u32[]{:S(2)}, u32[]{:S(2)}) collective-permute-start(bf16[96,2176]{1,0:T(8,128)(2,1)S(1)} %pad_maximum_fusion.refs_0_), channel_id=1, source_target_pairs={{0,1},{1,0},{2,3},{3,2},{4,5},{5,4},{6,7},{7,6},{8,9},{9,8},{10,11... | collective-permute-start | bytes 1253384 | tf_op jit(solution)/shard_map/exchange_rows/ppermute | solution.py:200
  35.3 27.2 %collective-permute-start.7 = (bf16[96,2176]{1,0:T(8,128)(2,1)S(1)}, bf16[96,2176]{1,0:T(8,128)(2,1)S(1)}, u32[]{:S(2)}, u32[]{:S(2)}) collective-permute-start(bf16[96,2176]{1,0:T(8,128)(2,1)S(1)} %collective-permute-done.6.refs_4_), channel_id=1, source_target_pairs={{0,1},{1,0},{2,3},{3,2},{4,5},{5,4},{6,7},{7,6},{8,9},{9,8},{10,11... | collective-permute-start | bytes 1253384 | tf_op jit(solution)/shard_map/exchange_rows/ppermute | solution.py:200
  49.8 13.1 %collective-permute-start.5 = (bf16[96,2176]{1,0:T(8,128)(2,1)S(1)}, bf16[96,2176]{1,0:T(8,128)(2,1)}, u32[]{:S(2)}, u32[]{:S(2)}) collective-permute-start(bf16[96,2176]{1,0:T(8,128)(2,1)S(1)} %collective-permute-done.4.refs_2_), channel_id=1, source_target_pairs={{0,1},{1,0},{2,3},{3,2},{4,5},{5,4},{6,7},{7,6},{8,9},{9,8},{10,11... | collective-permute-start | bytes 1253384 | tf_op jit(solution)/shard_map/exchange_rows/ppermute | solution.py:200
  49.8 13.2 %collective-permute-start.9 = (bf16[96,2176]{1,0:T(8,128)(2,1)S(1)}, bf16[96,2176]{1,0:T(8,128)(2,1)}, u32[]{:S(2)}, u32[]{:S(2)}) collective-permute-start(bf16[96,2176]{1,0:T(8,128)(2,1)S(1)} %collective-permute-done.8.refs_6_), channel_id=1, source_target_pairs={{0,1},{1,0},{2,3},{3,2},{4,5},{5,4},{6,7},{7,6},{8,9},{9,8},{10,11... | collective-permute-start | bytes 1253384 | tf_op jit(solution)/shard_map/exchange_rows/ppermute | solution.py:200
  50.3 0.8 copy-start.1
  51.1 11.3 %collective-permute-start.18 = (bf16[96,2048]{1,0:T(8,128)(2,1)}, bf16[96,2048]{1,0:T(8,128)(2,1)}, u32[]{:S(2)}, u32[]{:S(2)}) collective-permute-start(bf16[96,2048]{1,0:T(8,128)(2,1)} %collective-permute-done.16.refs_4_), channel_id=1, source_target_pairs={{0,2},{1,3},{2,0},{3,1},{4,6},{5,7},{6,4},{7,5},{8,10},{9,11},{10,... | collective-permute-start | bytes 1179656 | tf_op jit(solution)/shard_map/exchange_rows/ppermute | solution.py:200
  61.3 12.8 %copy-start.2 = (bf16[96,2048]{1,0:T(8,128)(2,1)S(1)}, bf16[96,2048]{1,0:T(8,128)(2,1)}, u32[]{:S(2)}) copy-start(bf16[96,2048]{1,0:T(8,128)(2,1)} %copy-done.1) | copy-start | bytes 1179652
  61.3 12.7 %collective-permute-start.13 = (bf16[96,2048]{1,0:T(8,128)(2,1)S(1)}, bf16[96,2048]{1,0:T(8,128)(2,1)S(1)}, u32[]{:S(2)}, u32[]{:S(2)}) collective-permute-start(bf16[96,2048]{1,0:T(8,128)(2,1)S(1)} %pad_maximum_fusion.1.refs_0_), channel_id=1, source_target_pairs={{0,1},{1,0},{2,3},{3,2},{4,5},{5,4},{6,7},{7,6},{8,9},{9,8},{10,11... | collective-permute-start | bytes 1179656 | tf_op jit(solution)/shard_map/exchange_rows/ppermute | solution.py:200
  62.4 11.5 %collective-permute-start.17 = (bf16[96,2048]{1,0:T(8,128)(2,1)}, bf16[96,2048]{1,0:T(8,128)(2,1)S(1)}, u32[]{:S(2)}, u32[]{:S(2)}) collective-permute-start(bf16[96,2048]{1,0:T(8,128)(2,1)} %collective-permute-done.16.refs_4_), channel_id=1, source_target_pairs={{0,1},{1,0},{2,3},{3,2},{4,5},{5,4},{6,7},{7,6},{8,9},{9,8},{10,11... | collective-permute-start | bytes 1179656 | tf_op jit(solution)/shard_map/exchange_rows/ppermute | solution.py:200
  62.4 11.5 %collective-permute-start.15 = (bf16[96,2048]{1,0:T(8,128)(2,1)}, bf16[96,2048]{1,0:T(8,128)(2,1)S(1)}, u32[]{:S(2)}, u32[]{:S(2)}) collective-permute-start(bf16[96,2048]{1,0:T(8,128)(2,1)} %copy-done.1), channel_id=1, source_target_pairs={{0,1},{1,0},{2,3},{3,2},{4,5},{5,4},{6,7},{7,6},{8,9},{9,8},{10,11... | collective-permute-start | bytes 1179656 | tf_op jit(solution)/shard_map/exchange_rows/ppermute | solution.py:200
  62.9 11.0 %collective-permute-start.19 = (bf16[96,2048]{1,0:T(8,128)(2,1)}, bf16[96,2048]{1,0:T(8,128)(2,1)S(1)}, u32[]{:S(2)}, u32[]{:S(2)}) collective-permute-start(bf16[96,2048]{1,0:T(8,128)(2,1)} %collective-permute-done.18.refs_6_), channel_id=1, source_target_pairs={{0,1},{1,0},{2,3},{3,2},{4,5},{5,4},{6,7},{7,6},{8,9},{9,8},{10,11... | collective-permute-start | bytes 1179656 | tf_op jit(solution)/shard_map/exchange_rows/ppermute | solution.py:200
  73.9 11.1 %copy-start.3 = (f32[4,128]{1,0:T(4,128)}, f32[4,128]{1,0:T(4,128)S(1)}, u32[]{:S(2)}) copy-start(f32[4,128]{1,0:T(4,128)S(1)} %get-tuple-element.9.rate_ref) | copy-start | bytes 6148
  85.1 0.9 copy-start

commit v2 on v0

v2 whole, which is shorter than its diff:
```python
import functools

import jax
import jax.numpy as jnp
from jax import lax
from jax.experimental import pallas as pl
from jax.experimental.pallas import tpu as pltpu
from jax.sharding import PartitionSpec as P

EXPERTS = 32
BLOCK = 64
ROWS_BLOCK = 24
MOST = 7
LANES = 128
MIB = 1024 * 1024
SPARE = 4

step_rate = 0.2

F32 = jnp.float32
BF16 = jnp.bfloat16


def dot_nn(a, b):
    return jnp.dot(a, b, preferred_element_type=F32)


def dot_nt(a, b):
    return lax.dot_general(a, b, (((1,), (1,)), ((), ())), preferred_element_type=F32)


def cuts_of(width, chunk):
    return [pl.ds(start, chunk) for start in range(0, width, chunk)]


def load_kernel(n_marks, *refs):
    base_ref, dual_ref, base_out, dual_out, sems = refs[n_marks:]
    copies = [
        pltpu.make_async_copy(base_ref, base_out, sems.at[0]),
        pltpu.make_async_copy(dual_ref, dual_out, sems.at[1]),
    ]
    for copy in copies:
        copy.start()
    for copy in copies:
        copy.wait()


def load(marks, base_weight, dual_start):
    anywhere = pl.BlockSpec(memory_space=pl.ANY)
    return pl.pallas_call(
        functools.partial(load_kernel, len(marks)),
        in_specs=[anywhere] * (len(marks) + 2),
        out_specs=[anywhere, anywhere],
        out_shape=[pltpu.VMEM(x.shape, x.dtype) for x in (base_weight, dual_start)],
        scratch_shapes=[pltpu.SemaphoreType.DMA((2,))],
        compiler_params=pltpu.CompilerParams(vmem_limit_bytes=16 * MIB),
        cost_estimate=pl.CostEstimate(flops=0, bytes_accessed=6 * base_weight.size, transcendentals=0),
    )(*marks, base_weight, dual_start)


def fused_kernel(chunk, topk, halves, *refs):
    gathered, (base_ref, dual_ref, keep_ref, weight_out, dual_out, rows, rank, hits, scale, mask) = refs[:halves], refs[halves:]
    expert, tile = pl.program_id(0), pl.program_id(1)
    tokens = gathered[0].shape[0]
    slots, width = rows.shape
    part_width = width // halves
    local = hits.shape[0]
    tall = weight_out.shape[1]
    blocks = tall // BLOCK
    cuts = cuts_of(width, chunk)

    @pl.when((expert == 0) & (tile == 0))
    def _():
        named = gathered[0][:, pl.ds(part_width, LANES)].astype(F32).T[:topk, :]
        for own in range(local):
            label = (lax.axis_index("exp") * local + own).astype(F32)
            hits[own : own + 1, :] = jnp.max(jnp.where(named == label, 1.0, 0.0), axis=0, keepdims=True)
        earlier = lax.broadcasted_iota(jnp.int32, (tokens, tokens), 0)
        later = lax.broadcasted_iota(jnp.int32, (tokens, tokens), 1)
        ahead = jnp.where(earlier < later, 1.0, 0.0).astype(BF16)
        rank[...] = dot_nn(hits[...].astype(BF16), ahead)
        count = keep_ref.shape[2]
        at = lax.broadcasted_iota(jnp.int32, (count, width), 0) * BLOCK
        column = lax.broadcasted_iota(jnp.int32, (count, width), 1)
        wide = jnp.where((column >= at) & (column < at + BLOCK), 1.0, 0.0).astype(BF16)
        for own in range(local):
            mask[own] = dot_nn(keep_ref[own].astype(F32).astype(BF16), wide)

    @pl.when(tile == 0)
    def _():
        hit = hits[pl.ds(expert, 1), :]
        place = rank[pl.ds(expert, 1), :]
        slot = lax.broadcasted_iota(jnp.int32, (slots, tokens), 0).astype(F32)
        taken = jnp.where((slot == place) & (hit > 0.5), 1.0, 0.0).astype(BF16)
        for cut in cuts:
            half, start = divmod(cut.start, part_width)
            rows[:, cut] = dot_nn(taken, gathered[half][:, pl.ds(start, chunk)]).astype(BF16)
        total = jnp.sum(hit, axis=1, keepdims=True)
        scale[...] = jnp.broadcast_to(step_rate / total, scale.shape)

    rate = scale[0:1, 0:1]
    parts = [slice(start, start + BLOCK) for start in range(0, tall, BLOCK)]
    sources = [pl.ds(pl.multiple_of(tile * tall + part.start, BLOCK), BLOCK) for part in parts]
    keeps = [pl.ds(tile * blocks + i, 1) for i in range(blocks)]

    resid = jnp.zeros((tall, slots), F32)
    for cut in cuts:
        deltas = [
            base_ref[expert, source, cut] * (mask[expert, at, cut] - 1.0).astype(BF16)
            for source, at in zip(sources, keeps)
        ]
        resid = resid + dot_nt(jnp.concatenate(deltas, axis=0), rows[:, cut])
    resid = resid.astype(BF16)

    after = jnp.zeros((tall, slots), F32)
    for cut in cuts:
        grad = dot_nn(resid, rows[:, cut])
        deltas = []
        for part, source, at in zip(parts, sources, keeps):
            base = base_ref[expert, source, cut].astype(F32)
            weight = mask[expert, at, cut] * base - step_rate * dual_ref[expert, source, cut] - rate * grad[part, :]
            weight_out[0, part, cut] = weight
            deltas.append((weight - base).astype(BF16))
        after = after + dot_nt(jnp.concatenate(deltas, axis=0), rows[:, cut])
    resid = after.astype(BF16)

    for cut in cuts:
        grad = dot_nn(resid, rows[:, cut])
        for part, source, at in zip(parts, sources, keeps):
            keep = mask[expert, at, cut]
            weight = weight_out[0, part, cut]
            both = weight + dual_ref[expert, source, cut]
            weight = (1.0 - step_rate) * weight - (step_rate - 2.0 * step_rate * keep) * both - rate * grad[part, :]
            weight_out[0, part, cut] = weight
            dual_out[0, part, cut] = (1.0 - keep) * (both + weight)


def fused(gathered, base_weight, keep_mask, dual_start, topk, tall):
    local, hidden, width = base_weight.shape
    tokens = gathered[0].shape[0]
    slots = -(-tokens // ROWS_BLOCK) * MOST
    slots = -(-min(slots, tokens) // 16) * 16
    block = pl.BlockSpec((1, tall, width), lambda e, t: (e, t, 0))
    whole = pl.BlockSpec(memory_space=pltpu.VMEM)
    out = jax.ShapeDtypeStruct(dual_start.shape, F32)
    scoped = 16 * tall * width + 2 * slots * (width + 2 * tokens) + 32 * local * width + SPARE * MIB
    macs = local * slots * width * (4 * hidden + tokens)
    held = [pltpu.with_memory_space_constraint(x, pltpu.VMEM) for x in (*gathered, base_weight, dual_start)]
    return pl.pallas_call(
        functools.partial(fused_kernel, 512, topk, len(gathered)),
        grid=(local, hidden // tall),
        in_specs=[whole] * len(held) + [whole],
        out_specs=[block, block],
        out_shape=[out, out],
        scratch_shapes=[
            pltpu.VMEM((slots, width), BF16),
            pltpu.VMEM((local, tokens), F32),
            pltpu.VMEM((local, tokens), F32),
            pltpu.VMEM((8, LANES), F32),
            pltpu.VMEM((local, keep_mask.shape[1], width), F32),
        ],
        compiler_params=pltpu.CompilerParams(
            vmem_limit_bytes=scoped, dimension_semantics=("arbitrary", "arbitrary")
        ),
        cost_estimate=pl.CostEstimate(flops=2 * macs, bytes_accessed=8 * base_weight.size, transcendentals=0),
    )(*held, keep_mask)


def spread(own):
    n_tok, n_exp = lax.axis_size("tok"), lax.axis_size("exp")
    top = n_exp.bit_length() - 1
    assert 1 << top == n_exp

    def swap(piece, bit):
        return lax.ppermute(piece, "exp", [(i, i ^ (1 << bit)) for i in range(n_exp)])

    column = [own]
    for shift in range(1, n_tok):
        column.append(lax.ppermute(own, "tok", [(i, (i + shift) % n_tok) for i in range(n_tok)]))
    pieces = {0: jnp.concatenate(column, axis=0)}
    if top == 3:
        one, two = swap(pieces[0], 1), swap(pieces[0], 2)
        middle = own.shape[1] // 2 // LANES * LANES
        far = jnp.concatenate([swap(one[:, :middle], 2), swap(two[:, middle:], 1)], axis=1)
        pieces.update({2: one, 4: two, 6: far})
    else:
        for bit in range(1, top):
            pieces.update({at ^ (1 << bit): swap(piece, bit) for at, piece in pieces.items()})
    pieces.update({at ^ 1: swap(piece, 0) for at, piece in pieces.items()})
    return jnp.concatenate([pieces[i] for i in range(n_exp)], axis=0), [pieces[i] for i in range(n_exp) if i.bit_count() == 1 and i > 1]


def on_device(x_rows, routes, base_weight, keep_mask, dual_start):
    local, hidden, width = base_weight.shape
    topk = routes.shape[1]
    halves = 2
    part = width // halves
    named = jnp.pad(routes.astype(BF16), ((0, 0), (0, LANES - topk)))
    sent = [x_rows[:, h * part : (h + 1) * part] for h in range(halves)]
    sent[0] = jnp.concatenate([sent[0], named], axis=1)
    with jax.named_scope("exchange_rows"):
        gathered, marks = zip(*[spread(own) for own in sent])
    with jax.named_scope("load_weights"):
        base_weight, dual_start = load(marks[-1], base_weight, dual_start)
    tall = 2 * BLOCK if hidden % (2 * BLOCK) == 0 else BLOCK
    with jax.named_scope("fused_iterations"):
        return fused(gathered, base_weight, keep_mask, dual_start, topk, tall)


def solution(mesh):
    return jax.shard_map(
        on_device,
        mesh=mesh,
        in_specs=(
            P(("tok", "exp"), None),
            P(("tok", "exp"), None),
            P("exp", "tok", None),
            P("exp", "tok", None),
            P("exp", "tok", None),
        ),
        out_specs=(P("exp", "tok", None), P("exp", "tok", None)),
        check_vma=False,
    )
```

time: 139 us -> 114 us (0.82)
  waiting for transfers between devices: 72.5 us -> 22.4 us
  starting transfers between devices: 0.04 us -> 21.8 us
  Pallas kernels: 47.1 us -> 63.3 us
  between operations: 14 us -> 0.91 us
  local copies, waits for them, and re-layouts: 1.74 us -> 3.6 us
    all_gather x1 -> x0, waiting for transfers between devices: 72.5 us -> none  [on_device(): gathered = lax.all_gather(own, ('tok', 'exp'), axis=0, tiled=True)]
    ppermute x0 -> x22, waiting for transfers between devices: none -> 22.4 us  [the longest x16 17.2 us: swap(): return lax.ppermute(piece, 'exp', [(i, i ^ 1 << bit) for i in range(n_exp)])]
    ppermute x0 -> x22, starting transfers between devices: none -> 21.8 us  [the longest x6 11.9 us: spread(): lax.ppermute(own, 'tok', [(i, (i + shift) % n_tok) for i in range(n_tok)])]
    pallas_call x1 -> x2, Pallas kernels: 47.1 us -> 63.3 us  [the longest x1 51.5 us: fused(): pl.pallas_call(functools.partial(fused_kernel, 512, topk, len(gathered)),...]
    unnamed x0 -> x21, local copies, waits for them, and re-layouts: none -> 1.78 us
    slice x0 -> x5, local copies, waits for them, and re-layouts: none -> 1.66 us  [the longest x1 1.6 us: on_device(): sent = [x_rows[:, h * part:(h + 1) * part] for h in range(halves)]]
    another operation x2 -> x0, local copies, waits for them, and re-layouts: 1.4 us -> none  [on_device(): mask = mask.reshape(local, hidden // tall, tall // BLOCK, width)]
  transfers between devices with their start and end apart: 1 -> 22, of which waited for: 1 -> 8; matrix products, arithmetic and copies ran while one was open for 2% -> 3% of each run, Pallas kernels for 0% -> 10%
where the time goes in v2:
time: 114 us
  Pallas kernels  63.3 us (56%)
  waiting for transfers between devices  22.4 us (20%)
  starting transfers between devices  21.8 us (19%)
  local copies, waits for them, and re-layouts  3.6 us (3%)
  other arithmetic  1.72 us (2%)
    pallas_call x1, Pallas kernels, fused(): pl.pallas_call(functools.partial(fused_kernel, 512, topk, len(gathered)),...  51.5 us
    ppermute x16, waiting for transfers between devices, swap(): return lax.ppermute(piece, 'exp', [(i, i ^ 1 << bit) for i in range(n_exp)])  17.2 us
    ppermute x6, starting transfers between devices, spread(): lax.ppermute(own, 'tok', [(i, (i + shift) % n_tok) for i in range(n_tok)])  11.9 us
    pallas_call x1, Pallas kernels, load(): pl.pallas_call(functools.partial(load_kernel, len(marks)), in_specs=[anyw...  11.8 us
    ppermute x16, starting transfers between devices, swap(): return lax.ppermute(piece, 'exp', [(i, i ^ 1 << bit) for i in range(n_exp)])  9.94 us
    ppermute x6, waiting for transfers between devices, spread(): lax.ppermute(own, 'tok', [(i, (i + shift) % n_tok) for i in range(n_tok)])  5.19 us
  transfers between devices with their start and end apart: 22, of which 8 were waited for; matrix products, arithmetic and copies ran while one was open for 3% of the time, Pallas kernels for 10%

profile of v2, /device:TPU:0, one launch (start us, length us, event | category | flops | bytes accessed | tf_op | source)
XLA Modules:
  0.0 113.7 jit_solution(628431256518130134)
XLA Ops:
  0.6 1.6 %fusion = (bf16[24,2048]{1,0:T(8,128)(2,1)}, bf16[768,2048]{1,0:T(8,128)(2,1)S(1)}, bf16[24,2048]{1,0:T(8,128)(2,1)S(1)}) fusion(bf16[24,4096]{1,0:T(8,128)(2,1)} %param.5), kind=kLoop, calls=%fused_computation.29 | loop fusion | bytes 491520 | tf_op jit(solution)/shard_map/slice | solution.py:199
  2.2 5.0 %collective-permute-start.13 = (bf16[24,2048]{1,0:T(8,128)(2,1)}, bf16[24,2048]{1,0:T(8,128)(2,1)S(1)}, u32[]{:S(2)}, u32[]{:S(2)}) collective-permute-start(bf16[24,2048]{1,0:T(8,128)(2,1)} %get-tuple-element.6), channel_id=1, source_target_pairs={{0,24},{8,0},{16,8},{24,16},{1,25},{9,1},{17,9},{25,17},{2,26},{10... | collective-permute-start | bytes 294920 | tf_op jit(solution)/shard_map/exchange_rows/ppermute | solution.py:179
  7.3 1.0 collective-permute-start.11
  8.3 0.7 convert_element_type.5
  9.1 2.0 %collective-permute-start.1 = (bf16[24,2176]{1,0:T(8,128)(2,1)S(1)}, bf16[24,2176]{1,0:T(8,128)(2,1)S(1)}, u32[]{:S(2)}, u32[]{:S(2)}) collective-permute-start(bf16[24,2176]{1,0:T(8,128)(2,1)S(1)} %get-tuple-element.9), channel_id=1, source_target_pairs={{0,16},{8,24},{16,0},{24,8},{1,17},{9,25},{17,1},{25,9},{2,18},{10... | collective-permute-start | bytes 313352 | tf_op jit(solution)/shard_map/exchange_rows/ppermute | solution.py:179
  11.1 1.5 %collective-permute-start = (bf16[24,2176]{1,0:T(8,128)(2,1)S(1)}, bf16[24,2176]{1,0:T(8,128)(2,1)S(1)}, u32[]{:S(2)}, u32[]{:S(2)}) collective-permute-start(bf16[24,2176]{1,0:T(8,128)(2,1)S(1)} %get-tuple-element.9), channel_id=1, source_target_pairs={{0,8},{8,16},{16,24},{24,0},{1,9},{9,17},{17,25},{25,1},{2,10},{10... | collective-permute-start | bytes 313352 | tf_op jit(solution)/shard_map/exchange_rows/ppermute | solution.py:179
  12.6 1.3 %copy.10.refs_4_ = s32[4,6,64]{2,1,0:T(8,128)} copy(s32[4,6,64]{2,0,1:T(4,128)} %param.8) | data formatting | bytes 12288 | tf_op args[3]
  13.9 2.4 %collective-permute-start.2 = (bf16[24,2176]{1,0:T(8,128)(2,1)S(1)}, bf16[24,2176]{1,0:T(8,128)(2,1)S(1)}, u32[]{:S(2)}, u32[]{:S(2)}) collective-permute-start(bf16[24,2176]{1,0:T(8,128)(2,1)S(1)} %get-tuple-element.9), channel_id=1, source_target_pairs={{0,24},{8,0},{16,8},{24,16},{1,25},{9,1},{17,9},{25,17},{2,26},{10... | collective-permute-start | bytes 313352 | tf_op jit(solution)/shard_map/exchange_rows/ppermute | solution.py:179
  16.2 5.2 %collective-permute-done.12 = bf16[24,2048]{1,0:T(8,128)(2,1)S(1)} collective-permute-done((bf16[24,2048]{1,0:T(8,128)(2,1)}, bf16[24,2048]{1,0:T(8,128)(2,1)S(1)}, u32[]{:S(2)}, u32[]{:S(2)}) %collective-permute-start.12) | collective-permute-done | bytes 98336 | tf_op jit(solution)/shard_map/exchange_rows/ppermute | solution.py:179
  21.4 0.9 pad_maximum_fusion.2
  22.3 1.6 %collective-permute-start.17 = (bf16[96,2048]{1,0:T(8,128)(2,1)S(1)}, bf16[96,2048]{1,0:T(8,128)(2,1)S(1)}, u32[]{:S(2)}, u32[]{:S(2)}) collective-permute-start(bf16[96,2048]{1,0:T(8,128)(2,1)S(1)} %pad_maximum_fusion.2), channel_id=1, source_target_pairs={{0,4},{1,5},{2,6},{3,7},{4,0},{5,1},{6,2},{7,3},{8,12},{9,13},{10,... | collective-permute-start | bytes 1179656 | tf_op jit(solution)/shard_map/exchange_rows/ppermute | solution.py:175
  23.9 1.5 %collective-permute-start.15 = (bf16[96,2048]{1,0:T(8,128)(2,1)S(1)}, bf16[96,2048]{1,0:T(8,128)(2,1)S(1)}, u32[]{:S(2)}, u32[]{:S(2)}) collective-permute-start(bf16[96,2048]{1,0:T(8,128)(2,1)S(1)} %pad_maximum_fusion.2), channel_id=1, source_target_pairs={{0,2},{1,3},{2,0},{3,1},{4,6},{5,7},{6,4},{7,5},{8,10},{9,11},{10,... | collective-permute-start | bytes 1179656 | tf_op jit(solution)/shard_map/exchange_rows/ppermute | solution.py:175
  25.6 0.6 collective-permute-start.6
  26.2 0.8 collective-permute-start.4
  27.0 7.5 %collective-permute-done.17.refs_1_ = bf16[96,2048]{1,0:T(8,128)(2,1)S(1)} collective-permute-done((bf16[96,2048]{1,0:T(8,128)(2,1)S(1)}, bf16[96,2048]{1,0:T(8,128)(2,1)S(1)}, u32[]{:S(2)}, u32[]{:S(2)}) %collective-permute-start.17) | collective-permute-done | bytes 393248 | tf_op jit(solution)/shard_map/exchange_rows/ppermute | solution.py:175
  34.5 1.5 %collective-permute-done.15.refs_0_ = bf16[96,2048]{1,0:T(8,128)(2,1)S(1)} collective-permute-done((bf16[96,2048]{1,0:T(8,128)(2,1)S(1)}, bf16[96,2048]{1,0:T(8,128)(2,1)S(1)}, u32[]{:S(2)}, u32[]{:S(2)}) %collective-permute-start.15) | collective-permute-done | bytes 393248 | tf_op jit(solution)/shard_map/exchange_rows/ppermute | solution.py:175
  36.0 1.5 %collective-permute-start.20 = (bf16[96,1024]{1,0:T(8,128)(2,1)S(1)}, bf16[96,1024]{1,0:T(8,128)(2,1)S(1)}, u32[]{:S(2)}, u32[]{:S(2)}) collective-permute-start(bf16[96,1024]{1,0:T(8,128)(2,1)S(1)} %slice.27), channel_id=1, source_target_pairs={{0,2},{1,3},{2,0},{3,1},{4,6},{5,7},{6,4},{7,5},{8,10},{9,11},{10,... | collective-permute-start | bytes 589832 | tf_op jit(solution)/shard_map/exchange_rows/ppermute | solution.py:175
  37.5 11.8 %load_weights.1 = (bf16[4,384,4096]{2,1,0:T(8,128)(2,1)S(1)}, f32[4,384,4096]{2,1,0:T(8,128)S(1)}) custom-call(bf16[96,2048]{1,0:T(8,128)(2,1)S(1)} %collective-permute-done.15.refs_0_, bf16[96,2048]{1,0:T(8,128)(2,1)S(1)} %collective-permute-done.17.refs_1_, bf16[4,384,4096]{2,1,0:T(8,128)(2,1)} %refs_2_.1, f32[4,384,4096]{2,1,0:T(8,128)} %refs_3_.1), custom_call_target="tpu_custom_call" | custom-call | bytes 37748736 | tf_op jit(solution)/shard_map/load_weights/pallas_call | solution.py:50
  50.7 0.6 collective-permute-start.9
  51.4 1.6 %collective-permute-start.8 = (bf16[96,1024]{1,0:T(8,128)(2,1)S(1)}, bf16[96,1024]{1,0:T(8,128)(2,1)S(1)}, u32[]{:S(2)}, u32[]{:S(2)}) collective-permute-start(bf16[96,1024]{1,0:T(8,128)(2,1)S(1)} %slice.24), channel_id=1, source_target_pairs={{0,4},{1,5},{2,6},{3,7},{4,0},{5,1},{6,2},{7,3},{8,12},{9,13},{10,... | collective-permute-start | bytes 589832 | tf_op jit(solution)/shard_map/exchange_rows/ppermute | solution.py:175
  52.9 3.4 %collective-permute-done.19 = bf16[96,1024]{1,0:T(8,128)(2,1)S(1)} collective-permute-done((bf16[96,1024]{1,0:T(8,128)(2,1)S(1)}, bf16[96,1024]{1,0:T(8,128)(2,1)S(1)}, u32[]{:S(2)}, u32[]{:S(2)}) %collective-permute-start.19) | collective-permute-done | bytes 196640 | tf_op jit(solution)/shard_map/exchange_rows/ppermute | solution.py:175
  56.4 2.9 %collective-permute-done.8 = bf16[96,1024]{1,0:T(8,128)(2,1)S(1)} collective-permute-done((bf16[96,1024]{1,0:T(8,128)(2,1)S(1)}, bf16[96,1024]{1,0:T(8,128)(2,1)S(1)}, u32[]{:S(2)}, u32[]{:S(2)}) %collective-permute-start.8) | collective-permute-done | bytes 196640 | tf_op jit(solution)/shard_map/exchange_rows/ppermute | solution.py:175
  60.1 1.0 collective-permute-done.5
  62.2 51.5 %fused_iterations.1 = (f32[4,384,4096]{2,1,0:T(8,128)}, f32[4,384,4096]{2,1,0:T(8,128)}) custom-call(bf16[768,2176]{1,0:T(8,128)(2,1)S(1)} %constant_dynamic-update-slice_fusion.refs_0_, bf16[768,2048]{1,0:T(8,128)(2,1)S(1)} %constant_dynamic-update-slice_fusion.11.refs_1_, bf16[4,384,4096]{2,1,0:T(8,128)(2,1)S(1)} %get-tuple-element.4.refs_2_, ...), custom_call_target="tpu_custom_call" | custom-call | flops 16911433728 | bytes 50331648 | tf_op jit(solution)/shard_map/fused_iterations/pallas_call | solution.py:149
  (58 shorter events, 3.6 us)
Async XLA Ops:
  2.2 11.6 %collective-permute-start.13 = (bf16[24,2048]{1,0:T(8,128)(2,1)}, bf16[24,2048]{1,0:T(8,128)(2,1)S(1)}, u32[]{:S(2)}, u32[]{:S(2)}) collective-permute-start(bf16[24,2048]{1,0:T(8,128)(2,1)} %get-tuple-element.6), channel_id=1, source_target_pairs={{0,24},{8,0},{16,8},{24,16},{1,25},{9,1},{17,9},{25,17},{2,26},{10... | collective-permute-start | bytes 294920 | tf_op jit(solution)/shard_map/exchange_rows/ppermute | solution.py:179
  7.3 14.1 %collective-permute-start.12 = (bf16[24,2048]{1,0:T(8,128)(2,1)}, bf16[24,2048]{1,0:T(8,128)(2,1)S(1)}, u32[]{:S(2)}, u32[]{:S(2)}) collective-permute-start(bf16[24,2048]{1,0:T(8,128)(2,1)} %get-tuple-element.6), channel_id=1, source_target_pairs={{0,16},{8,24},{16,0},{24,8},{1,17},{9,25},{17,1},{25,9},{2,18},{10... | collective-permute-start | bytes 294920 | tf_op jit(solution)/shard_map/exchange_rows/ppermute | solution.py:179
  7.3 14.1 %collective-permute-start.11 = (bf16[24,2048]{1,0:T(8,128)(2,1)}, bf16[24,2048]{1,0:T(8,128)(2,1)S(1)}, u32[]{:S(2)}, u32[]{:S(2)}) collective-permute-start(bf16[24,2048]{1,0:T(8,128)(2,1)} %get-tuple-element.6), channel_id=1, source_target_pairs={{0,8},{8,16},{16,24},{24,0},{1,9},{9,17},{17,25},{25,1},{2,10},{10... | collective-permute-start | bytes 294920 | tf_op jit(solution)/shard_map/exchange_rows/ppermute | solution.py:179
  9.1 16.3 %collective-permute-start.1 = (bf16[24,2176]{1,0:T(8,128)(2,1)S(1)}, bf16[24,2176]{1,0:T(8,128)(2,1)S(1)}, u32[]{:S(2)}, u32[]{:S(2)}) collective-permute-start(bf16[24,2176]{1,0:T(8,128)(2,1)S(1)} %get-tuple-element.9), channel_id=1, source_target_pairs={{0,16},{8,24},{16,0},{24,8},{1,17},{9,25},{17,1},{25,9},{2,18},{10... | collective-permute-start | bytes 313352 | tf_op jit(solution)/shard_map/exchange_rows/ppermute | solution.py:179
  11.1 14.4 %collective-permute-start = (bf16[24,2176]{1,0:T(8,128)(2,1)S(1)}, bf16[24,2176]{1,0:T(8,128)(2,1)S(1)}, u32[]{:S(2)}, u32[]{:S(2)}) collective-permute-start(bf16[24,2176]{1,0:T(8,128)(2,1)S(1)} %get-tuple-element.9), channel_id=1, source_target_pairs={{0,8},{8,16},{16,24},{24,0},{1,9},{9,17},{17,25},{25,1},{2,10},{10... | collective-permute-start | bytes 313352 | tf_op jit(solution)/shard_map/exchange_rows/ppermute | solution.py:179
  13.9 11.7 %collective-permute-start.2 = (bf16[24,2176]{1,0:T(8,128)(2,1)S(1)}, bf16[24,2176]{1,0:T(8,128)(2,1)S(1)}, u32[]{:S(2)}, u32[]{:S(2)}) collective-permute-start(bf16[24,2176]{1,0:T(8,128)(2,1)S(1)} %get-tuple-element.9), channel_id=1, source_target_pairs={{0,24},{8,0},{16,8},{24,16},{1,25},{9,1},{17,9},{25,17},{2,26},{10... | collective-permute-start | bytes 313352 | tf_op jit(solution)/shard_map/exchange_rows/ppermute | solution.py:179
  22.3 12.1 %collective-permute-start.17 = (bf16[96,2048]{1,0:T(8,128)(2,1)S(1)}, bf16[96,2048]{1,0:T(8,128)(2,1)S(1)}, u32[]{:S(2)}, u32[]{:S(2)}) collective-permute-start(bf16[96,2048]{1,0:T(8,128)(2,1)S(1)} %pad_maximum_fusion.2), channel_id=1, source_target_pairs={{0,4},{1,5},{2,6},{3,7},{4,0},{5,1},{6,2},{7,3},{8,12},{9,13},{10,... | collective-permute-start | bytes 1179656 | tf_op jit(solution)/shard_map/exchange_rows/ppermute | solution.py:175
  23.9 12.1 %collective-permute-start.15 = (bf16[96,2048]{1,0:T(8,128)(2,1)S(1)}, bf16[96,2048]{1,0:T(8,128)(2,1)S(1)}, u32[]{:S(2)}, u32[]{:S(2)}) collective-permute-start(bf16[96,2048]{1,0:T(8,128)(2,1)S(1)} %pad_maximum_fusion.2), channel_id=1, source_target_pairs={{0,2},{1,3},{2,0},{3,1},{4,6},{5,7},{6,4},{7,5},{8,10},{9,11},{10,... | collective-permute-start | bytes 1179656 | tf_op jit(solution)/shard_map/exchange_rows/ppermute | solution.py:175
  25.5 23.8 %collective-permute-start.14 = (bf16[96,2048]{1,0:T(8,128)(2,1)S(1)}, bf16[96,2048]{1,0:T(8,128)(2,1)S(1)}, u32[]{:S(2)}, u32[]{:S(2)}) collective-permute-start(bf16[96,2048]{1,0:T(8,128)(2,1)S(1)} %pad_maximum_fusion.2), channel_id=1, source_target_pairs={{0,1},{1,0},{2,3},{3,2},{4,5},{5,4},{6,7},{7,6},{8,9},{9,8},{10,11... | collective-permute-start | bytes 1179656 | tf_op jit(solution)/shard_map/exchange_rows/ppermute | solution.py:175
  25.6 24.4 %collective-permute-start.6 = (bf16[96,2176]{1,0:T(8,128)(2,1)S(1)}, bf16[96,2176]{1,0:T(8,128)(2,1)S(1)}, u32[]{:S(2)}, u32[]{:S(2)}) collective-permute-start(bf16[96,2176]{1,0:T(8,128)(2,1)S(1)} %pad_maximum_fusion), channel_id=1, source_target_pairs={{0,4},{1,5},{2,6},{3,7},{4,0},{5,1},{6,2},{7,3},{8,12},{9,13},{10,... | collective-permute-start | bytes 1253384 | tf_op jit(solution)/shard_map/exchange_rows/ppermute | solution.py:175
  26.2 23.9 %collective-permute-start.4 = (bf16[96,2176]{1,0:T(8,128)(2,1)S(1)}, bf16[96,2176]{1,0:T(8,128)(2,1)S(1)}, u32[]{:S(2)}, u32[]{:S(2)}) collective-permute-start(bf16[96,2176]{1,0:T(8,128)(2,1)S(1)} %pad_maximum_fusion), channel_id=1, source_target_pairs={{0,2},{1,3},{2,0},{3,1},{4,6},{5,7},{6,4},{7,5},{8,10},{9,11},{10,... | collective-permute-start | bytes 1253384 | tf_op jit(solution)/shard_map/exchange_rows/ppermute | solution.py:175
  34.4 16.2 %collective-permute-start.3 = (bf16[96,2176]{1,0:T(8,128)(2,1)S(1)}, bf16[96,2176]{1,0:T(8,128)(2,1)S(1)}, u32[]{:S(2)}, u32[]{:S(2)}) collective-permute-start(bf16[96,2176]{1,0:T(8,128)(2,1)S(1)} %pad_maximum_fusion), channel_id=1, source_target_pairs={{0,1},{1,0},{2,3},{3,2},{4,5},{5,4},{6,7},{7,6},{8,9},{9,8},{10,11... | collective-permute-start | bytes 1253384 | tf_op jit(solution)/shard_map/exchange_rows/ppermute | solution.py:175
  36.0 15.4 %collective-permute-start.20 = (bf16[96,1024]{1,0:T(8,128)(2,1)S(1)}, bf16[96,1024]{1,0:T(8,128)(2,1)S(1)}, u32[]{:S(2)}, u32[]{:S(2)}) collective-permute-start(bf16[96,1024]{1,0:T(8,128)(2,1)S(1)} %slice.27), channel_id=1, source_target_pairs={{0,2},{1,3},{2,0},{3,1},{4,6},{5,7},{6,4},{7,5},{8,10},{9,11},{10,... | collective-permute-start | bytes 589832 | tf_op jit(solution)/shard_map/exchange_rows/ppermute | solution.py:175
  49.3 7.1 %collective-permute-start.19 = (bf16[96,1024]{1,0:T(8,128)(2,1)S(1)}, bf16[96,1024]{1,0:T(8,128)(2,1)S(1)}, u32[]{:S(2)}, u32[]{:S(2)}) collective-permute-start(bf16[96,1024]{1,0:T(8,128)(2,1)S(1)} %slice.26), channel_id=1, source_target_pairs={{0,4},{1,5},{2,6},{3,7},{4,0},{5,1},{6,2},{7,3},{8,12},{9,13},{10,... | collective-permute-start | bytes 589832 | tf_op jit(solution)/shard_map/exchange_rows/ppermute | solution.py:175
  50.0 10.0 %collective-permute-start.18 = (bf16[96,2048]{1,0:T(8,128)(2,1)S(1)}, bf16[96,2048]{1,0:T(8,128)(2,1)S(1)}, u32[]{:S(2)}, u32[]{:S(2)}) collective-permute-start(bf16[96,2048]{1,0:T(8,128)(2,1)S(1)} %collective-permute-done.17.refs_1_), channel_id=1, source_target_pairs={{0,1},{1,0},{2,3},{3,2},{4,5},{5,4},{6,7},{7,6},{8,9},{9,8},{10,11... | collective-permute-start | bytes 1179656 | tf_op jit(solution)/shard_map/exchange_rows/ppermute | solution.py:175
  50.1 9.7 %collective-permute-start.16 = (bf16[96,2048]{1,0:T(8,128)(2,1)S(1)}, bf16[96,2048]{1,0:T(8,128)(2,1)S(1)}, u32[]{:S(2)}, u32[]{:S(2)}) collective-permute-start(bf16[96,2048]{1,0:T(8,128)(2,1)S(1)} %collective-permute-done.15.refs_0_), channel_id=1, source_target_pairs={{0,1},{1,0},{2,3},{3,2},{4,5},{5,4},{6,7},{7,6},{8,9},{9,8},{10,11... | collective-permute-start | bytes 1179656 | tf_op jit(solution)/shard_map/exchange_rows/ppermute | solution.py:175
  50.7 8.6 %collective-permute-start.9 = (bf16[96,1152]{1,0:T(8,128)(2,1)S(1)}, bf16[96,1152]{1,0:T(8,128)(2,1)S(1)}, u32[]{:S(2)}, u32[]{:S(2)}) collective-permute-start(bf16[96,1152]{1,0:T(8,128)(2,1)S(1)} %slice.25), channel_id=1, source_target_pairs={{0,2},{1,3},{2,0},{3,1},{4,6},{5,7},{6,4},{7,5},{8,10},{9,11},{10,... | collective-permute-start | bytes 663560 | tf_op jit(solution)/shard_map/exchange_rows/ppermute | solution.py:175
  51.4 7.9 %collective-permute-start.8 = (bf16[96,1024]{1,0:T(8,128)(2,1)S(1)}, bf16[96,1024]{1,0:T(8,128)(2,1)S(1)}, u32[]{:S(2)}, u32[]{:S(2)}) collective-permute-start(bf16[96,1024]{1,0:T(8,128)(2,1)S(1)} %slice.24), channel_id=1, source_target_pairs={{0,4},{1,5},{2,6},{3,7},{4,0},{5,1},{6,2},{7,3},{8,12},{9,13},{10,... | collective-permute-start | bytes 589832 | tf_op jit(solution)/shard_map/exchange_rows/ppermute | solution.py:175
  56.4 4.7 %collective-permute-start.7 = (bf16[96,2176]{1,0:T(8,128)(2,1)S(1)}, bf16[96,2176]{1,0:T(8,128)(2,1)S(1)}, u32[]{:S(2)}, u32[]{:S(2)}) collective-permute-start(bf16[96,2176]{1,0:T(8,128)(2,1)S(1)} %collective-permute-done.6), channel_id=1, source_target_pairs={{0,1},{1,0},{2,3},{3,2},{4,5},{5,4},{6,7},{7,6},{8,9},{9,8},{10,11... | collective-permute-start | bytes 1253384 | tf_op jit(solution)/shard_map/exchange_rows/ppermute | solution.py:175
  59.3 1.8 %collective-permute-start.5 = (bf16[96,2176]{1,0:T(8,128)(2,1)S(1)}, bf16[96,2176]{1,0:T(8,128)(2,1)S(1)}, u32[]{:S(2)}, u32[]{:S(2)}) collective-permute-start(bf16[96,2176]{1,0:T(8,128)(2,1)S(1)} %collective-permute-done.4), channel_id=1, source_target_pairs={{0,1},{1,0},{2,3},{3,2},{4,5},{5,4},{6,7},{7,6},{8,9},{9,8},{10,11... | collective-permute-start | bytes 1253384 | tf_op jit(solution)/shard_map/exchange_rows/ppermute | solution.py:175
  59.3 2.3 %collective-permute-start.21 = (bf16[96,2048]{1,0:T(8,128)(2,1)S(1)}, bf16[96,2048]{1,0:T(8,128)(2,1)S(1)}, u32[]{:S(2)}, u32[]{:S(2)}) collective-permute-start(bf16[96,2048]{1,0:T(8,128)(2,1)S(1)} %pad_maximum_fusion.3), channel_id=1, source_target_pairs={{0,1},{1,0},{2,3},{3,2},{4,5},{5,4},{6,7},{7,6},{8,9},{9,8},{10,11... | collective-permute-start | bytes 1179656 | tf_op jit(solution)/shard_map/exchange_rows/ppermute | solution.py:175
  59.8 2.4 %collective-permute-start.10 = (bf16[96,2176]{1,0:T(8,128)(2,1)S(1)}, bf16[96,2176]{1,0:T(8,128)(2,1)S(1)}, u32[]{:S(2)}, u32[]{:S(2)}) collective-permute-start(bf16[96,2176]{1,0:T(8,128)(2,1)S(1)} %pad_maximum_fusion.1), channel_id=1, source_target_pairs={{0,1},{1,0},{2,3},{3,2},{4,5},{5,4},{6,7},{7,6},{8,9},{9,8},{10,11... | collective-permute-start | bytes 1253384 | tf_op jit(solution)/shard_map/exchange_rows/ppermute | solution.py:175

commit v3 on v2

v3 whole, which is shorter than its diff:
```python
import functools

import jax
import jax.numpy as jnp
from jax import lax
from jax.experimental import pallas as pl
from jax.experimental.pallas import tpu as pltpu
from jax.sharding import PartitionSpec as P

EXPERTS = 32
BLOCK = 64
ROWS_BLOCK = 24
MOST = 7
ITERS = 2
LANES = 128
MIB = 1024 * 1024
SPARE = 6

step_rate = 0.2

F32 = jnp.float32
BF16 = jnp.bfloat16


def dot_nn(a, b):
    return jnp.dot(a, b, preferred_element_type=F32)


def dot_nt(a, b):
    return lax.dot_general(a, b, (((1,), (1,)), ((), ())), preferred_element_type=F32)


def cuts_of(width, chunk):
    return [pl.ds(start, chunk) for start in range(0, width, chunk)]


def load_kernel(n_marks, *refs):
    base_ref, dual_ref, base_out, dual_out, sems = refs[n_marks:]
    copies = [
        pltpu.make_async_copy(base_ref, base_out, sems.at[0]),
        pltpu.make_async_copy(dual_ref, dual_out, sems.at[1]),
    ]
    for copy in copies:
        copy.start()
    for copy in copies:
        copy.wait()


def load(marks, base_weight, dual_start):
    anywhere = pl.BlockSpec(memory_space=pl.ANY)
    return pl.pallas_call(
        functools.partial(load_kernel, len(marks)),
        in_specs=[anywhere] * (len(marks) + 2),
        out_specs=[anywhere, anywhere],
        out_shape=[pltpu.VMEM(x.shape, x.dtype) for x in (base_weight, dual_start)],
        scratch_shapes=[pltpu.SemaphoreType.DMA((2,))],
        compiler_params=pltpu.CompilerParams(vmem_limit_bytes=16 * MIB),
        cost_estimate=pl.CostEstimate(flops=0, bytes_accessed=6 * base_weight.size, transcendentals=0),
    )(*marks, base_weight, dual_start)


def fused_kernel(chunk, topk, halves, *refs):
    gathered = refs[:halves]
    base_ref, _, keep_ref, weight_hbm, dual_hbm, dual, *refs = refs[halves:]
    rows, across, held, rank, hits, mask, weight_sems, dual_sems = refs
    expert = pl.program_id(0)
    tokens = gathered[0].shape[0]
    slots, width = rows.shape
    part_width = width // halves
    local, tall, _ = base_ref.shape
    cuts = cuts_of(width, chunk)
    parts = [slice(start, start + BLOCK) for start in range(0, tall, BLOCK)]

    def weight_copy(at, i):
        return pltpu.make_async_copy(held.at[:, cuts[i]], weight_hbm.at[at, :, cuts[i]], weight_sems.at[i])

    def dual_copy(at, i):
        return pltpu.make_async_copy(dual.at[at, :, cuts[i]], dual_hbm.at[at, :, cuts[i]], dual_sems.at[at, i])

    @pl.when(expert == 0)
    def _():
        named = gathered[0][:, pl.ds(part_width, LANES)].astype(F32).T[:topk, :]
        for own in range(local):
            label = (lax.axis_index("exp") * local + own).astype(F32)
            hits[own : own + 1, :] = jnp.max(jnp.where(named == label, 1.0, 0.0), axis=0, keepdims=True)
        earlier = lax.broadcasted_iota(jnp.int32, (tokens, tokens), 0)
        later = lax.broadcasted_iota(jnp.int32, (tokens, tokens), 1)
        ahead = jnp.where(earlier < later, 1.0, 0.0).astype(BF16)
        rank[...] = dot_nn(hits[...].astype(BF16), ahead)
        count = keep_ref.shape[2]
        at = lax.broadcasted_iota(jnp.int32, (count, width), 0) * BLOCK
        column = lax.broadcasted_iota(jnp.int32, (count, width), 1)
        wide = jnp.where((column >= at) & (column < at + BLOCK), 1.0, 0.0).astype(BF16)
        for own in range(local):
            mask[own] = dot_nn(keep_ref[own].astype(F32).astype(BF16), wide)

    hit = hits[pl.ds(expert, 1), :]
    place = rank[pl.ds(expert, 1), :]
    slot = lax.broadcasted_iota(jnp.int32, (slots, tokens), 0).astype(F32)
    taken = jnp.where((slot == place) & (hit > 0.5), 1.0, 0.0).astype(BF16)
    rate = step_rate / jnp.sum(hit, axis=1, keepdims=True)
    resid = jnp.zeros((tall, slots), F32)
    for cut in cuts:
        half, start = divmod(cut.start, part_width)
        picked = dot_nn(taken, gathered[half][:, pl.ds(start, chunk)])
        rows[:, cut] = picked.astype(BF16)
        across[cut, :] = picked.T.astype(BF16)
        deltas = [
            base_ref[expert, part, cut] * (mask[expert, i : i + 1, cut] - 1.0).astype(BF16) for i, part in enumerate(parts)
        ]
        resid = resid + dot_nn(jnp.concatenate(deltas, axis=0), across[cut, :])
    resid = resid.astype(BF16)

    @pl.when(expert > 0)
    def _():
        for i in range(len(cuts)):
            weight_copy(expert - 1, i).wait()

    after = jnp.zeros((tall, slots), F32)
    for cut in cuts:
        grad = dot_nn(resid, rows[:, cut])
        deltas = []
        for i, part in enumerate(parts):
            base = base_ref[expert, part, cut].astype(F32)
            weight = mask[expert, i : i + 1, cut] * base - step_rate * dual[expert, part, cut] - rate * grad[part, :]
            held[part, cut] = weight
            deltas.append((weight - base).astype(BF16))
        after = after + dot_nn(jnp.concatenate(deltas, axis=0), across[cut, :])
    resid = after.astype(BF16)

    for n, cut in enumerate(cuts):
        grad = dot_nn(resid, rows[:, cut])
        for i, part in enumerate(parts):
            keep = mask[expert, i : i + 1, cut]
            weight = held[part, cut]
            both = weight + dual[expert, part, cut]
            weight = (1.0 - step_rate) * weight - (step_rate - 2.0 * step_rate * keep) * both - rate * grad[part, :]
            held[part, cut] = weight
            dual[expert, part, cut] = (1.0 - keep) * (both + weight)
        weight_copy(expert, n).start()
        dual_copy(expert, n).start()

    @pl.when(expert == local - 1)
    def _():
        for i in range(len(cuts)):
            weight_copy(expert, i).wait()
        for at in range(local):
            for i in range(len(cuts)):
                dual_copy(at, i).wait()


def fused(gathered, base_weight, keep_mask, dual_start, topk):
    local, tall, width = base_weight.shape
    chunk = 512
    tokens = gathered[0].shape[0]
    slots = min(-(-tokens // ROWS_BLOCK) * MOST, tokens)
    slots = -(-slots // LANES) * LANES
    whole = pl.BlockSpec(memory_space=pltpu.VMEM)
    anywhere = pl.BlockSpec(memory_space=pl.ANY)
    out = jax.ShapeDtypeStruct(dual_start.shape, F32)
    macs = local * slots * width * (4 * tall + tokens)
    scoped = 4 * tall * width + 4 * slots * (width + tokens) + SPARE * MIB
    held = [pltpu.with_memory_space_constraint(x, pltpu.VMEM) for x in (*gathered, base_weight, dual_start)]
    outs = pl.pallas_call(
        functools.partial(fused_kernel, chunk, topk, len(gathered)),
        grid=(local,),
        in_specs=[whole] * (len(held) + 1),
        out_specs=[anywhere, anywhere, whole],
        out_shape=[out, out, pltpu.VMEM(dual_start.shape, F32)],
        input_output_aliases={len(held) - 1: 2},
        scratch_shapes=[
            pltpu.VMEM((slots, width), BF16),
            pltpu.VMEM((width, slots), BF16),
            pltpu.VMEM((tall, width), F32),
            pltpu.VMEM((local, tokens), F32),
            pltpu.VMEM((local, tokens), F32),
            pltpu.VMEM((local, keep_mask.shape[1], width), F32),
            pltpu.SemaphoreType.DMA((width // chunk,)),
            pltpu.SemaphoreType.DMA((local, width // chunk)),
        ],
        compiler_params=pltpu.CompilerParams(vmem_limit_bytes=scoped, dimension_semantics=("arbitrary",)),
        cost_estimate=pl.CostEstimate(flops=2 * macs, bytes_accessed=8 * base_weight.size, transcendentals=0),
    )(*held, keep_mask)
    return outs[0], outs[1]


def plain(gathered, base_weight, keep_mask, dual, topk):
    local, _, width = base_weight.shape
    part = width // len(gathered)
    routes = gathered[0][:, part : part + topk].astype(jnp.int32)
    rows = jnp.concatenate([piece[:, :part] for piece in gathered], axis=1)
    tokens = rows.shape[0]
    slots = min(-(-tokens // ROWS_BLOCK) * MOST, tokens)
    labels = lax.axis_index("exp") * local + jnp.arange(local, dtype=jnp.int32)
    hits = jnp.any(routes[:, :, None] == labels, axis=1)
    rank = jnp.cumsum(hits.astype(jnp.int32), axis=0) - 1
    taken = hits[:, :, None] & (rank[:, :, None] == jnp.arange(slots, dtype=jnp.int32))
    picked = jnp.einsum("rls,rd->lsd", taken.astype(BF16), rows, preferred_element_type=F32).astype(BF16)
    rate = (step_rate / jnp.sum(hits.astype(F32), axis=0))[:, None, None]
    mask = jnp.repeat(jnp.repeat(keep_mask.astype(F32), BLOCK, 1), BLOCK, 2)
    base = base_weight.astype(F32)
    weight = zed = mask * base
    for _ in range(ITERS):
        delta = (weight - base).astype(BF16)
        resid = jnp.einsum("lnd,lcd->lcn", picked, delta, preferred_element_type=F32).astype(BF16)
        grad = jnp.einsum("lcn,lnd->lcd", resid, picked, preferred_element_type=F32)
        weight = weight - rate * grad - step_rate * (weight - zed + dual)
        zed = mask * (weight + dual)
        dual = dual + weight - zed
    return weight, dual


def spread(own):
    n_tok, n_exp = lax.axis_size("tok"), lax.axis_size("exp")
    top = n_exp.bit_length() - 1
    assert 1 << top == n_exp

    def swap(piece, bit):
        return lax.ppermute(piece, "exp", [(i, i ^ (1 << bit)) for i in range(n_exp)])

    column = [own]
    for shift in range(1, n_tok):
        column.append(lax.ppermute(own, "tok", [(i, (i + shift) % n_tok) for i in range(n_tok)]))
    pieces = {0: jnp.concatenate(column, axis=0)}
    if top == 3:
        one, two = swap(pieces[0], 1), swap(pieces[0], 2)
        middle = own.shape[1] // 2 // LANES * LANES
        far = jnp.concatenate([swap(one[:, :middle], 2), swap(two[:, middle:], 1)], axis=1)
        pieces.update({2: one, 4: two, 6: far})
    else:
        for bit in range(1, top):
            pieces.update({at ^ (1 << bit): swap(piece, bit) for at, piece in pieces.items()})
    pieces.update({at ^ 1: swap(piece, 0) for at, piece in pieces.items()})
    first = [pieces[i] for i in range(n_exp) if i > 1 and i.bit_count() == 1]
    return jnp.concatenate([pieces[i] for i in range(n_exp)], axis=0), first


def on_device(x_rows, routes, base_weight, keep_mask, dual_start):
    local, hidden, width = base_weight.shape
    topk = routes.shape[1]
    halves = 2
    part = width // halves
    named = jnp.pad(routes.astype(BF16), ((0, 0), (0, LANES - topk)))
    sent = [x_rows[:, h * part : (h + 1) * part] for h in range(halves)]
    sent[0] = jnp.concatenate([sent[0], named], axis=1)
    with jax.named_scope("exchange_rows"):
        gathered, marks = zip(*[spread(own) for own in sent])
    if 2 * gathered[0].shape[0] * width > 16 * MIB:
        return plain(gathered, base_weight, keep_mask, dual_start, topk)
    with jax.named_scope("load_weights"):
        base_weight, dual_start = load(marks[-1], base_weight, dual_start)
    with jax.named_scope("fused_iterations"):
        return fused(gathered, base_weight, keep_mask, dual_start, topk)


def solution(mesh):
    return jax.shard_map(
        on_device,
        mesh=mesh,
        in_specs=(
            P(("tok", "exp"), None),
            P(("tok", "exp"), None),
            P("exp", "tok", None),
            P("exp", "tok", None),
            P("exp", "tok", None),
        ),
        out_specs=(P("exp", "tok", None), P("exp", "tok", None)),
        check_vma=False,
    )
```

time: 114 us -> 98.1 us (0.86)
  Pallas kernels: 63.3 us -> 48.5 us
  local copies, waits for them, and re-layouts: 3.6 us -> 5.79 us
  waiting for transfers between devices: 22.4 us -> 20.5 us
    pallas_call x1, Pallas kernels: 51.5 us -> 36.6 us  [fused(): pl.pallas_call(functools.partial(fused_kernel, chunk, topk, len(gathered)...]
    unnamed x21 -> x23, local copies, waits for them, and re-layouts: 1.78 us -> 3.96 us
    ppermute x16, waiting for transfers between devices: 17.2 us -> 15.6 us  [swap(): return lax.ppermute(piece, 'exp', [(i, i ^ 1 << bit) for i in range(n_exp)])]
  transfers between devices with their start and end apart: 22 -> 22, of which waited for: 8 -> 8; matrix products, arithmetic and copies ran while one was open for 3% -> 5% of each run, Pallas kernels for 10% -> 12%
where the time goes in v3:
time: 98.1 us; the launch traced here: 97.8 us
  Pallas kernels  48.5 us (49%)
  starting transfers between devices  21.3 us (22%)
  waiting for transfers between devices  20.5 us (21%)
  local copies, waits for them, and re-layouts  5.79 us (6%)
    pallas_call x1, Pallas kernels, fused(): pl.pallas_call(functools.partial(fused_kernel, chunk, topk, len(gathered)...  36.6 us
    ppermute x16, waiting for transfers between devices, swap(): return lax.ppermute(piece, 'exp', [(i, i ^ 1 << bit) for i in range(n_exp)])  15.6 us
    pallas_call x1, Pallas kernels, load(): pl.pallas_call(functools.partial(load_kernel, len(marks)), in_specs=[anyw...  11.9 us
    ppermute x6, starting transfers between devices, spread(): lax.ppermute(own, 'tok', [(i, (i + shift) % n_tok) for i in range(n_tok)])  11.9 us
    ppermute x16, starting transfers between devices, swap(): return lax.ppermute(piece, 'exp', [(i, i ^ 1 << bit) for i in range(n_exp)])  9.39 us
    ppermute x6, waiting for transfers between devices, spread(): lax.ppermute(own, 'tok', [(i, (i + shift) % n_tok) for i in range(n_tok)])  4.93 us
    unnamed x23, local copies, waits for them, and re-layouts  3.96 us
  transfers between devices with their start and end apart: 22, of which 8 were waited for; matrix products, arithmetic and copies ran while one was open for 5% of the time, Pallas kernels for 12%

profile of v3, /device:TPU:0, one launch (start us, length us, event | category | flops | bytes accessed | tf_op | source)
XLA Modules:
  0.0 97.8 jit_solution(4945165854789745111)
XLA Ops:
  0.6 1.6 %fusion = (bf16[24,2048]{1,0:T(8,128)(2,1)S(1)}, bf16[768,2048]{1,0:T(8,128)(2,1)}, bf16[24,2048]{1,0:T(8,128)(2,1)S(1)}) fusion(bf16[24,4096]{1,0:T(8,128)(2,1)} %param.5), kind=kLoop, calls=%fused_computation.29 | loop fusion | bytes 491520 | tf_op jit(solution)/shard_map/slice | solution.py:244
  2.2 5.0 %collective-permute-start.13 = (bf16[24,2048]{1,0:T(8,128)(2,1)S(1)}, bf16[24,2048]{1,0:T(8,128)(2,1)S(1)}, u32[]{:S(2)}, u32[]{:S(2)}) collective-permute-start(bf16[24,2048]{1,0:T(8,128)(2,1)S(1)} %get-tuple-element.10), channel_id=1, source_target_pairs={{0,24},{8,0},{16,8},{24,16},{1,25},{9,1},{17,9},{25,17},{2,26},{10... | collective-permute-start | bytes 294920 | tf_op jit(solution)/shard_map/exchange_rows/ppermute | solution.py:223
  7.3 1.0 %collective-permute-start.11 = (bf16[24,2048]{1,0:T(8,128)(2,1)S(1)}, bf16[24,2048]{1,0:T(8,128)(2,1)S(1)}, u32[]{:S(2)}, u32[]{:S(2)}) collective-permute-start(bf16[24,2048]{1,0:T(8,128)(2,1)S(1)} %get-tuple-element.10), channel_id=1, source_target_pairs={{0,8},{8,16},{16,24},{24,0},{1,9},{9,17},{17,25},{25,1},{2,10},{10... | collective-permute-start | bytes 294920 | tf_op jit(solution)/shard_map/exchange_rows/ppermute | solution.py:223
  8.3 0.7 convert_element_type.5
  9.1 2.0 %collective-permute-start.1 = (bf16[24,2176]{1,0:T(8,128)(2,1)S(1)}, bf16[24,2176]{1,0:T(8,128)(2,1)S(1)}, u32[]{:S(2)}, u32[]{:S(2)}) collective-permute-start(bf16[24,2176]{1,0:T(8,128)(2,1)S(1)} %get-tuple-element.13), channel_id=1, source_target_pairs={{0,16},{8,24},{16,0},{24,8},{1,17},{9,25},{17,1},{25,9},{2,18},{10... | collective-permute-start | bytes 313352 | tf_op jit(solution)/shard_map/exchange_rows/ppermute | solution.py:223
  11.1 1.5 %collective-permute-start = (bf16[24,2176]{1,0:T(8,128)(2,1)S(1)}, bf16[24,2176]{1,0:T(8,128)(2,1)S(1)}, u32[]{:S(2)}, u32[]{:S(2)}) collective-permute-start(bf16[24,2176]{1,0:T(8,128)(2,1)S(1)} %get-tuple-element.13), channel_id=1, source_target_pairs={{0,8},{8,16},{16,24},{24,0},{1,9},{9,17},{17,25},{25,1},{2,10},{10... | collective-permute-start | bytes 313352 | tf_op jit(solution)/shard_map/exchange_rows/ppermute | solution.py:223
  12.6 1.3 %copy.11.refs_4_ = s32[4,6,64]{2,1,0:T(8,128)} copy(s32[4,6,64]{2,0,1:T(4,128)} %param.8) | data formatting | bytes 12288 | tf_op args[3]
  13.9 2.4 %collective-permute-start.2 = (bf16[24,2176]{1,0:T(8,128)(2,1)S(1)}, bf16[24,2176]{1,0:T(8,128)(2,1)S(1)}, u32[]{:S(2)}, u32[]{:S(2)}) collective-permute-start(bf16[24,2176]{1,0:T(8,128)(2,1)S(1)} %get-tuple-element.13), channel_id=1, source_target_pairs={{0,24},{8,0},{16,8},{24,16},{1,25},{9,1},{17,9},{25,17},{2,26},{10... | collective-permute-start | bytes 313352 | tf_op jit(solution)/shard_map/exchange_rows/ppermute | solution.py:223
  16.2 4.9 %collective-permute-done.12 = bf16[24,2048]{1,0:T(8,128)(2,1)S(1)} collective-permute-done((bf16[24,2048]{1,0:T(8,128)(2,1)S(1)}, bf16[24,2048]{1,0:T(8,128)(2,1)S(1)}, u32[]{:S(2)}, u32[]{:S(2)}) %collective-permute-start.12) | collective-permute-done | bytes 98336 | tf_op jit(solution)/shard_map/exchange_rows/ppermute | solution.py:223
  21.2 1.6 %collective-permute-start.17 = (bf16[96,2048]{1,0:T(8,128)(2,1)S(1)}, bf16[96,2048]{1,0:T(8,128)(2,1)S(1)}, u32[]{:S(2)}, u32[]{:S(2)}) collective-permute-start(bf16[96,2048]{1,0:T(8,128)(2,1)S(1)} %pad_maximum_fusion.2), channel_id=1, source_target_pairs={{0,4},{1,5},{2,6},{3,7},{4,0},{5,1},{6,2},{7,3},{8,12},{9,13},{10,... | collective-permute-start | bytes 1179656 | tf_op jit(solution)/shard_map/exchange_rows/ppermute | solution.py:219
  22.8 1.5 %collective-permute-start.15 = (bf16[96,2048]{1,0:T(8,128)(2,1)S(1)}, bf16[96,2048]{1,0:T(8,128)(2,1)S(1)}, u32[]{:S(2)}, u32[]{:S(2)}) collective-permute-start(bf16[96,2048]{1,0:T(8,128)(2,1)S(1)} %pad_maximum_fusion.2), channel_id=1, source_target_pairs={{0,2},{1,3},{2,0},{3,1},{4,6},{5,7},{6,4},{7,5},{8,10},{9,11},{10,... | collective-permute-start | bytes 1179656 | tf_op jit(solution)/shard_map/exchange_rows/ppermute | solution.py:219
  24.3 0.6 constant_dynamic-update-slice_fusion.20
  24.9 0.6 constant_dynamic-update-slice_fusion.19
  25.6 0.6 constant_dynamic-update-slice_fusion.18
  26.3 0.6 collective-permute-start.6
  27.4 5.1 %collective-permute-done.17.refs_1_ = bf16[96,2048]{1,0:T(8,128)(2,1)S(1)} collective-permute-done((bf16[96,2048]{1,0:T(8,128)(2,1)S(1)}, bf16[96,2048]{1,0:T(8,128)(2,1)S(1)}, u32[]{:S(2)}, u32[]{:S(2)}) %collective-permute-start.17) | collective-permute-done | bytes 393248 | tf_op jit(solution)/shard_map/exchange_rows/ppermute | solution.py:219
  32.5 2.2 %collective-permute-done.15.refs_0_ = bf16[96,2048]{1,0:T(8,128)(2,1)S(1)} collective-permute-done((bf16[96,2048]{1,0:T(8,128)(2,1)S(1)}, bf16[96,2048]{1,0:T(8,128)(2,1)S(1)}, u32[]{:S(2)}, u32[]{:S(2)}) %collective-permute-start.15) | collective-permute-done | bytes 393248 | tf_op jit(solution)/shard_map/exchange_rows/ppermute | solution.py:219
  34.7 1.6 %collective-permute-start.20 = (bf16[96,1024]{1,0:T(8,128)(2,1)S(1)}, bf16[96,1024]{1,0:T(8,128)(2,1)S(1)}, u32[]{:S(2)}, u32[]{:S(2)}) collective-permute-start(bf16[96,1024]{1,0:T(8,128)(2,1)S(1)} %slice.27), channel_id=1, source_target_pairs={{0,2},{1,3},{2,0},{3,1},{4,6},{5,7},{6,4},{7,5},{8,10},{9,11},{10,... | collective-permute-start | bytes 589832 | tf_op jit(solution)/shard_map/exchange_rows/ppermute | solution.py:219
  36.3 11.9 %load_weights.1 = (bf16[4,384,4096]{2,1,0:T(8,128)(2,1)S(1)}, f32[4,384,4096]{2,1,0:T(8,128)S(1)}) custom-call(bf16[96,2048]{1,0:T(8,128)(2,1)S(1)} %collective-permute-done.15.refs_0_, bf16[96,2048]{1,0:T(8,128)(2,1)S(1)} %collective-permute-done.17.refs_1_, bf16[4,384,4096]{2,1,0:T(8,128)(2,1)} %refs_2_.1, f32[4,384,4096]{2,1,0:T(8,128)} %refs_3_.1), custom_call_target="tpu_custom_call" | custom-call | bytes 37748736 | tf_op jit(solution)/shard_map/load_weights/pallas_call | solution.py:51
  50.3 1.5 %collective-permute-start.8 = (bf16[96,1024]{1,0:T(8,128)(2,1)S(1)}, bf16[96,1024]{1,0:T(8,128)(2,1)S(1)}, u32[]{:S(2)}, u32[]{:S(2)}) collective-permute-start(bf16[96,1024]{1,0:T(8,128)(2,1)S(1)} %slice.24), channel_id=1, source_target_pairs={{0,4},{1,5},{2,6},{3,7},{4,0},{5,1},{6,2},{7,3},{8,12},{9,13},{10,... | collective-permute-start | bytes 589832 | tf_op jit(solution)/shard_map/exchange_rows/ppermute | solution.py:219
  51.8 3.5 %collective-permute-done.19 = bf16[96,1024]{1,0:T(8,128)(2,1)S(1)} collective-permute-done((bf16[96,1024]{1,0:T(8,128)(2,1)S(1)}, bf16[96,1024]{1,0:T(8,128)(2,1)S(1)}, u32[]{:S(2)}, u32[]{:S(2)}) %collective-permute-start.19) | collective-permute-done | bytes 196640 | tf_op jit(solution)/shard_map/exchange_rows/ppermute | solution.py:219
  55.3 2.9 %collective-permute-done.8 = bf16[96,1024]{1,0:T(8,128)(2,1)S(1)} collective-permute-done((bf16[96,1024]{1,0:T(8,128)(2,1)S(1)}, bf16[96,1024]{1,0:T(8,128)(2,1)S(1)}, u32[]{:S(2)}, u32[]{:S(2)}) %collective-permute-start.8) | collective-permute-done | bytes 196640 | tf_op jit(solution)/shard_map/exchange_rows/ppermute | solution.py:219
  59.0 1.0 collective-permute-done.5
  61.2 36.6 %fused_iterations.1 = (f32[4,384,4096]{2,1,0:T(8,128)}, f32[4,384,4096]{2,1,0:T(8,128)}, f32[4,384,4096]{2,1,0:T(8,128)S(1)}) custom-call(bf16[768,2176]{1,0:T(8,128)(2,1)S(1)} %constant_dynamic-update-slice_fusion.refs_0_, bf16[768,2048]{1,0:T(8,128)(2,1)S(1)} %constant_dynamic-update-slice_fusion.11.refs_1_, ...), custom_call_target="tpu_custom_call", output_to_operand_aliasing={{2}: (3, {})} | custom-call | flops 19327352832 | bytes 50331648 | tf_op jit(solution)/shard_map/fused_iterations/pallas_call | solution.py:164
  (60 shorter events, 4.7 us)
Async XLA Ops:
  2.2 11.6 %collective-permute-start.13 = (bf16[24,2048]{1,0:T(8,128)(2,1)S(1)}, bf16[24,2048]{1,0:T(8,128)(2,1)S(1)}, u32[]{:S(2)}, u32[]{:S(2)}) collective-permute-start(bf16[24,2048]{1,0:T(8,128)(2,1)S(1)} %get-tuple-element.10), channel_id=1, source_target_pairs={{0,24},{8,0},{16,8},{24,16},{1,25},{9,1},{17,9},{25,17},{2,26},{10... | collective-permute-start | bytes 294920 | tf_op jit(solution)/shard_map/exchange_rows/ppermute | solution.py:223
  7.3 13.9 %collective-permute-start.12 = (bf16[24,2048]{1,0:T(8,128)(2,1)S(1)}, bf16[24,2048]{1,0:T(8,128)(2,1)S(1)}, u32[]{:S(2)}, u32[]{:S(2)}) collective-permute-start(bf16[24,2048]{1,0:T(8,128)(2,1)S(1)} %get-tuple-element.10), channel_id=1, source_target_pairs={{0,16},{8,24},{16,0},{24,8},{1,17},{9,25},{17,1},{25,9},{2,18},{10... | collective-permute-start | bytes 294920 | tf_op jit(solution)/shard_map/exchange_rows/ppermute | solution.py:223
  7.3 13.9 %collective-permute-start.11 = (bf16[24,2048]{1,0:T(8,128)(2,1)S(1)}, bf16[24,2048]{1,0:T(8,128)(2,1)S(1)}, u32[]{:S(2)}, u32[]{:S(2)}) collective-permute-start(bf16[24,2048]{1,0:T(8,128)(2,1)S(1)} %get-tuple-element.10), channel_id=1, source_target_pairs={{0,8},{8,16},{16,24},{24,0},{1,9},{9,17},{17,25},{25,1},{2,10},{10... | collective-permute-start | bytes 294920 | tf_op jit(solution)/shard_map/exchange_rows/ppermute | solution.py:223
  9.1 17.1 %collective-permute-start.1 = (bf16[24,2176]{1,0:T(8,128)(2,1)S(1)}, bf16[24,2176]{1,0:T(8,128)(2,1)S(1)}, u32[]{:S(2)}, u32[]{:S(2)}) collective-permute-start(bf16[24,2176]{1,0:T(8,128)(2,1)S(1)} %get-tuple-element.13), channel_id=1, source_target_pairs={{0,16},{8,24},{16,0},{24,8},{1,17},{9,25},{17,1},{25,9},{2,18},{10... | collective-permute-start | bytes 313352 | tf_op jit(solution)/shard_map/exchange_rows/ppermute | solution.py:223
  11.1 15.1 %collective-permute-start = (bf16[24,2176]{1,0:T(8,128)(2,1)S(1)}, bf16[24,2176]{1,0:T(8,128)(2,1)S(1)}, u32[]{:S(2)}, u32[]{:S(2)}) collective-permute-start(bf16[24,2176]{1,0:T(8,128)(2,1)S(1)} %get-tuple-element.13), channel_id=1, source_target_pairs={{0,8},{8,16},{16,24},{24,0},{1,9},{9,17},{17,25},{25,1},{2,10},{10... | collective-permute-start | bytes 313352 | tf_op jit(solution)/shard_map/exchange_rows/ppermute | solution.py:223
  13.9 12.4 %collective-permute-start.2 = (bf16[24,2176]{1,0:T(8,128)(2,1)S(1)}, bf16[24,2176]{1,0:T(8,128)(2,1)S(1)}, u32[]{:S(2)}, u32[]{:S(2)}) collective-permute-start(bf16[24,2176]{1,0:T(8,128)(2,1)S(1)} %get-tuple-element.13), channel_id=1, source_target_pairs={{0,24},{8,0},{16,8},{24,16},{1,25},{9,1},{17,9},{25,17},{2,26},{10... | collective-permute-start | bytes 313352 | tf_op jit(solution)/shard_map/exchange_rows/ppermute | solution.py:223
  21.2 11.3 %collective-permute-start.17 = (bf16[96,2048]{1,0:T(8,128)(2,1)S(1)}, bf16[96,2048]{1,0:T(8,128)(2,1)S(1)}, u32[]{:S(2)}, u32[]{:S(2)}) collective-permute-start(bf16[96,2048]{1,0:T(8,128)(2,1)S(1)} %pad_maximum_fusion.2), channel_id=1, source_target_pairs={{0,4},{1,5},{2,6},{3,7},{4,0},{5,1},{6,2},{7,3},{8,12},{9,13},{10,... | collective-permute-start | bytes 1179656 | tf_op jit(solution)/shard_map/exchange_rows/ppermute | solution.py:219
  22.8 12.0 %collective-permute-start.15 = (bf16[96,2048]{1,0:T(8,128)(2,1)S(1)}, bf16[96,2048]{1,0:T(8,128)(2,1)S(1)}, u32[]{:S(2)}, u32[]{:S(2)}) collective-permute-start(bf16[96,2048]{1,0:T(8,128)(2,1)S(1)} %pad_maximum_fusion.2), channel_id=1, source_target_pairs={{0,2},{1,3},{2,0},{3,1},{4,6},{5,7},{6,4},{7,5},{8,10},{9,11},{10,... | collective-permute-start | bytes 1179656 | tf_op jit(solution)/shard_map/exchange_rows/ppermute | solution.py:219
  26.2 22.1 %collective-permute-start.14 = (bf16[96,2048]{1,0:T(8,128)(2,1)S(1)}, bf16[96,2048]{1,0:T(8,128)(2,1)S(1)}, u32[]{:S(2)}, u32[]{:S(2)}) collective-permute-start(bf16[96,2048]{1,0:T(8,128)(2,1)S(1)} %pad_maximum_fusion.2), channel_id=1, source_target_pairs={{0,1},{1,0},{2,3},{3,2},{4,5},{5,4},{6,7},{7,6},{8,9},{9,8},{10,11... | collective-permute-start | bytes 1179656 | tf_op jit(solution)/shard_map/exchange_rows/ppermute | solution.py:219
  26.3 22.8 %collective-permute-start.6 = (bf16[96,2176]{1,0:T(8,128)(2,1)S(1)}, bf16[96,2176]{1,0:T(8,128)(2,1)S(1)}, u32[]{:S(2)}, u32[]{:S(2)}) collective-permute-start(bf16[96,2176]{1,0:T(8,128)(2,1)S(1)} %pad_maximum_fusion), channel_id=1, source_target_pairs={{0,4},{1,5},{2,6},{3,7},{4,0},{5,1},{6,2},{7,3},{8,12},{9,13},{10,... | collective-permute-start | bytes 1253384 | tf_op jit(solution)/shard_map/exchange_rows/ppermute | solution.py:219
  26.8 22.3 %collective-permute-start.4 = (bf16[96,2176]{1,0:T(8,128)(2,1)S(1)}, bf16[96,2176]{1,0:T(8,128)(2,1)S(1)}, u32[]{:S(2)}, u32[]{:S(2)}) collective-permute-start(bf16[96,2176]{1,0:T(8,128)(2,1)S(1)} %pad_maximum_fusion), channel_id=1, source_target_pairs={{0,2},{1,3},{2,0},{3,1},{4,6},{5,7},{6,4},{7,5},{8,10},{9,11},{10,... | collective-permute-start | bytes 1253384 | tf_op jit(solution)/shard_map/exchange_rows/ppermute | solution.py:219
  32.5 17.2 %collective-permute-start.3 = (bf16[96,2176]{1,0:T(8,128)(2,1)S(1)}, bf16[96,2176]{1,0:T(8,128)(2,1)S(1)}, u32[]{:S(2)}, u32[]{:S(2)}) collective-permute-start(bf16[96,2176]{1,0:T(8,128)(2,1)S(1)} %pad_maximum_fusion), channel_id=1, source_target_pairs={{0,1},{1,0},{2,3},{3,2},{4,5},{5,4},{6,7},{7,6},{8,9},{9,8},{10,11... | collective-permute-start | bytes 1253384 | tf_op jit(solution)/shard_map/exchange_rows/ppermute | solution.py:219
  34.7 15.6 %collective-permute-start.20 = (bf16[96,1024]{1,0:T(8,128)(2,1)S(1)}, bf16[96,1024]{1,0:T(8,128)(2,1)S(1)}, u32[]{:S(2)}, u32[]{:S(2)}) collective-permute-start(bf16[96,1024]{1,0:T(8,128)(2,1)S(1)} %slice.27), channel_id=1, source_target_pairs={{0,2},{1,3},{2,0},{3,1},{4,6},{5,7},{6,4},{7,5},{8,10},{9,11},{10,... | collective-permute-start | bytes 589832 | tf_op jit(solution)/shard_map/exchange_rows/ppermute | solution.py:219
  36.3 12.6 %copy-start = (bf16[768,2048]{1,0:T(8,128)(2,1)S(1)}, bf16[768,2048]{1,0:T(8,128)(2,1)}, u32[]{:S(2)}) copy-start(bf16[768,2048]{1,0:T(8,128)(2,1)} %constant_dynamic-update-slice_fusion.18) | copy-start | bytes 9437188
  48.3 7.0 %collective-permute-start.19 = (bf16[96,1024]{1,0:T(8,128)(2,1)S(1)}, bf16[96,1024]{1,0:T(8,128)(2,1)S(1)}, u32[]{:S(2)}, u32[]{:S(2)}) collective-permute-start(bf16[96,1024]{1,0:T(8,128)(2,1)S(1)} %slice.26), channel_id=1, source_target_pairs={{0,4},{1,5},{2,6},{3,7},{4,0},{5,1},{6,2},{7,3},{8,12},{9,13},{10,... | collective-permute-start | bytes 589832 | tf_op jit(solution)/shard_map/exchange_rows/ppermute | solution.py:219
  49.0 9.9 %collective-permute-start.18 = (bf16[96,2048]{1,0:T(8,128)(2,1)S(1)}, bf16[96,2048]{1,0:T(8,128)(2,1)S(1)}, u32[]{:S(2)}, u32[]{:S(2)}) collective-permute-start(bf16[96,2048]{1,0:T(8,128)(2,1)S(1)} %collective-permute-done.17.refs_1_), channel_id=1, source_target_pairs={{0,1},{1,0},{2,3},{3,2},{4,5},{5,4},{6,7},{7,6},{8,9},{9,8},{10,11... | collective-permute-start | bytes 1179656 | tf_op jit(solution)/shard_map/exchange_rows/ppermute | solution.py:219
  49.1 9.6 %collective-permute-start.16 = (bf16[96,2048]{1,0:T(8,128)(2,1)S(1)}, bf16[96,2048]{1,0:T(8,128)(2,1)S(1)}, u32[]{:S(2)}, u32[]{:S(2)}) collective-permute-start(bf16[96,2048]{1,0:T(8,128)(2,1)S(1)} %collective-permute-done.15.refs_0_), channel_id=1, source_target_pairs={{0,1},{1,0},{2,3},{3,2},{4,5},{5,4},{6,7},{7,6},{8,9},{9,8},{10,11... | collective-permute-start | bytes 1179656 | tf_op jit(solution)/shard_map/exchange_rows/ppermute | solution.py:219
  49.7 8.5 %collective-permute-start.9 = (bf16[96,1152]{1,0:T(8,128)(2,1)S(1)}, bf16[96,1152]{1,0:T(8,128)(2,1)S(1)}, u32[]{:S(2)}, u32[]{:S(2)}) collective-permute-start(bf16[96,1152]{1,0:T(8,128)(2,1)S(1)} %slice.25), channel_id=1, source_target_pairs={{0,2},{1,3},{2,0},{3,1},{4,6},{5,7},{6,4},{7,5},{8,10},{9,11},{10,... | collective-permute-start | bytes 663560 | tf_op jit(solution)/shard_map/exchange_rows/ppermute | solution.py:219
  50.3 7.9 %collective-permute-start.8 = (bf16[96,1024]{1,0:T(8,128)(2,1)S(1)}, bf16[96,1024]{1,0:T(8,128)(2,1)S(1)}, u32[]{:S(2)}, u32[]{:S(2)}) collective-permute-start(bf16[96,1024]{1,0:T(8,128)(2,1)S(1)} %slice.24), channel_id=1, source_target_pairs={{0,4},{1,5},{2,6},{3,7},{4,0},{5,1},{6,2},{7,3},{8,12},{9,13},{10,... | collective-permute-start | bytes 589832 | tf_op jit(solution)/shard_map/exchange_rows/ppermute | solution.py:219
  55.3 4.8 %collective-permute-start.7 = (bf16[96,2176]{1,0:T(8,128)(2,1)S(1)}, bf16[96,2176]{1,0:T(8,128)(2,1)S(1)}, u32[]{:S(2)}, u32[]{:S(2)}) collective-permute-start(bf16[96,2176]{1,0:T(8,128)(2,1)S(1)} %collective-permute-done.6), channel_id=1, source_target_pairs={{0,1},{1,0},{2,3},{3,2},{4,5},{5,4},{6,7},{7,6},{8,9},{9,8},{10,11... | collective-permute-start | bytes 1253384 | tf_op jit(solution)/shard_map/exchange_rows/ppermute | solution.py:219
  58.2 1.8 %collective-permute-start.5 = (bf16[96,2176]{1,0:T(8,128)(2,1)S(1)}, bf16[96,2176]{1,0:T(8,128)(2,1)S(1)}, u32[]{:S(2)}, u32[]{:S(2)}) collective-permute-start(bf16[96,2176]{1,0:T(8,128)(2,1)S(1)} %collective-permute-done.4), channel_id=1, source_target_pairs={{0,1},{1,0},{2,3},{3,2},{4,5},{5,4},{6,7},{7,6},{8,9},{9,8},{10,11... | collective-permute-start | bytes 1253384 | tf_op jit(solution)/shard_map/exchange_rows/ppermute | solution.py:219
  58.2 2.3 %collective-permute-start.21 = (bf16[96,2048]{1,0:T(8,128)(2,1)S(1)}, bf16[96,2048]{1,0:T(8,128)(2,1)S(1)}, u32[]{:S(2)}, u32[]{:S(2)}) collective-permute-start(bf16[96,2048]{1,0:T(8,128)(2,1)S(1)} %pad_maximum_fusion.3), channel_id=1, source_target_pairs={{0,1},{1,0},{2,3},{3,2},{4,5},{5,4},{6,7},{7,6},{8,9},{9,8},{10,11... | collective-permute-start | bytes 1179656 | tf_op jit(solution)/shard_map/exchange_rows/ppermute | solution.py:219
  58.8 2.4 %collective-permute-start.10 = (bf16[96,2176]{1,0:T(8,128)(2,1)S(1)}, bf16[96,2176]{1,0:T(8,128)(2,1)S(1)}, u32[]{:S(2)}, u32[]{:S(2)}) collective-permute-start(bf16[96,2176]{1,0:T(8,128)(2,1)S(1)} %pad_maximum_fusion.1), channel_id=1, source_target_pairs={{0,1},{1,0},{2,3},{3,2},{4,5},{5,4},{6,7},{7,6},{8,9},{9,8},{10,11... | collective-permute-start | bytes 1253384 | tf_op jit(solution)/shard_map/exchange_rows/ppermute | solution.py:219

commit v4 on v3

--- a/solution.py
+++ b/solution.py
@@ -35,13 +35,14 @@
 
 
 def load_kernel(n_marks, *refs):
-    base_ref, dual_ref, base_out, dual_out, sems = refs[n_marks:]
+    base_ref, dual_ref, base_out, dual_out, token, sems = refs[n_marks:]
     copies = [
         pltpu.make_async_copy(base_ref, base_out, sems.at[0]),
         pltpu.make_async_copy(dual_ref, dual_out, sems.at[1]),
     ]
     for copy in copies:
         copy.start()
+    token[...] = jnp.ones_like(token)
     for copy in copies:
         copy.wait()
 
@@ -51,8 +52,9 @@
     return pl.pallas_call(
         functools.partial(load_kernel, len(marks)),
         in_specs=[anywhere] * (len(marks) + 2),
-        out_specs=[anywhere, anywhere],
-        out_shape=[pltpu.VMEM(x.shape, x.dtype) for x in (base_weight, dual_start)],
+        out_specs=[anywhere, anywhere, pl.BlockSpec(memory_space=pltpu.VMEM)],
+        out_shape=[pltpu.VMEM(x.shape, x.dtype) for x in (base_weight, dual_start)]
+        + [jax.ShapeDtypeStruct(marks[0].shape, BF16)],
         scratch_shapes=[pltpu.SemaphoreType.DMA((2,))],
         compiler_params=pltpu.CompilerParams(vmem_limit_bytes=16 * MIB),
         cost_estimate=pl.CostEstimate(flops=0, bytes_accessed=6 * base_weight.size, transcendentals=0),
@@ -210,45 +212,47 @@
     return weight, dual
 
 
-def spread(own):
-    n_tok, n_exp = lax.axis_size("tok"), lax.axis_size("exp")
-    top = n_exp.bit_length() - 1
-    assert 1 << top == n_exp
-
-    def swap(piece, bit):
-        return lax.ppermute(piece, "exp", [(i, i ^ (1 << bit)) for i in range(n_exp)])
-
+def after(ones, array):
+    return array * ones[: array.shape[0], : array.shape[1]]
+
+
+def swap(piece, bit):
+    n = lax.axis_size("exp")
+    return lax.ppermute(piece, "exp", [(i, i ^ (1 << bit)) for i in range(n)])
+
+
+def column_rows(own):
+    n = lax.axis_size("tok")
     column = [own]
-    for shift in range(1, n_tok):
-        column.append(lax.ppermute(own, "tok", [(i, (i + shift) % n_tok) for i in range(n_tok)]))
-    pieces = {0: jnp.concatenate(column, axis=0)}
-    if top == 3:
-        one, two = swap(pieces[0], 1), swap(pieces[0], 2)
-        middle = own.shape[1] // 2 // LANES * LANES
-        far = jnp.concatenate([swap(one[:, :middle], 2), swap(two[:, middle:], 1)], axis=1)
-        pieces.update({2: one, 4: two, 6: far})
-    else:
-        for bit in range(1, top):
-            pieces.update({at ^ (1 << bit): swap(piece, bit) for at, piece in pieces.items()})
-    pieces.update({at ^ 1: swap(piece, 0) for at, piece in pieces.items()})
-    first = [pieces[i] for i in range(n_exp) if i > 1 and i.bit_count() == 1]
-    return jnp.concatenate([pieces[i] for i in range(n_exp)], axis=0), first
+    for shift in range(1, n):
+        column.append(lax.ppermute(own, "tok", [(i, (i + shift) % n) for i in range(n)]))
+    return jnp.concatenate(column, axis=0)
 
 
 def on_device(x_rows, routes, base_weight, keep_mask, dual_start):
     local, hidden, width = base_weight.shape
     topk = routes.shape[1]
-    halves = 2
-    part = width // halves
+    n_exp = lax.axis_size("exp")
+    top = n_exp.bit_length() - 1
+    assert 1 << top == n_exp
     named = jnp.pad(routes.astype(BF16), ((0, 0), (0, LANES - topk)))
-    sent = [x_rows[:, h * part : (h + 1) * part] for h in range(halves)]
-    sent[0] = jnp.concatenate([sent[0], named], axis=1)
     with jax.named_scope("exchange_rows"):
-        gathered, marks = zip(*[spread(own) for own in sent])
-    if 2 * gathered[0].shape[0] * width > 16 * MIB:
-        return plain(gathered, base_weight, keep_mask, dual_start, topk)
+        mine = column_rows(jnp.concatenate([x_rows, named], axis=1))
+    if top != 3 or 2 * n_exp * mine.shape[0] * width > 16 * MIB:
+        pieces = {0: mine}
+        for bit in [*range(1, top), 0]:
+            pieces.update({at ^ (1 << bit): swap(piece, bit) for at, piece in pieces.items()})
+        gathered = jnp.concatenate([pieces[i] for i in range(n_exp)], axis=0)
+        return plain([gathered], base_weight, keep_mask, dual_start, topk)
     with jax.named_scope("load_weights"):
-        base_weight, dual_start = load(marks[-1], base_weight, dual_start)
+        base_weight, dual_start, token = load([mine], base_weight, dual_start)
+    with jax.named_scope("exchange_rows"):
+        one, two = swap(mine, 1), swap(mine, 2)
+        middle = mine.shape[1] // 2 // LANES * LANES
+        far = [swap(after(token, one[:, :middle]), 2), swap(after(token, two[:, middle:]), 1)]
+        pieces = [mine, one, two, jnp.concatenate(far, axis=1)]
+        pieces += [swap(piece, 0) for piece in pieces]
+    gathered = [jnp.concatenate(pieces, axis=0)]
     with jax.named_scope("fused_iterations"):
         return fused(gathered, base_weight, keep_mask, dual_start, topk)
 

time: 98.1 us -> 100 us (1.019)
  the two profiles are of different devices: /device:TPU:0 before, /device:TPU:17 now
where the time goes in v4:
time: 100 us; the launch traced here: 99.6 us
  Pallas kernels  50 us (50%)
  waiting for transfers between devices  31.5 us (32%)
  starting transfers between devices  11.3 us (11%)
  local copies, waits for them, and re-layouts  3.23 us (3%)
  other arithmetic  2.81 us (3%)
    pallas_call x1, Pallas kernels, fused(): pl.pallas_call(functools.partial(fused_kernel, chunk, topk, len(gathered)...  38.2 us
    ppermute x3, waiting for transfers between devices, column_rows(): lax.ppermute(own, 'tok', [(i, (i + shift) % n) for i in range(n)])  17.1 us
    ppermute x8, waiting for transfers between devices, swap(): return lax.ppermute(piece, 'exp', [(i, i ^ 1 << bit) for i in range(n)])  14.4 us
    pallas_call x1, Pallas kernels, load(): pl.pallas_call(functools.partial(load_kernel, len(marks)), in_specs=[anyw...  11.8 us
    ppermute x8, starting transfers between devices, swap(): return lax.ppermute(piece, 'exp', [(i, i ^ 1 << bit) for i in range(n)])  8.77 us
    ppermute x3, starting transfers between devices, column_rows(): lax.ppermute(own, 'tok', [(i, (i + shift) % n) for i in range(n)])  2.54 us
  transfers between devices with their start and end apart: 11, of which 6 were waited for; matrix products, arithmetic and copies ran while one was open for 2% of the time, Pallas kernels for 12%

profile of v4, /device:TPU:17, one launch (start us, length us, event | category | flops | bytes accessed | tf_op | source)
XLA Modules:
  0.0 99.6 jit_solution(9893278105995306074)
XLA Ops:
  0.6 0.7 convert_element_type.5
  1.4 1.0 pad_maximum_fusion.2
  2.5 1.3 %collective-permute-start = (bf16[24,4224]{1,0:T(8,128)(2,1)S(1)}, bf16[24,4224]{1,0:T(8,128)(2,1)S(1)}, u32[]{:S(2)}, u32[]{:S(2)}) collective-permute-start(bf16[24,4224]{1,0:T(8,128)(2,1)S(1)} %get-tuple-element.12), channel_id=1, source_target_pairs={{0,8},{8,16},{16,24},{24,0},{1,9},{9,17},{17,25},{25,1},{2,10},{10... | collective-permute-start | bytes 608264 | tf_op jit(solution)/shard_map/exchange_rows/ppermute | solution.py:228
  3.8 1.1 %collective-permute-start.2 = (bf16[24,4224]{1,0:T(8,128)(2,1)S(1)}, bf16[24,4224]{1,0:T(8,128)(2,1)S(1)}, u32[]{:S(2)}, u32[]{:S(2)}) collective-permute-start(bf16[24,4224]{1,0:T(8,128)(2,1)S(1)} %get-tuple-element.12), channel_id=1, source_target_pairs={{0,24},{8,0},{16,8},{24,16},{1,25},{9,1},{17,9},{25,17},{2,26},{10... | collective-permute-start | bytes 608264 | tf_op jit(solution)/shard_map/exchange_rows/ppermute | solution.py:228
  4.9 1.3 %copy.11.refs_3_ = s32[4,6,64]{2,1,0:T(8,128)} copy(s32[4,6,64]{2,0,1:T(4,128)} %param.8) | data formatting | bytes 12288 | tf_op args[3]
  6.2 9.0 %collective-permute-done.1 = bf16[24,4224]{1,0:T(8,128)(2,1)S(1)} collective-permute-done((bf16[24,4224]{1,0:T(8,128)(2,1)S(1)}, bf16[24,4224]{1,0:T(8,128)(2,1)S(1)}, u32[]{:S(2)}, u32[]{:S(2)}) %collective-permute-start.1) | collective-permute-done | bytes 202784 | tf_op jit(solution)/shard_map/exchange_rows/ppermute | solution.py:228
  15.2 8.1 %collective-permute-done = bf16[24,4224]{1,0:T(8,128)(2,1)S(1)} collective-permute-done((bf16[24,4224]{1,0:T(8,128)(2,1)S(1)}, bf16[24,4224]{1,0:T(8,128)(2,1)S(1)}, u32[]{:S(2)}, u32[]{:S(2)}) %collective-permute-start) | collective-permute-done | bytes 202784 | tf_op jit(solution)/shard_map/exchange_rows/ppermute | solution.py:228
  23.3 1.0 pad_maximum_fusion.refs_0_
  24.3 0.6 collective-permute-start.7
  24.9 1.3 %collective-permute-start.4 = (bf16[96,4224]{1,0:T(8,128)(2,1)S(1)}, bf16[96,4224]{1,0:T(8,128)(2,1)S(1)}, u32[]{:S(2)}, u32[]{:S(2)}) collective-permute-start(bf16[96,4224]{1,0:T(8,128)(2,1)S(1)} %pad_maximum_fusion.refs_0_), channel_id=1, source_target_pairs={{0,4},{1,5},{2,6},{3,7},{4,0},{5,1},{6,2},{7,3},{8,12},{9,13},{10,... | collective-permute-start | bytes 2433032 | tf_op jit(solution)/shard_map/exchange_rows/ppermute | solution.py:221
  26.1 1.2 %collective-permute-start.3 = (bf16[96,4224]{1,0:T(8,128)(2,1)S(1)}, bf16[96,4224]{1,0:T(8,128)(2,1)S(1)}, u32[]{:S(2)}, u32[]{:S(2)}) collective-permute-start(bf16[96,4224]{1,0:T(8,128)(2,1)S(1)} %pad_maximum_fusion.refs_0_), channel_id=1, source_target_pairs={{0,2},{1,3},{2,0},{3,1},{4,6},{5,7},{6,4},{7,5},{8,10},{9,11},{10,... | collective-permute-start | bytes 2433032 | tf_op jit(solution)/shard_map/exchange_rows/ppermute | solution.py:221
  27.4 11.8 %load_weights.1 = (bf16[4,384,4096]{2,1,0:T(8,128)(2,1)S(1)}, f32[4,384,4096]{2,1,0:T(8,128)S(1)}, bf16[96,4224]{1,0:T(8,128)(2,1)S(1)}) custom-call(bf16[96,4224]{1,0:T(8,128)(2,1)S(1)} %pad_maximum_fusion.refs_0_, bf16[4,384,4096]{2,1,0:T(8,128)(2,1)} %refs_1_.1, f32[4,384,4096]{2,1,0:T(8,128)} %refs_2_.1), custom_call_target="tpu_custom_call" | custom-call | bytes 37748736 | tf_op jit(solution)/shard_map/load_weights/pallas_call | solution.py:52
  39.2 6.2 %collective-permute-done.3 = bf16[96,4224]{1,0:T(8,128)(2,1)S(1)} collective-permute-done((bf16[96,4224]{1,0:T(8,128)(2,1)S(1)}, bf16[96,4224]{1,0:T(8,128)(2,1)S(1)}, u32[]{:S(2)}, u32[]{:S(2)}) %collective-permute-start.3) | collective-permute-done | bytes 811040 | tf_op jit(solution)/shard_map/exchange_rows/ppermute | solution.py:221
  45.5 0.3 collective-permute-start.5
  45.9 1.3 %collective-permute-start.6 = (bf16[96,2176]{1,0:T(8,128)(2,1)S(1)}, bf16[96,2176]{1,0:T(8,128)(2,1)S(1)}, u32[]{:S(2)}, u32[]{:S(2)}) collective-permute-start(bf16[96,2176]{1,0:T(8,128)(2,1)S(1)} %slice_multiply_fusion), channel_id=1, source_target_pairs={{0,2},{1,3},{2,0},{3,1},{4,6},{5,7},{6,4},{7,5},{8,10},{9,11},{10,... | collective-permute-start | bytes 1253384 | tf_op jit(solution)/shard_map/exchange_rows/ppermute | solution.py:221
  47.1 1.7 %collective-permute-start.9 = (bf16[96,4224]{1,0:T(8,128)(2,1)S(1)}, bf16[96,4224]{1,0:T(8,128)(2,1)S(1)}, u32[]{:S(2)}, u32[]{:S(2)}) collective-permute-start(bf16[96,4224]{1,0:T(8,128)(2,1)S(1)} %collective-permute-done.4), channel_id=1, source_target_pairs={{0,1},{1,0},{2,3},{3,2},{4,5},{5,4},{6,7},{7,6},{8,9},{9,8},{10,11... | collective-permute-start | bytes 2433032 | tf_op jit(solution)/shard_map/exchange_rows/ppermute | solution.py:221
  49.0 0.1 constant_dynamic-update-slice_fusion.5
  49.1 5.9 %collective-permute-done.5 = bf16[96,2048]{1,0:T(8,128)(2,1)S(1)} collective-permute-done((bf16[96,2048]{1,0:T(8,128)(2,1)S(1)}, bf16[96,2048]{1,0:T(8,128)(2,1)S(1)}, u32[]{:S(2)}, u32[]{:S(2)}) %collective-permute-start.5) | collective-permute-done | bytes 393248 | tf_op jit(solution)/shard_map/exchange_rows/ppermute | solution.py:221
  55.0 0.6 collective-permute-done.6
  55.7 2.4 %collective-permute-start.10 = (bf16[96,4224]{1,0:T(8,128)(2,1)S(1)}, bf16[96,4224]{1,0:T(8,128)(2,1)}, u32[]{:S(2)}, u32[]{:S(2)}) collective-permute-start(bf16[96,4224]{1,0:T(8,128)(2,1)S(1)} %pad_maximum_fusion.1), channel_id=1, source_target_pairs={{0,1},{1,0},{2,3},{3,2},{4,5},{5,4},{6,7},{7,6},{8,9},{9,8},{10,11... | collective-permute-start | bytes 2433032 | tf_op jit(solution)/shard_map/exchange_rows/ppermute | solution.py:221
  58.4 0.1 constant_dynamic-update-slice_fusion.1
  58.5 1.7 %collective-permute-done.10 = bf16[96,4224]{1,0:T(8,128)(2,1)} collective-permute-done((bf16[96,4224]{1,0:T(8,128)(2,1)S(1)}, bf16[96,4224]{1,0:T(8,128)(2,1)}, u32[]{:S(2)}, u32[]{:S(2)}) %collective-permute-start.10) | collective-permute-done | bytes 811040 | tf_op jit(solution)/shard_map/exchange_rows/ppermute | solution.py:221
  60.2 1.2 %constant_dynamic-update-slice_fusion.refs_0_ = bf16[768,4224]{1,0:T(8,128)(2,1)S(1)} fusion(bf16[768,4224]{1,0:T(8,128)(2,1)S(1)} %constant_dynamic-update-slice_fusion.1, bf16[96,4224]{1,0:T(8,128)(2,1)} %collective-permute-done.10), kind=kLoop, calls=%fused_computation.5 | loop fusion | bytes 1622016 | tf_op jit(solution)/shard_map/concatenate | solution.py:255
  61.4 38.2 %fused_iterations.1 = (f32[4,384,4096]{2,1,0:T(8,128)}, f32[4,384,4096]{2,1,0:T(8,128)}, f32[4,384,4096]{2,1,0:T(8,128)S(1)}) custom-call(bf16[768,4224]{1,0:T(8,128)(2,1)S(1)} %constant_dynamic-update-slice_fusion.refs_0_, bf16[4,384,4096]{2,1,0:T(8,128)(2,1)S(1)} %get-tuple-element.8.refs_1_, ...), custom_call_target="tpu_custom_call", output_to_operand_aliasing={{2}: (2, {})} | custom-call | flops 19327352832 | bytes 50331648 | tf_op jit(solution)/shard_map/fused_iterations/pallas_call | solution.py:166
  (20 shorter events, 0.8 us)
Async XLA Ops:
  2.4 12.8 %collective-permute-start.1 = (bf16[24,4224]{1,0:T(8,128)(2,1)S(1)}, bf16[24,4224]{1,0:T(8,128)(2,1)S(1)}, u32[]{:S(2)}, u32[]{:S(2)}) collective-permute-start(bf16[24,4224]{1,0:T(8,128)(2,1)S(1)} %get-tuple-element.12), channel_id=1, source_target_pairs={{0,16},{8,24},{16,0},{24,8},{1,17},{9,25},{17,1},{25,9},{2,18},{10... | collective-permute-start | bytes 608264 | tf_op jit(solution)/shard_map/exchange_rows/ppermute | solution.py:228
  2.5 20.9 %collective-permute-start = (bf16[24,4224]{1,0:T(8,128)(2,1)S(1)}, bf16[24,4224]{1,0:T(8,128)(2,1)S(1)}, u32[]{:S(2)}, u32[]{:S(2)}) collective-permute-start(bf16[24,4224]{1,0:T(8,128)(2,1)S(1)} %get-tuple-element.12), channel_id=1, source_target_pairs={{0,8},{8,16},{16,24},{24,0},{1,9},{9,17},{17,25},{25,1},{2,10},{10... | collective-permute-start | bytes 608264 | tf_op jit(solution)/shard_map/exchange_rows/ppermute | solution.py:228
  3.8 19.5 %collective-permute-start.2 = (bf16[24,4224]{1,0:T(8,128)(2,1)S(1)}, bf16[24,4224]{1,0:T(8,128)(2,1)S(1)}, u32[]{:S(2)}, u32[]{:S(2)}) collective-permute-start(bf16[24,4224]{1,0:T(8,128)(2,1)S(1)} %get-tuple-element.12), channel_id=1, source_target_pairs={{0,24},{8,0},{16,8},{24,16},{1,25},{9,1},{17,9},{25,17},{2,26},{10... | collective-permute-start | bytes 608264 | tf_op jit(solution)/shard_map/exchange_rows/ppermute | solution.py:228
  24.3 33.8 %collective-permute-start.7 = (bf16[96,4224]{1,0:T(8,128)(2,1)S(1)}, bf16[96,4224]{1,0:T(8,128)(2,1)S(1)}, u32[]{:S(2)}, u32[]{:S(2)}) collective-permute-start(bf16[96,4224]{1,0:T(8,128)(2,1)S(1)} %pad_maximum_fusion.refs_0_), channel_id=1, source_target_pairs={{0,1},{1,0},{2,3},{3,2},{4,5},{5,4},{6,7},{7,6},{8,9},{9,8},{10,11... | collective-permute-start | bytes 2433032 | tf_op jit(solution)/shard_map/exchange_rows/ppermute | solution.py:221
  24.9 20.9 %collective-permute-start.4 = (bf16[96,4224]{1,0:T(8,128)(2,1)S(1)}, bf16[96,4224]{1,0:T(8,128)(2,1)S(1)}, u32[]{:S(2)}, u32[]{:S(2)}) collective-permute-start(bf16[96,4224]{1,0:T(8,128)(2,1)S(1)} %pad_maximum_fusion.refs_0_), channel_id=1, source_target_pairs={{0,4},{1,5},{2,6},{3,7},{4,0},{5,1},{6,2},{7,3},{8,12},{9,13},{10,... | collective-permute-start | bytes 2433032 | tf_op jit(solution)/shard_map/exchange_rows/ppermute | solution.py:221
  26.1 19.3 %collective-permute-start.3 = (bf16[96,4224]{1,0:T(8,128)(2,1)S(1)}, bf16[96,4224]{1,0:T(8,128)(2,1)S(1)}, u32[]{:S(2)}, u32[]{:S(2)}) collective-permute-start(bf16[96,4224]{1,0:T(8,128)(2,1)S(1)} %pad_maximum_fusion.refs_0_), channel_id=1, source_target_pairs={{0,2},{1,3},{2,0},{3,1},{4,6},{5,7},{6,4},{7,5},{8,10},{9,11},{10,... | collective-permute-start | bytes 2433032 | tf_op jit(solution)/shard_map/exchange_rows/ppermute | solution.py:221
  45.5 9.5 %collective-permute-start.5 = (bf16[96,2048]{1,0:T(8,128)(2,1)S(1)}, bf16[96,2048]{1,0:T(8,128)(2,1)S(1)}, u32[]{:S(2)}, u32[]{:S(2)}) collective-permute-start(bf16[96,2048]{1,0:T(8,128)(2,1)S(1)} %slice_multiply_fusion.1), channel_id=1, source_target_pairs={{0,4},{1,5},{2,6},{3,7},{4,0},{5,1},{6,2},{7,3},{8,12},{9,13},{10,... | collective-permute-start | bytes 1179656 | tf_op jit(solution)/shard_map/exchange_rows/ppermute | solution.py:221
  45.9 9.7 %collective-permute-start.6 = (bf16[96,2176]{1,0:T(8,128)(2,1)S(1)}, bf16[96,2176]{1,0:T(8,128)(2,1)S(1)}, u32[]{:S(2)}, u32[]{:S(2)}) collective-permute-start(bf16[96,2176]{1,0:T(8,128)(2,1)S(1)} %slice_multiply_fusion), channel_id=1, source_target_pairs={{0,2},{1,3},{2,0},{3,1},{4,6},{5,7},{6,4},{7,5},{8,10},{9,11},{10,... | collective-permute-start | bytes 1253384 | tf_op jit(solution)/shard_map/exchange_rows/ppermute | solution.py:221
  47.1 11.2 %collective-permute-start.9 = (bf16[96,4224]{1,0:T(8,128)(2,1)S(1)}, bf16[96,4224]{1,0:T(8,128)(2,1)S(1)}, u32[]{:S(2)}, u32[]{:S(2)}) collective-permute-start(bf16[96,4224]{1,0:T(8,128)(2,1)S(1)} %collective-permute-done.4), channel_id=1, source_target_pairs={{0,1},{1,0},{2,3},{3,2},{4,5},{5,4},{6,7},{7,6},{8,9},{9,8},{10,11... | collective-permute-start | bytes 2433032 | tf_op jit(solution)/shard_map/exchange_rows/ppermute | solution.py:221
  48.9 9.4 %collective-permute-start.8 = (bf16[96,4224]{1,0:T(8,128)(2,1)S(1)}, bf16[96,4224]{1,0:T(8,128)(2,1)S(1)}, u32[]{:S(2)}, u32[]{:S(2)}) collective-permute-start(bf16[96,4224]{1,0:T(8,128)(2,1)S(1)} %collective-permute-done.3), channel_id=1, source_target_pairs={{0,1},{1,0},{2,3},{3,2},{4,5},{5,4},{6,7},{7,6},{8,9},{9,8},{10,11... | collective-permute-start | bytes 2433032 | tf_op jit(solution)/shard_map/exchange_rows/ppermute | solution.py:221
  55.7 4.5 %collective-permute-start.10 = (bf16[96,4224]{1,0:T(8,128)(2,1)S(1)}, bf16[96,4224]{1,0:T(8,128)(2,1)}, u32[]{:S(2)}, u32[]{:S(2)}) collective-permute-start(bf16[96,4224]{1,0:T(8,128)(2,1)S(1)} %pad_maximum_fusion.1), channel_id=1, source_target_pairs={{0,1},{1,0},{2,3},{3,2},{4,5},{5,4},{6,7},{7,6},{8,9},{9,8},{10,11... | collective-permute-start | bytes 2433032 | tf_op jit(solution)/shard_map/exchange_rows/ppermute | solution.py:221

commit v5 on v4

v5 whole, which is shorter than its diff:
```python
import functools

import jax
import jax.numpy as jnp
from jax import lax
from jax.experimental import pallas as pl
from jax.experimental.pallas import tpu as pltpu
from jax.sharding import PartitionSpec as P

EXPERTS = 32
BLOCK = 64
ROWS_BLOCK = 24
MOST = 7
ITERS = 2
LANES = 128
MIB = 1024 * 1024
SPARE = 10

step_rate = 0.2

F32 = jnp.float32
BF16 = jnp.bfloat16


def dot_nn(a, b):
    return jnp.dot(a, b, preferred_element_type=F32)


def dot_nt(a, b):
    return lax.dot_general(a, b, (((1,), (1,)), ((), ())), preferred_element_type=F32)


def cuts_of(width, chunk):
    return [pl.ds(start, chunk) for start in range(0, width, chunk)]


def load_kernel(n_marks, *refs):
    source, held, token, sem = refs[n_marks:]
    copy = pltpu.make_async_copy(source, held, sem)
    copy.start()
    token[...] = jnp.ones_like(token)
    copy.wait()


def load(marks, array, scoped):
    anywhere = pl.BlockSpec(memory_space=pl.ANY)
    size = array.size * array.dtype.itemsize
    return pl.pallas_call(
        functools.partial(load_kernel, len(marks)),
        in_specs=[anywhere] * (len(marks) + 1),
        out_specs=[anywhere, pl.BlockSpec(memory_space=pltpu.VMEM)],
        out_shape=[pltpu.VMEM(array.shape, array.dtype), jax.ShapeDtypeStruct(marks[0].shape, BF16)],
        scratch_shapes=[pltpu.SemaphoreType.DMA],
        compiler_params=pltpu.CompilerParams(vmem_limit_bytes=scoped),
        cost_estimate=pl.CostEstimate(flops=0, bytes_accessed=size, transcendentals=0),
    )(*marks, array)


def fused_kernel(chunk, topk, halves, block_rows, *refs):
    gathered = refs[:halves]
    base_hbm, _, keep_ref, weight_hbm, dual_hbm, dual, *refs = refs[halves:]
    base_held, rows, across, held, mask, counts, base_sem, weight_sems, dual_sems = refs
    expert = pl.program_id(0)
    tokens = gathered[0].shape[0]
    local, slots, width = rows.shape
    tall = held.shape[0]
    part_width = width // halves
    cuts = cuts_of(width, chunk)
    parts = [slice(start, start + BLOCK) for start in range(0, tall, BLOCK)]
    per = slots // (tokens // block_rows)
    lanes = local * per

    def base_copy(at):
        return pltpu.make_async_copy(base_hbm.at[at], base_held, base_sem)

    def weight_copy(at, i):
        return pltpu.make_async_copy(held.at[:, cuts[i]], weight_hbm.at[at, :, cuts[i]], weight_sems.at[i])

    def dual_copy(at, i):
        return pltpu.make_async_copy(dual.at[at, :, cuts[i]], dual_hbm.at[at, :, cuts[i]], dual_sems.at[at, i])

    @pl.when(expert == 0)
    def _():
        base_copy(0).start()
        lane = lax.broadcasted_iota(jnp.int32, (block_rows, lanes), 1)
        which = sum(jnp.where(lane >= per * own, 1, 0) for own in range(1, local))
        label = (lax.axis_index("exp") * local + which).astype(F32)
        slot = (lane - which * per).astype(F32)
        later = lax.broadcasted_iota(jnp.int32, (block_rows, block_rows), 0)
        earlier = lax.broadcasted_iota(jnp.int32, (block_rows, block_rows), 1)
        ahead = jnp.where(earlier < later, 1.0, 0.0).astype(BF16)

        def pack(p, total):
            block = pl.ds(pl.multiple_of(p * block_rows, 16), block_rows)
            named = gathered[0][block, pl.ds(part_width, LANES)].astype(F32)
            hit = jnp.zeros((block_rows, lanes), F32)
            for k in range(topk):
                hit = jnp.where(named[:, k : k + 1] == label, 1.0, hit)
            taken = jnp.where(dot_nn(ahead, hit.astype(BF16)) == slot, hit, 0.0)
            spare = jnp.zeros((-block_rows % LANES, lanes), F32)
            taken = jnp.concatenate([taken, spare], axis=0).T[:, :block_rows].astype(BF16)
            for cut in cuts:
                half, start = divmod(cut.start, part_width)
                picked = dot_nn(taken, gathered[half][block, pl.ds(start, chunk)]).astype(BF16)
                for own in range(local):
                    rows[own, pl.ds(pl.multiple_of(p * per, 16), per), cut] = picked[own * per : (own + 1) * per, :]
            return total + jnp.sum(hit, axis=0, keepdims=True)

        counts[...] = lax.fori_loop(0, tokens // block_rows, pack, jnp.zeros((1, lanes), F32))
        count = keep_ref.shape[2]
        at = lax.broadcasted_iota(jnp.int32, (count, width), 0) * BLOCK
        column = lax.broadcasted_iota(jnp.int32, (count, width), 1)
        wide = jnp.where((column >= at) & (column < at + BLOCK), 1.0, 0.0).astype(BF16)
        for own in range(local):
            mask[own] = dot_nn(keep_ref[own].astype(F32).astype(BF16), wide)

    base_copy(expert).wait()
    mine = lax.broadcasted_iota(jnp.int32, (1, lanes), 1) == expert * per
    rate = step_rate / jnp.sum(jnp.where(mine, counts[...], 0.0), axis=1, keepdims=True)

    resid = jnp.zeros((tall, slots), F32)
    for cut in cuts:
        across[cut, :] = rows[expert, :, cut].T
        deltas = [
            base_held[part, cut] * (mask[expert, i : i + 1, cut] - 1.0).astype(BF16) for i, part in enumerate(parts)
        ]
        resid = resid + dot_nn(jnp.concatenate(deltas, axis=0), across[cut, :])
    resid = resid.astype(BF16)

    @pl.when(expert > 0)
    def _():
        for i in range(len(cuts)):
            weight_copy(expert - 1, i).wait()

    after = jnp.zeros((tall, slots), F32)
    for cut in cuts:
        grad = dot_nn(resid, rows[expert, :, cut])
        deltas = []
        for i, part in enumerate(parts):
            base = base_held[part, cut].astype(F32)
            weight = mask[expert, i : i + 1, cut] * base - step_rate * dual[expert, part, cut] - rate * grad[part, :]
            held[part, cut] = weight
            deltas.append((weight - base).astype(BF16))
        after = after + dot_nn(jnp.concatenate(deltas, axis=0), across[cut, :])
    resid = after.astype(BF16)

    @pl.when(expert < local - 1)
    def _():
        base_copy(expert + 1).start()

    for n, cut in enumerate(cuts):
        grad = dot_nn(resid, rows[expert, :, cut])
        for i, part in enumerate(parts):
            keep = mask[expert, i : i + 1, cut]
            weight = held[part, cut]
            both = weight + dual[expert, part, cut]
            weight = (1.0 - step_rate) * weight - (step_rate - 2.0 * step_rate * keep) * both - rate * grad[part, :]
            held[part, cut] = weight
            dual[expert, part, cut] = (1.0 - keep) * (both + weight)
        weight_copy(expert, n).start()
        dual_copy(expert, n).start()

    @pl.when(expert == local - 1)
    def _():
        for i in range(len(cuts)):
            weight_copy(expert, i).wait()
        for at in range(local):
            for i in range(len(cuts)):
                dual_copy(at, i).wait()


def fused(gathered, base_weight, keep_mask, dual_start, topk, per, scoped):
    local, tall, width = base_weight.shape
    chunk = 512
    block_rows = gathered[0].shape[0] // lax.axis_size("exp")
    slots = lax.axis_size("exp") * per
    whole = pl.BlockSpec(memory_space=pltpu.VMEM)
    anywhere = pl.BlockSpec(memory_space=pl.ANY)
    out = jax.ShapeDtypeStruct(dual_start.shape, F32)
    macs = local * slots * width * (4 * tall + block_rows)
    held = [pltpu.with_memory_space_constraint(x, pltpu.VMEM) for x in (*gathered, dual_start)]
    operands = [*held[:-1], base_weight, held[-1], keep_mask]
    outs = pl.pallas_call(
        functools.partial(fused_kernel, chunk, topk, len(gathered), block_rows),
        grid=(local,),
        in_specs=[whole] * len(gathered) + [anywhere, whole, whole],
        out_specs=[anywhere, anywhere, whole],
        out_shape=[out, out, pltpu.VMEM(dual_start.shape, F32)],
        input_output_aliases={len(operands) - 2: 2},
        scratch_shapes=[
            pltpu.VMEM((tall, width), BF16),
            pltpu.VMEM((local, slots, width), BF16),
            pltpu.VMEM((width, slots), BF16),
            pltpu.VMEM((tall, width), F32),
            pltpu.VMEM((local, keep_mask.shape[1], width), F32),
            pltpu.VMEM((1, local * per), F32),
            pltpu.SemaphoreType.DMA,
            pltpu.SemaphoreType.DMA((width // chunk,)),
            pltpu.SemaphoreType.DMA((local, width // chunk)),
        ],
        compiler_params=pltpu.CompilerParams(vmem_limit_bytes=scoped, dimension_semantics=("arbitrary",)),
        cost_estimate=pl.CostEstimate(flops=2 * macs, bytes_accessed=8 * base_weight.size, transcendentals=0),
    )(*operands)
    return outs[0], outs[1]


def plain(gathered, base_weight, keep_mask, dual, topk):
    local, _, width = base_weight.shape
    part = width // len(gathered)
    routes = gathered[0][:, part : part + topk].astype(jnp.int32)
    rows = jnp.concatenate([piece[:, :part] for piece in gathered], axis=1)
    tokens = rows.shape[0]
    slots = min(-(-tokens // ROWS_BLOCK) * MOST, tokens)
    labels = lax.axis_index("exp") * local + jnp.arange(local, dtype=jnp.int32)
    hits = jnp.any(routes[:, :, None] == labels, axis=1)
    rank = jnp.cumsum(hits.astype(jnp.int32), axis=0) - 1
    taken = hits[:, :, None] & (rank[:, :, None] == jnp.arange(slots, dtype=jnp.int32))
    picked = jnp.einsum("rls,rd->lsd", taken.astype(BF16), rows, preferred_element_type=F32).astype(BF16)
    rate = (step_rate / jnp.sum(hits.astype(F32), axis=0))[:, None, None]
    mask = jnp.repeat(jnp.repeat(keep_mask.astype(F32), BLOCK, 1), BLOCK, 2)
    base = base_weight.astype(F32)
    weight = zed = mask * base
    for _ in range(ITERS):
        delta = (weight - base).astype(BF16)
        resid = jnp.einsum("lnd,lcd->lcn", picked, delta, preferred_element_type=F32).astype(BF16)
        grad = jnp.einsum("lcn,lnd->lcd", resid, picked, preferred_element_type=F32)
        weight = weight - rate * grad - step_rate * (weight - zed + dual)
        zed = mask * (weight + dual)
        dual = dual + weight - zed
    return weight, dual


def after(ones, array):
    return array * ones[: array.shape[0], : array.shape[1]]


def swap(piece, bit):
    n = lax.axis_size("exp")
    return lax.ppermute(piece, "exp", [(i, i ^ (1 << bit)) for i in range(n)])


def column_rows(own):
    n = lax.axis_size("tok")
    column = [own]
    for shift in range(1, n):
        column.append(lax.ppermute(own, "tok", [(i, (i + shift) % n) for i in range(n)]))
    return jnp.concatenate(column, axis=0)


def on_device(x_rows, routes, base_weight, keep_mask, dual_start):
    local, hidden, width = base_weight.shape
    topk = routes.shape[1]
    n_exp = lax.axis_size("exp")
    top = n_exp.bit_length() - 1
    assert 1 << top == n_exp
    halves = 2
    part = width // halves
    named = jnp.pad(routes.astype(BF16), ((0, 0), (0, LANES - topk)))
    sent = [x_rows[:, h * part : (h + 1) * part] for h in range(halves)]
    sent[0] = jnp.concatenate([sent[0], named], axis=1)
    with jax.named_scope("exchange_rows"):
        mine = [column_rows(own) for own in sent]
    if top != 3 or 2 * n_exp * mine[0].shape[0] * width > 16 * MIB:
        gathered = []
        for own in mine:
            pieces = {0: own}
            for bit in [*range(1, top), 0]:
                pieces.update({at ^ (1 << bit): swap(piece, bit) for at, piece in pieces.items()})
            gathered.append(jnp.concatenate([pieces[i] for i in range(n_exp)], axis=0))
        return plain(gathered, base_weight, keep_mask, dual_start, topk)
    per = -(-(mine[0].shape[0] // ROWS_BLOCK) * MOST // 16) * 16
    scoped = 6 * hidden * width + 2 * (local + 1) * n_exp * per * width + SPARE * MIB
    with jax.named_scope("load_duals"):
        dual_start, token = load(mine, dual_start, scoped)
    gathered = []
    with jax.named_scope("exchange_rows"):
        for own in mine:
            one, two = swap(own, 1), swap(own, 2)
            middle = own.shape[1] // 2 // LANES * LANES
            far = [swap(after(token, one[:, :middle]), 2), swap(after(token, two[:, middle:]), 1)]
            pieces = [own, one, two, jnp.concatenate(far, axis=1)]
            gathered.append(jnp.concatenate(pieces + [swap(piece, 0) for piece in pieces], axis=0))
    with jax.named_scope("fused_iterations"):
        return fused(gathered, base_weight, keep_mask, dual_start, topk, per, scoped)


def solution(mesh):
    return jax.shard_map(
        on_device,
        mesh=mesh,
        in_specs=(
            P(("tok", "exp"), None),
            P(("tok", "exp"), None),
            P("exp", "tok", None),
            P("exp", "tok", None),
            P("exp", "tok", None),
        ),
        out_specs=(P("exp", "tok", None), P("exp", "tok", None)),
        check_vma=False,
    )
```

time: 100 us -> 118 us (1.18)
  the two profiles are of different devices: /device:TPU:17 before, /device:TPU:0 now
where the time goes in v5:
time: 118 us
  Pallas kernels  57.7 us (49%)
  waiting for transfers between devices  30.5 us (26%)
  starting transfers between devices  22.3 us (19%)
  local copies, waits for them, and re-layouts  5.61 us (5%)
    pallas_call x1, Pallas kernels, fused(): pl.pallas_call(functools.partial(fused_kernel, chunk, topk, len(gathered)...  49.4 us
    ppermute x16, waiting for transfers between devices, swap(): return lax.ppermute(piece, 'exp', [(i, i ^ 1 << bit) for i in range(n)])  25.6 us
    ppermute x6, starting transfers between devices, column_rows(): lax.ppermute(own, 'tok', [(i, (i + shift) % n) for i in range(n)])  11.9 us
    ppermute x16, starting transfers between devices, swap(): return lax.ppermute(piece, 'exp', [(i, i ^ 1 << bit) for i in range(n)])  10.4 us
    pallas_call x1, Pallas kernels, load(): pl.pallas_call(functools.partial(load_kernel, len(marks)), in_specs=[anyw...  8.32 us
    unnamed x26, local copies, waits for them, and re-layouts  5.45 us
    ppermute x6, waiting for transfers between devices, column_rows(): lax.ppermute(own, 'tok', [(i, (i + shift) % n) for i in range(n)])  4.93 us
  transfers between devices with their start and end apart: 22, of which 8 were waited for; matrix products, arithmetic and copies ran while one was open for 4% of the time, Pallas kernels for 7%

profile of v5, /device:TPU:0, one launch (start us, length us, event | category | flops | bytes accessed | tf_op | source)
XLA Modules:
  0.0 118.0 jit_solution(4111682672152114738)
XLA Ops:
  0.6 1.6 %constant_dynamic-update-slice_fusion.21 = (bf16[768,2048]{1,0:T(8,128)(2,1)}, bf16[24,2048]{1,0:T(8,128)(2,1)S(1)}, bf16[24,2048]{1,0:T(8,128)(2,1)S(1)}) fusion(bf16[24,4096]{1,0:T(8,128)(2,1)} %param.5), kind=kLoop, calls=%fused_computation.30 | loop fusion | bytes 491520
  2.2 5.0 %collective-permute-start.7 = (bf16[24,2048]{1,0:T(8,128)(2,1)S(1)}, bf16[24,2048]{1,0:T(8,128)(2,1)S(1)}, u32[]{:S(2)}, u32[]{:S(2)}) collective-permute-start(bf16[24,2048]{1,0:T(8,128)(2,1)S(1)} %get-tuple-element.14), channel_id=1, source_target_pairs={{0,24},{8,0},{16,8},{24,16},{1,25},{9,1},{17,9},{25,17},{2,26},{10... | collective-permute-start | bytes 294920 | tf_op jit(solution)/shard_map/exchange_rows/ppermute | solution.py:246
  7.3 1.0 collective-permute-start.5
  8.3 0.7 convert_element_type.5
  9.1 2.0 %collective-permute-start.1 = (bf16[24,2176]{1,0:T(8,128)(2,1)S(1)}, bf16[24,2176]{1,0:T(8,128)(2,1)S(1)}, u32[]{:S(2)}, u32[]{:S(2)}) collective-permute-start(bf16[24,2176]{1,0:T(8,128)(2,1)S(1)} %get-tuple-element.16), channel_id=1, source_target_pairs={{0,16},{8,24},{16,0},{24,8},{1,17},{9,25},{17,1},{25,9},{2,18},{10... | collective-permute-start | bytes 313352 | tf_op jit(solution)/shard_map/exchange_rows/ppermute | solution.py:246
  11.1 1.5 %collective-permute-start = (bf16[24,2176]{1,0:T(8,128)(2,1)S(1)}, bf16[24,2176]{1,0:T(8,128)(2,1)S(1)}, u32[]{:S(2)}, u32[]{:S(2)}) collective-permute-start(bf16[24,2176]{1,0:T(8,128)(2,1)S(1)} %get-tuple-element.16), channel_id=1, source_target_pairs={{0,8},{8,16},{16,24},{24,0},{1,9},{9,17},{17,25},{25,1},{2,10},{10... | collective-permute-start | bytes 313352 | tf_op jit(solution)/shard_map/exchange_rows/ppermute | solution.py:246
  12.6 1.3 %copy.11.refs_4_ = s32[4,6,64]{2,1,0:T(8,128)} copy(s32[4,6,64]{2,0,1:T(4,128)} %param.8) | data formatting | bytes 12288 | tf_op args[3]
  13.9 2.4 %collective-permute-start.2 = (bf16[24,2176]{1,0:T(8,128)(2,1)S(1)}, bf16[24,2176]{1,0:T(8,128)(2,1)S(1)}, u32[]{:S(2)}, u32[]{:S(2)}) collective-permute-start(bf16[24,2176]{1,0:T(8,128)(2,1)S(1)} %get-tuple-element.16), channel_id=1, source_target_pairs={{0,24},{8,0},{16,8},{24,16},{1,25},{9,1},{17,9},{25,17},{2,26},{10... | collective-permute-start | bytes 313352 | tf_op jit(solution)/shard_map/exchange_rows/ppermute | solution.py:246
  16.2 4.9 %collective-permute-done.6 = bf16[24,2048]{1,0:T(8,128)(2,1)S(1)} collective-permute-done((bf16[24,2048]{1,0:T(8,128)(2,1)S(1)}, bf16[24,2048]{1,0:T(8,128)(2,1)S(1)}, u32[]{:S(2)}, u32[]{:S(2)}) %collective-permute-start.6) | collective-permute-done | bytes 98336 | tf_op jit(solution)/shard_map/exchange_rows/ppermute | solution.py:246
  21.3 1.6 %collective-permute-start.15 = (bf16[96,2048]{1,0:T(8,128)(2,1)S(1)}, bf16[96,2048]{1,0:T(8,128)(2,1)S(1)}, u32[]{:S(2)}, u32[]{:S(2)}) collective-permute-start(bf16[96,2048]{1,0:T(8,128)(2,1)S(1)} %pad_maximum_fusion.2.refs_1_), channel_id=1, source_target_pairs={{0,4},{1,5},{2,6},{3,7},{4,0},{5,1},{6,2},{7,3},{8,12},{9,13},{10,... | collective-permute-start | bytes 1179656 | tf_op jit(solution)/shard_map/exchange_rows/ppermute | solution.py:239
  22.8 0.6 constant_dynamic-update-slice_fusion.20
  23.5 0.6 constant_dynamic-update-slice_fusion.19
  24.1 0.6 constant_dynamic-update-slice_fusion.18
  24.8 1.5 %collective-permute-start.14 = (bf16[96,2048]{1,0:T(8,128)(2,1)S(1)}, bf16[96,2048]{1,0:T(8,128)(2,1)S(1)}, u32[]{:S(2)}, u32[]{:S(2)}) collective-permute-start(bf16[96,2048]{1,0:T(8,128)(2,1)S(1)} %pad_maximum_fusion.2.refs_1_), channel_id=1, source_target_pairs={{0,2},{1,3},{2,0},{3,1},{4,6},{5,7},{6,4},{7,5},{8,10},{9,11},{10,... | collective-permute-start | bytes 1179656 | tf_op jit(solution)/shard_map/exchange_rows/ppermute | solution.py:239
  27.1 8.3 %load_duals.1 = (f32[4,384,4096]{2,1,0:T(8,128)S(1)}, bf16[96,2176]{1,0:T(8,128)(2,1)S(1)}) custom-call(bf16[96,2176]{1,0:T(8,128)(2,1)} %copy-done.1, bf16[96,2048]{1,0:T(8,128)(2,1)S(1)} %pad_maximum_fusion.2.refs_1_, f32[4,384,4096]{2,1,0:T(8,128)} %refs_2_.2), custom_call_target="tpu_custom_call" | custom-call | bytes 25165824 | tf_op jit(solution)/shard_map/load_duals/pallas_call | solution.py:48
  36.2 11.2 %collective-permute-done.3 = bf16[96,2176]{1,0:T(8,128)(2,1)S(1)} collective-permute-done((bf16[96,2176]{1,0:T(8,128)(2,1)}, bf16[96,2176]{1,0:T(8,128)(2,1)S(1)}, u32[]{:S(2)}, u32[]{:S(2)}) %collective-permute-start.3) | collective-permute-done | bytes 417824 | tf_op jit(solution)/shard_map/exchange_rows/ppermute | solution.py:239
  48.1 1.6 %collective-permute-start.16 = (bf16[96,1024]{1,0:T(8,128)(2,1)S(1)}, bf16[96,1024]{1,0:T(8,128)(2,1)S(1)}, u32[]{:S(2)}, u32[]{:S(2)}) collective-permute-start(bf16[96,1024]{1,0:T(8,128)(2,1)S(1)} %get-tuple-element.11), channel_id=1, source_target_pairs={{0,4},{1,5},{2,6},{3,7},{4,0},{5,1},{6,2},{7,3},{8,12},{9,13},{10,... | collective-permute-start | bytes 589832 | tf_op jit(solution)/shard_map/exchange_rows/ppermute | solution.py:239
  49.8 4.2 %collective-permute-done.16 = bf16[96,1024]{1,0:T(8,128)(2,1)S(1)} collective-permute-done((bf16[96,1024]{1,0:T(8,128)(2,1)S(1)}, bf16[96,1024]{1,0:T(8,128)(2,1)S(1)}, u32[]{:S(2)}, u32[]{:S(2)}) %collective-permute-start.16) | collective-permute-done | bytes 196640 | tf_op jit(solution)/shard_map/exchange_rows/ppermute | solution.py:239
  54.0 1.6 %collective-permute-start.8 = (bf16[96,1024]{1,0:T(8,128)(2,1)S(1)}, bf16[96,1024]{1,0:T(8,128)(2,1)S(1)}, u32[]{:S(2)}, u32[]{:S(2)}) collective-permute-start(bf16[96,1024]{1,0:T(8,128)(2,1)S(1)} %get-tuple-element.12), channel_id=1, source_target_pairs={{0,4},{1,5},{2,6},{3,7},{4,0},{5,1},{6,2},{7,3},{8,12},{9,13},{10,... | collective-permute-start | bytes 589832 | tf_op jit(solution)/shard_map/exchange_rows/ppermute | solution.py:239
  55.7 4.0 %collective-permute-done.8 = bf16[96,1024]{1,0:T(8,128)(2,1)S(1)} collective-permute-done((bf16[96,1024]{1,0:T(8,128)(2,1)S(1)}, bf16[96,1024]{1,0:T(8,128)(2,1)S(1)}, u32[]{:S(2)}, u32[]{:S(2)}) %collective-permute-start.8) | collective-permute-done | bytes 196640 | tf_op jit(solution)/shard_map/exchange_rows/ppermute | solution.py:239
  59.7 1.5 %collective-permute-start.9 = (bf16[96,1152]{1,0:T(8,128)(2,1)S(1)}, bf16[96,1152]{1,0:T(8,128)(2,1)S(1)}, u32[]{:S(2)}, u32[]{:S(2)}) collective-permute-start(bf16[96,1152]{1,0:T(8,128)(2,1)S(1)} %slice_multiply_fusion), channel_id=1, source_target_pairs={{0,2},{1,3},{2,0},{3,1},{4,6},{5,7},{6,4},{7,5},{8,10},{9,11},{10,... | collective-permute-start | bytes 663560 | tf_op jit(solution)/shard_map/exchange_rows/ppermute | solution.py:239
  61.3 4.3 %collective-permute-done.9 = bf16[96,1152]{1,0:T(8,128)(2,1)S(1)} collective-permute-done((bf16[96,1152]{1,0:T(8,128)(2,1)S(1)}, bf16[96,1152]{1,0:T(8,128)(2,1)S(1)}, u32[]{:S(2)}, u32[]{:S(2)}) %collective-permute-start.9) | collective-permute-done | bytes 221216 | tf_op jit(solution)/shard_map/exchange_rows/ppermute | solution.py:239
  66.5 0.9 collective-permute-done.11
  68.5 49.4 %fused_iterations.1 = (f32[4,384,4096]{2,1,0:T(8,128)}, f32[4,384,4096]{2,1,0:T(8,128)}, f32[4,384,4096]{2,1,0:T(8,128)S(1)}) custom-call(bf16[768,2176]{1,0:T(8,128)(2,1)S(1)} %constant_dynamic-update-slice_fusion.refs_0_, bf16[768,2048]{1,0:T(8,128)(2,1)S(1)} %constant_dynamic-update-slice_fusion.11.refs_1_, ...), custom_call_target="tpu_custom_call", output_to_operand_aliasing={{2}: (3, {})} | custom-call | flops 13690208256 | bytes 50331648 | tf_op jit(solution)/shard_map/fused_iterations/pallas_call | solution.py:183
  (60 shorter events, 4.8 us)
Async XLA Ops:
  2.2 11.6 %collective-permute-start.7 = (bf16[24,2048]{1,0:T(8,128)(2,1)S(1)}, bf16[24,2048]{1,0:T(8,128)(2,1)S(1)}, u32[]{:S(2)}, u32[]{:S(2)}) collective-permute-start(bf16[24,2048]{1,0:T(8,128)(2,1)S(1)} %get-tuple-element.14), channel_id=1, source_target_pairs={{0,24},{8,0},{16,8},{24,16},{1,25},{9,1},{17,9},{25,17},{2,26},{10... | collective-permute-start | bytes 294920 | tf_op jit(solution)/shard_map/exchange_rows/ppermute | solution.py:246
  7.3 13.9 %collective-permute-start.6 = (bf16[24,2048]{1,0:T(8,128)(2,1)S(1)}, bf16[24,2048]{1,0:T(8,128)(2,1)S(1)}, u32[]{:S(2)}, u32[]{:S(2)}) collective-permute-start(bf16[24,2048]{1,0:T(8,128)(2,1)S(1)} %get-tuple-element.14), channel_id=1, source_target_pairs={{0,16},{8,24},{16,0},{24,8},{1,17},{9,25},{17,1},{25,9},{2,18},{10... | collective-permute-start | bytes 294920 | tf_op jit(solution)/shard_map/exchange_rows/ppermute | solution.py:246
  7.3 13.9 %collective-permute-start.5 = (bf16[24,2048]{1,0:T(8,128)(2,1)S(1)}, bf16[24,2048]{1,0:T(8,128)(2,1)S(1)}, u32[]{:S(2)}, u32[]{:S(2)}) collective-permute-start(bf16[24,2048]{1,0:T(8,128)(2,1)S(1)} %get-tuple-element.14), channel_id=1, source_target_pairs={{0,8},{8,16},{16,24},{24,0},{1,9},{9,17},{17,25},{25,1},{2,10},{10... | collective-permute-start | bytes 294920 | tf_op jit(solution)/shard_map/exchange_rows/ppermute | solution.py:246
  9.1 15.7 %collective-permute-start.1 = (bf16[24,2176]{1,0:T(8,128)(2,1)S(1)}, bf16[24,2176]{1,0:T(8,128)(2,1)S(1)}, u32[]{:S(2)}, u32[]{:S(2)}) collective-permute-start(bf16[24,2176]{1,0:T(8,128)(2,1)S(1)} %get-tuple-element.16), channel_id=1, source_target_pairs={{0,16},{8,24},{16,0},{24,8},{1,17},{9,25},{17,1},{25,9},{2,18},{10... | collective-permute-start | bytes 313352 | tf_op jit(solution)/shard_map/exchange_rows/ppermute | solution.py:246
  11.1 15.2 %collective-permute-start = (bf16[24,2176]{1,0:T(8,128)(2,1)S(1)}, bf16[24,2176]{1,0:T(8,128)(2,1)S(1)}, u32[]{:S(2)}, u32[]{:S(2)}) collective-permute-start(bf16[24,2176]{1,0:T(8,128)(2,1)S(1)} %get-tuple-element.16), channel_id=1, source_target_pairs={{0,8},{8,16},{16,24},{24,0},{1,9},{9,17},{17,25},{25,1},{2,10},{10... | collective-permute-start | bytes 313352 | tf_op jit(solution)/shard_map/exchange_rows/ppermute | solution.py:246
  13.9 12.4 %collective-permute-start.2 = (bf16[24,2176]{1,0:T(8,128)(2,1)S(1)}, bf16[24,2176]{1,0:T(8,128)(2,1)S(1)}, u32[]{:S(2)}, u32[]{:S(2)}) collective-permute-start(bf16[24,2176]{1,0:T(8,128)(2,1)S(1)} %get-tuple-element.16), channel_id=1, source_target_pairs={{0,24},{8,0},{16,8},{24,16},{1,25},{9,1},{17,9},{25,17},{2,26},{10... | collective-permute-start | bytes 313352 | tf_op jit(solution)/shard_map/exchange_rows/ppermute | solution.py:246
  21.2 40.0 %collective-permute-start.18 = (bf16[96,2048]{1,0:T(8,128)(2,1)S(1)}, bf16[96,2048]{1,0:T(8,128)(2,1)S(1)}, u32[]{:S(2)}, u32[]{:S(2)}) collective-permute-start(bf16[96,2048]{1,0:T(8,128)(2,1)S(1)} %pad_maximum_fusion.2.refs_1_), channel_id=1, source_target_pairs={{0,1},{1,0},{2,3},{3,2},{4,5},{5,4},{6,7},{7,6},{8,9},{9,8},{10,11... | collective-permute-start | bytes 1179656 | tf_op jit(solution)/shard_map/exchange_rows/ppermute | solution.py:239
  21.3 14.2 %collective-permute-start.15 = (bf16[96,2048]{1,0:T(8,128)(2,1)S(1)}, bf16[96,2048]{1,0:T(8,128)(2,1)S(1)}, u32[]{:S(2)}, u32[]{:S(2)}) collective-permute-start(bf16[96,2048]{1,0:T(8,128)(2,1)S(1)} %pad_maximum_fusion.2.refs_1_), channel_id=1, source_target_pairs={{0,4},{1,5},{2,6},{3,7},{4,0},{5,1},{6,2},{7,3},{8,12},{9,13},{10,... | collective-permute-start | bytes 1179656 | tf_op jit(solution)/shard_map/exchange_rows/ppermute | solution.py:239
  24.8 11.3 %collective-permute-start.14 = (bf16[96,2048]{1,0:T(8,128)(2,1)S(1)}, bf16[96,2048]{1,0:T(8,128)(2,1)S(1)}, u32[]{:S(2)}, u32[]{:S(2)}) collective-permute-start(bf16[96,2048]{1,0:T(8,128)(2,1)S(1)} %pad_maximum_fusion.2.refs_1_), channel_id=1, source_target_pairs={{0,2},{1,3},{2,0},{3,1},{4,6},{5,7},{6,4},{7,5},{8,10},{9,11},{10,... | collective-permute-start | bytes 1179656 | tf_op jit(solution)/shard_map/exchange_rows/ppermute | solution.py:239
  26.3 0.8 copy-start.1
  26.3 39.3 %collective-permute-start.10 = (bf16[96,2176]{1,0:T(8,128)(2,1)S(1)}, bf16[96,2176]{1,0:T(8,128)(2,1)S(1)}, u32[]{:S(2)}, u32[]{:S(2)}) collective-permute-start(bf16[96,2176]{1,0:T(8,128)(2,1)S(1)} %pad_maximum_fusion.refs_0_), channel_id=1, source_target_pairs={{0,1},{1,0},{2,3},{3,2},{4,5},{5,4},{6,7},{7,6},{8,9},{9,8},{10,11... | collective-permute-start | bytes 1253384 | tf_op jit(solution)/shard_map/exchange_rows/ppermute | solution.py:239
  26.4 21.7 %collective-permute-start.4 = (bf16[96,2176]{1,0:T(8,128)(2,1)S(1)}, bf16[96,2176]{1,0:T(8,128)(2,1)S(1)}, u32[]{:S(2)}, u32[]{:S(2)}) collective-permute-start(bf16[96,2176]{1,0:T(8,128)(2,1)S(1)} %pad_maximum_fusion.refs_0_), channel_id=1, source_target_pairs={{0,4},{1,5},{2,6},{3,7},{4,0},{5,1},{6,2},{7,3},{8,12},{9,13},{10,... | collective-permute-start | bytes 1253384 | tf_op jit(solution)/shard_map/exchange_rows/ppermute | solution.py:239
  27.1 9.0 %copy-start = (bf16[768,2048]{1,0:T(8,128)(2,1)S(1)}, bf16[768,2048]{1,0:T(8,128)(2,1)}, u32[]{:S(2)}) copy-start(bf16[768,2048]{1,0:T(8,128)(2,1)} %constant_dynamic-update-slice_fusion.18) | copy-start | bytes 9437188
  35.4 11.9 %collective-permute-start.3 = (bf16[96,2176]{1,0:T(8,128)(2,1)}, bf16[96,2176]{1,0:T(8,128)(2,1)S(1)}, u32[]{:S(2)}, u32[]{:S(2)}) collective-permute-start(bf16[96,2176]{1,0:T(8,128)(2,1)} %copy-done.1), channel_id=1, source_target_pairs={{0,2},{1,3},{2,0},{3,1},{4,6},{5,7},{6,4},{7,5},{8,10},{9,11},{10,... | collective-permute-start | bytes 1253384 | tf_op jit(solution)/shard_map/exchange_rows/ppermute | solution.py:239
  36.0 30.4 %collective-permute-start.20 = (bf16[96,2048]{1,0:T(8,128)(2,1)S(1)}, bf16[96,2048]{1,0:T(8,128)(2,1)S(1)}, u32[]{:S(2)}, u32[]{:S(2)}) collective-permute-start(bf16[96,2048]{1,0:T(8,128)(2,1)S(1)} %collective-permute-done.15), channel_id=1, source_target_pairs={{0,1},{1,0},{2,3},{3,2},{4,5},{5,4},{6,7},{7,6},{8,9},{9,8},{10,11... | collective-permute-start | bytes 1179656 | tf_op jit(solution)/shard_map/exchange_rows/ppermute | solution.py:239
  47.4 8.1 %collective-permute-start.17 = (bf16[96,1024]{1,0:T(8,128)(2,1)S(1)}, bf16[96,1024]{1,0:T(8,128)(2,1)S(1)}, u32[]{:S(2)}, u32[]{:S(2)}) collective-permute-start(bf16[96,1024]{1,0:T(8,128)(2,1)S(1)} %get-tuple-element.10), channel_id=1, source_target_pairs={{0,2},{1,3},{2,0},{3,1},{4,6},{5,7},{6,4},{7,5},{8,10},{9,11},{10,... | collective-permute-start | bytes 589832 | tf_op jit(solution)/shard_map/exchange_rows/ppermute | solution.py:239
  48.1 5.9 %collective-permute-start.16 = (bf16[96,1024]{1,0:T(8,128)(2,1)S(1)}, bf16[96,1024]{1,0:T(8,128)(2,1)S(1)}, u32[]{:S(2)}, u32[]{:S(2)}) collective-permute-start(bf16[96,1024]{1,0:T(8,128)(2,1)S(1)} %get-tuple-element.11), channel_id=1, source_target_pairs={{0,4},{1,5},{2,6},{3,7},{4,0},{5,1},{6,2},{7,3},{8,12},{9,13},{10,... | collective-permute-start | bytes 589832 | tf_op jit(solution)/shard_map/exchange_rows/ppermute | solution.py:239
  54.0 5.7 %collective-permute-start.8 = (bf16[96,1024]{1,0:T(8,128)(2,1)S(1)}, bf16[96,1024]{1,0:T(8,128)(2,1)S(1)}, u32[]{:S(2)}, u32[]{:S(2)}) collective-permute-start(bf16[96,1024]{1,0:T(8,128)(2,1)S(1)} %get-tuple-element.12), channel_id=1, source_target_pairs={{0,4},{1,5},{2,6},{3,7},{4,0},{5,1},{6,2},{7,3},{8,12},{9,13},{10,... | collective-permute-start | bytes 589832 | tf_op jit(solution)/shard_map/exchange_rows/ppermute | solution.py:239
  55.6 10.7 %collective-permute-start.19 = (bf16[96,2048]{1,0:T(8,128)(2,1)S(1)}, bf16[96,2048]{1,0:T(8,128)(2,1)S(1)}, u32[]{:S(2)}, u32[]{:S(2)}) collective-permute-start(bf16[96,2048]{1,0:T(8,128)(2,1)S(1)} %collective-permute-done.14), channel_id=1, source_target_pairs={{0,1},{1,0},{2,3},{3,2},{4,5},{5,4},{6,7},{7,6},{8,9},{9,8},{10,11... | collective-permute-start | bytes 1179656 | tf_op jit(solution)/shard_map/exchange_rows/ppermute | solution.py:239
  59.7 5.9 %collective-permute-start.9 = (bf16[96,1152]{1,0:T(8,128)(2,1)S(1)}, bf16[96,1152]{1,0:T(8,128)(2,1)S(1)}, u32[]{:S(2)}, u32[]{:S(2)}) collective-permute-start(bf16[96,1152]{1,0:T(8,128)(2,1)S(1)} %slice_multiply_fusion), channel_id=1, source_target_pairs={{0,2},{1,3},{2,0},{3,1},{4,6},{5,7},{6,4},{7,5},{8,10},{9,11},{10,... | collective-permute-start | bytes 663560 | tf_op jit(solution)/shard_map/exchange_rows/ppermute | solution.py:239
  61.2 6.2 %collective-permute-start.12 = (bf16[96,2176]{1,0:T(8,128)(2,1)S(1)}, bf16[96,2176]{1,0:T(8,128)(2,1)S(1)}, u32[]{:S(2)}, u32[]{:S(2)}) collective-permute-start(bf16[96,2176]{1,0:T(8,128)(2,1)S(1)} %collective-permute-done.4), channel_id=1, source_target_pairs={{0,1},{1,0},{2,3},{3,2},{4,5},{5,4},{6,7},{7,6},{8,9},{9,8},{10,11... | collective-permute-start | bytes 1253384 | tf_op jit(solution)/shard_map/exchange_rows/ppermute | solution.py:239
  65.6 1.8 %collective-permute-start.11 = (bf16[96,2176]{1,0:T(8,128)(2,1)S(1)}, bf16[96,2176]{1,0:T(8,128)(2,1)S(1)}, u32[]{:S(2)}, u32[]{:S(2)}) collective-permute-start(bf16[96,2176]{1,0:T(8,128)(2,1)S(1)} %collective-permute-done.3), channel_id=1, source_target_pairs={{0,1},{1,0},{2,3},{3,2},{4,5},{5,4},{6,7},{7,6},{8,9},{9,8},{10,11... | collective-permute-start | bytes 1253384 | tf_op jit(solution)/shard_map/exchange_rows/ppermute | solution.py:239
  65.7 2.2 %collective-permute-start.21 = (bf16[96,2048]{1,0:T(8,128)(2,1)S(1)}, bf16[96,2048]{1,0:T(8,128)(2,1)S(1)}, u32[]{:S(2)}, u32[]{:S(2)}) collective-permute-start(bf16[96,2048]{1,0:T(8,128)(2,1)S(1)} %pad_maximum_fusion.3), channel_id=1, source_target_pairs={{0,1},{1,0},{2,3},{3,2},{4,5},{5,4},{6,7},{7,6},{8,9},{9,8},{10,11... | collective-permute-start | bytes 1179656 | tf_op jit(solution)/shard_map/exchange_rows/ppermute | solution.py:239
  66.3 2.2 %collective-permute-start.13 = (bf16[96,2176]{1,0:T(8,128)(2,1)S(1)}, bf16[96,2176]{1,0:T(8,128)(2,1)S(1)}, u32[]{:S(2)}, u32[]{:S(2)}) collective-permute-start(bf16[96,2176]{1,0:T(8,128)(2,1)S(1)} %pad_maximum_fusion.1), channel_id=1, source_target_pairs={{0,1},{1,0},{2,3},{3,2},{4,5},{5,4},{6,7},{7,6},{8,9},{9,8},{10,11... | collective-permute-start | bytes 1253384 | tf_op jit(solution)/shard_map/exchange_rows/ppermute | solution.py:239

commit v6 on v4

--- a/solution.py
+++ b/solution.py
@@ -64,7 +64,7 @@
 def fused_kernel(chunk, topk, halves, *refs):
     gathered = refs[:halves]
     base_ref, _, keep_ref, weight_hbm, dual_hbm, dual, *refs = refs[halves:]
-    rows, across, held, rank, hits, mask, weight_sems, dual_sems = refs
+    rows, held, rank, hits, mask, weight_sems, dual_sems = refs
     expert = pl.program_id(0)
     tokens = gathered[0].shape[0]
     slots, width = rows.shape
@@ -104,13 +104,11 @@
     resid = jnp.zeros((tall, slots), F32)
     for cut in cuts:
         half, start = divmod(cut.start, part_width)
-        picked = dot_nn(taken, gathered[half][:, pl.ds(start, chunk)])
-        rows[:, cut] = picked.astype(BF16)
-        across[cut, :] = picked.T.astype(BF16)
+        rows[:, cut] = dot_nn(taken, gathered[half][:, pl.ds(start, chunk)]).astype(BF16)
         deltas = [
             base_ref[expert, part, cut] * (mask[expert, i : i + 1, cut] - 1.0).astype(BF16) for i, part in enumerate(parts)
         ]
-        resid = resid + dot_nn(jnp.concatenate(deltas, axis=0), across[cut, :])
+        resid = resid + dot_nt(jnp.concatenate(deltas, axis=0), rows[:, cut])
     resid = resid.astype(BF16)
 
     @pl.when(expert > 0)
@@ -127,7 +125,7 @@
             weight = mask[expert, i : i + 1, cut] * base - step_rate * dual[expert, part, cut] - rate * grad[part, :]
             held[part, cut] = weight
             deltas.append((weight - base).astype(BF16))
-        after = after + dot_nn(jnp.concatenate(deltas, axis=0), across[cut, :])
+        after = after + dot_nt(jnp.concatenate(deltas, axis=0), rows[:, cut])
     resid = after.astype(BF16)
 
     for n, cut in enumerate(cuts):
@@ -161,7 +159,7 @@
     anywhere = pl.BlockSpec(memory_space=pl.ANY)
     out = jax.ShapeDtypeStruct(dual_start.shape, F32)
     macs = local * slots * width * (4 * tall + tokens)
-    scoped = 4 * tall * width + 4 * slots * (width + tokens) + SPARE * MIB
+    scoped = 4 * tall * width + 2 * slots * (width + 2 * tokens) + SPARE * MIB
     held = [pltpu.with_memory_space_constraint(x, pltpu.VMEM) for x in (*gathered, base_weight, dual_start)]
     outs = pl.pallas_call(
         functools.partial(fused_kernel, chunk, topk, len(gathered)),
@@ -172,7 +170,6 @@
         input_output_aliases={len(held) - 1: 2},
         scratch_shapes=[
             pltpu.VMEM((slots, width), BF16),
-            pltpu.VMEM((width, slots), BF16),
             pltpu.VMEM((tall, width), F32),
             pltpu.VMEM((local, tokens), F32),
             pltpu.VMEM((local, tokens), F32),
@@ -235,24 +232,32 @@
     n_exp = lax.axis_size("exp")
     top = n_exp.bit_length() - 1
     assert 1 << top == n_exp
+    halves = 2
+    part = width // halves
     named = jnp.pad(routes.astype(BF16), ((0, 0), (0, LANES - topk)))
+    sent = [x_rows[:, h * part : (h + 1) * part] for h in range(halves)]
+    sent[0] = jnp.concatenate([sent[0], named], axis=1)
     with jax.named_scope("exchange_rows"):
-        mine = column_rows(jnp.concatenate([x_rows, named], axis=1))
-    if top != 3 or 2 * n_exp * mine.shape[0] * width > 16 * MIB:
-        pieces = {0: mine}
-        for bit in [*range(1, top), 0]:
-            pieces.update({at ^ (1 << bit): swap(piece, bit) for at, piece in pieces.items()})
-        gathered = jnp.concatenate([pieces[i] for i in range(n_exp)], axis=0)
-        return plain([gathered], base_weight, keep_mask, dual_start, topk)
+        mine = [column_rows(own) for own in sent]
+    if top != 3 or 2 * n_exp * mine[0].shape[0] * width > 16 * MIB:
+        gathered = []
+        for own in mine:
+            pieces = {0: own}
+            for bit in [*range(1, top), 0]:
+                pieces.update({at ^ (1 << bit): swap(piece, bit) for at, piece in pieces.items()})
+            gathered.append(jnp.concatenate([pieces[i] for i in range(n_exp)], axis=0))
+        return plain(gathered, base_weight, keep_mask, dual_start, topk)
     with jax.named_scope("load_weights"):
-        base_weight, dual_start, token = load([mine], base_weight, dual_start)
+        base_weight, dual_start, token = load(mine, base_weight, dual_start)
+    gathered = []
     with jax.named_scope("exchange_rows"):
-        one, two = swap(mine, 1), swap(mine, 2)
-        middle = mine.shape[1] // 2 // LANES * LANES
-        far = [swap(after(token, one[:, :middle]), 2), swap(after(token, two[:, middle:]), 1)]
-        pieces = [mine, one, two, jnp.concatenate(far, axis=1)]
-        pieces += [swap(piece, 0) for piece in pieces]
-    gathered = [jnp.concatenate(pieces, axis=0)]
+        for own in mine:
+            one, two = swap(own, 1), swap(own, 2)
+            middle = own.shape[1] // 2 // LANES * LANES
+            far = [swap(after(token, one[:, :middle]), 2), swap(after(token, two[:, middle:]), 1)]
+            pieces = [own, one, two, jnp.concatenate(far, axis=1)]
+            others = [swap(piece, 0) for piece in (after(token, own), *pieces[1:])]
+            gathered.append(jnp.concatenate(pieces + others, axis=0))
     with jax.named_scope("fused_iterations"):
         return fused(gathered, base_weight, keep_mask, dual_start, topk)
 

time: 100 us -> 101 us (1.010)
  the two profiles are of different devices: /device:TPU:17 before, /device:TPU:0 now
where the time goes in v6:
time: 101 us
  Pallas kernels  48 us (48%)
  waiting for transfers between devices  24.3 us (24%)
  starting transfers between devices  21.1 us (21%)
  local copies, waits for them, and re-layouts  3.54 us (4%)
  other arithmetic  2.93 us (3%)
    pallas_call x1, Pallas kernels, fused(): pl.pallas_call(functools.partial(fused_kernel, chunk, topk, len(gathered)...  36.2 us
    ppermute x16, waiting for transfers between devices, swap(): return lax.ppermute(piece, 'exp', [(i, i ^ 1 << bit) for i in range(n)])  19.1 us
    ppermute x6, starting transfers between devices, column_rows(): lax.ppermute(own, 'tok', [(i, (i + shift) % n) for i in range(n)])  11.9 us
    pallas_call x1, Pallas kernels, load(): pl.pallas_call(functools.partial(load_kernel, len(marks)), in_specs=[anyw...  11.8 us
    ppermute x16, starting transfers between devices, swap(): return lax.ppermute(piece, 'exp', [(i, i ^ 1 << bit) for i in range(n)])  9.23 us
    ppermute x6, waiting for transfers between devices, column_rows(): lax.ppermute(own, 'tok', [(i, (i + shift) % n) for i in range(n)])  5.19 us
    unnamed x22, local copies, waits for them, and re-layouts  3.38 us
  transfers between devices with their start and end apart: 22, of which 8 were waited for; matrix products, arithmetic and copies ran while one was open for 5% of the time, Pallas kernels for 12%

profile of v6, /device:TPU:0, one launch (start us, length us, event | category | flops | bytes accessed | tf_op | source)
XLA Modules:
  0.0 100.7 jit_solution(739705890437641072)
XLA Ops:
  0.6 1.6 %constant_dynamic-update-slice_fusion.21 = (bf16[768,2048]{1,0:T(8,128)(2,1)S(1)}, bf16[24,2048]{1,0:T(8,128)(2,1)}, bf16[24,2048]{1,0:T(8,128)(2,1)S(1)}) fusion(bf16[24,4096]{1,0:T(8,128)(2,1)} %param.5), kind=kLoop, calls=%fused_computation.31 | loop fusion | bytes 491520
  2.2 5.0 %collective-permute-start.7 = (bf16[24,2048]{1,0:T(8,128)(2,1)}, bf16[24,2048]{1,0:T(8,128)(2,1)S(1)}, u32[]{:S(2)}, u32[]{:S(2)}) collective-permute-start(bf16[24,2048]{1,0:T(8,128)(2,1)} %get-tuple-element.16), channel_id=1, source_target_pairs={{0,24},{8,0},{16,8},{24,16},{1,25},{9,1},{17,9},{25,17},{2,26},{10... | collective-permute-start | bytes 294920 | tf_op jit(solution)/shard_map/exchange_rows/ppermute | solution.py:225
  7.3 1.0 %collective-permute-start.5 = (bf16[24,2048]{1,0:T(8,128)(2,1)}, bf16[24,2048]{1,0:T(8,128)(2,1)S(1)}, u32[]{:S(2)}, u32[]{:S(2)}) collective-permute-start(bf16[24,2048]{1,0:T(8,128)(2,1)} %get-tuple-element.16), channel_id=1, source_target_pairs={{0,8},{8,16},{16,24},{24,0},{1,9},{9,17},{17,25},{25,1},{2,10},{10... | collective-permute-start | bytes 294920 | tf_op jit(solution)/shard_map/exchange_rows/ppermute | solution.py:225
  8.3 0.7 convert_element_type.5
  9.1 2.0 %collective-permute-start.1 = (bf16[24,2176]{1,0:T(8,128)(2,1)S(1)}, bf16[24,2176]{1,0:T(8,128)(2,1)S(1)}, u32[]{:S(2)}, u32[]{:S(2)}) collective-permute-start(bf16[24,2176]{1,0:T(8,128)(2,1)S(1)} %get-tuple-element.18), channel_id=1, source_target_pairs={{0,16},{8,24},{16,0},{24,8},{1,17},{9,25},{17,1},{25,9},{2,18},{10... | collective-permute-start | bytes 313352 | tf_op jit(solution)/shard_map/exchange_rows/ppermute | solution.py:225
  11.1 1.5 %collective-permute-start = (bf16[24,2176]{1,0:T(8,128)(2,1)S(1)}, bf16[24,2176]{1,0:T(8,128)(2,1)S(1)}, u32[]{:S(2)}, u32[]{:S(2)}) collective-permute-start(bf16[24,2176]{1,0:T(8,128)(2,1)S(1)} %get-tuple-element.18), channel_id=1, source_target_pairs={{0,8},{8,16},{16,24},{24,0},{1,9},{9,17},{17,25},{25,1},{2,10},{10... | collective-permute-start | bytes 313352 | tf_op jit(solution)/shard_map/exchange_rows/ppermute | solution.py:225
  12.6 1.3 %copy.11.refs_4_ = s32[4,6,64]{2,1,0:T(8,128)} copy(s32[4,6,64]{2,0,1:T(4,128)} %param.8) | data formatting | bytes 12288 | tf_op args[3]
  13.9 2.4 %collective-permute-start.2 = (bf16[24,2176]{1,0:T(8,128)(2,1)S(1)}, bf16[24,2176]{1,0:T(8,128)(2,1)S(1)}, u32[]{:S(2)}, u32[]{:S(2)}) collective-permute-start(bf16[24,2176]{1,0:T(8,128)(2,1)S(1)} %get-tuple-element.18), channel_id=1, source_target_pairs={{0,24},{8,0},{16,8},{24,16},{1,25},{9,1},{17,9},{25,17},{2,26},{10... | collective-permute-start | bytes 313352 | tf_op jit(solution)/shard_map/exchange_rows/ppermute | solution.py:225
  16.2 5.2 %collective-permute-done.6 = bf16[24,2048]{1,0:T(8,128)(2,1)S(1)} collective-permute-done((bf16[24,2048]{1,0:T(8,128)(2,1)}, bf16[24,2048]{1,0:T(8,128)(2,1)S(1)}, u32[]{:S(2)}, u32[]{:S(2)}) %collective-permute-start.6) | collective-permute-done | bytes 98336 | tf_op jit(solution)/shard_map/exchange_rows/ppermute | solution.py:225
  21.4 0.9 pad_maximum_fusion.2.refs_1_
  22.3 1.6 %collective-permute-start.15 = (bf16[96,2048]{1,0:T(8,128)(2,1)S(1)}, bf16[96,2048]{1,0:T(8,128)(2,1)S(1)}, u32[]{:S(2)}, u32[]{:S(2)}) collective-permute-start(bf16[96,2048]{1,0:T(8,128)(2,1)S(1)} %pad_maximum_fusion.2.refs_1_), channel_id=1, source_target_pairs={{0,4},{1,5},{2,6},{3,7},{4,0},{5,1},{6,2},{7,3},{8,12},{9,13},{10,... | collective-permute-start | bytes 1179656 | tf_op jit(solution)/shard_map/exchange_rows/ppermute | solution.py:218
  23.9 1.5 %collective-permute-start.14 = (bf16[96,2048]{1,0:T(8,128)(2,1)S(1)}, bf16[96,2048]{1,0:T(8,128)(2,1)S(1)}, u32[]{:S(2)}, u32[]{:S(2)}) collective-permute-start(bf16[96,2048]{1,0:T(8,128)(2,1)S(1)} %pad_maximum_fusion.2.refs_1_), channel_id=1, source_target_pairs={{0,2},{1,3},{2,0},{3,1},{4,6},{5,7},{6,4},{7,5},{8,10},{9,11},{10,... | collective-permute-start | bytes 1179656 | tf_op jit(solution)/shard_map/exchange_rows/ppermute | solution.py:218
  25.5 0.6 collective-permute-start.4
  26.1 0.8 collective-permute-start.3
  26.9 11.8 %load_weights.1 = (bf16[4,384,4096]{2,1,0:T(8,128)(2,1)S(1)}, f32[4,384,4096]{2,1,0:T(8,128)S(1)}, bf16[96,2176]{1,0:T(8,128)(2,1)S(1)}) custom-call(bf16[96,2176]{1,0:T(8,128)(2,1)S(1)} %pad_maximum_fusion.refs_0_, bf16[96,2048]{1,0:T(8,128)(2,1)S(1)} %pad_maximum_fusion.2.refs_1_, bf16[4,384,4096]{2,1,0:T(8,128)(2,1)} %refs_2_.1, f32[4,384,4096]{2,1,0:T(8,128)} %refs_3_.1), custom_call_target="tpu_custom_call" | custom-call | bytes 37748736 | tf_op jit(solution)/shard_map/load_weights/pallas_call | solution.py:52
  38.7 1.0 slice_multiply_fusion
  40.7 1.8 %collective-permute-done.3 = bf16[96,2176]{1,0:T(8,128)(2,1)S(1)} collective-permute-done((bf16[96,2176]{1,0:T(8,128)(2,1)S(1)}, bf16[96,2176]{1,0:T(8,128)(2,1)S(1)}, u32[]{:S(2)}, u32[]{:S(2)}) %collective-permute-start.3) | collective-permute-done | bytes 417824 | tf_op jit(solution)/shard_map/exchange_rows/ppermute | solution.py:218
  42.5 1.6 %collective-permute-start.17 = (bf16[96,1024]{1,0:T(8,128)(2,1)S(1)}, bf16[96,1024]{1,0:T(8,128)(2,1)S(1)}, u32[]{:S(2)}, u32[]{:S(2)}) collective-permute-start(bf16[96,1024]{1,0:T(8,128)(2,1)S(1)} %get-tuple-element.12), channel_id=1, source_target_pairs={{0,2},{1,3},{2,0},{3,1},{4,6},{5,7},{6,4},{7,5},{8,10},{9,11},{10,... | collective-permute-start | bytes 589832 | tf_op jit(solution)/shard_map/exchange_rows/ppermute | solution.py:218
  44.8 5.2 %collective-permute-done.16 = bf16[96,1024]{1,0:T(8,128)(2,1)S(1)} collective-permute-done((bf16[96,1024]{1,0:T(8,128)(2,1)S(1)}, bf16[96,1024]{1,0:T(8,128)(2,1)S(1)}, u32[]{:S(2)}, u32[]{:S(2)}) %collective-permute-start.16) | collective-permute-done | bytes 196640 | tf_op jit(solution)/shard_map/exchange_rows/ppermute | solution.py:218
  50.0 0.7 collective-permute-start.8
  50.8 4.9 %collective-permute-done.8 = bf16[96,1024]{1,0:T(8,128)(2,1)S(1)} collective-permute-done((bf16[96,1024]{1,0:T(8,128)(2,1)S(1)}, bf16[96,1024]{1,0:T(8,128)(2,1)S(1)}, u32[]{:S(2)}, u32[]{:S(2)}) %collective-permute-start.8) | collective-permute-done | bytes 196640 | tf_op jit(solution)/shard_map/exchange_rows/ppermute | solution.py:218
  56.3 5.3 %collective-permute-done.9 = bf16[96,1152]{1,0:T(8,128)(2,1)S(1)} collective-permute-done((bf16[96,1152]{1,0:T(8,128)(2,1)S(1)}, bf16[96,1152]{1,0:T(8,128)(2,1)S(1)}, u32[]{:S(2)}, u32[]{:S(2)}) %collective-permute-start.9) | collective-permute-done | bytes 221216 | tf_op jit(solution)/shard_map/exchange_rows/ppermute | solution.py:218
  62.4 0.9 collective-permute-done.11
  64.5 36.2 %fused_iterations.1 = (f32[4,384,4096]{2,1,0:T(8,128)}, f32[4,384,4096]{2,1,0:T(8,128)}, f32[4,384,4096]{2,1,0:T(8,128)S(1)}) custom-call(bf16[768,2176]{1,0:T(8,128)(2,1)S(1)} %constant_dynamic-update-slice_fusion.refs_0_, bf16[768,2048]{1,0:T(8,128)(2,1)S(1)} %constant_dynamic-update-slice_fusion.11.refs_1_, ...), custom_call_target="tpu_custom_call", output_to_operand_aliasing={{2}: (3, {})} | custom-call | flops 19327352832 | bytes 50331648 | tf_op jit(solution)/shard_map/fused_iterations/pallas_call | solution.py:164
  (58 shorter events, 4.6 us)
Async XLA Ops:
  2.2 11.6 %collective-permute-start.7 = (bf16[24,2048]{1,0:T(8,128)(2,1)}, bf16[24,2048]{1,0:T(8,128)(2,1)S(1)}, u32[]{:S(2)}, u32[]{:S(2)}) collective-permute-start(bf16[24,2048]{1,0:T(8,128)(2,1)} %get-tuple-element.16), channel_id=1, source_target_pairs={{0,24},{8,0},{16,8},{24,16},{1,25},{9,1},{17,9},{25,17},{2,26},{10... | collective-permute-start | bytes 294920 | tf_op jit(solution)/shard_map/exchange_rows/ppermute | solution.py:225
  7.3 14.1 %collective-permute-start.6 = (bf16[24,2048]{1,0:T(8,128)(2,1)}, bf16[24,2048]{1,0:T(8,128)(2,1)S(1)}, u32[]{:S(2)}, u32[]{:S(2)}) collective-permute-start(bf16[24,2048]{1,0:T(8,128)(2,1)} %get-tuple-element.16), channel_id=1, source_target_pairs={{0,16},{8,24},{16,0},{24,8},{1,17},{9,25},{17,1},{25,9},{2,18},{10... | collective-permute-start | bytes 294920 | tf_op jit(solution)/shard_map/exchange_rows/ppermute | solution.py:225
  7.3 14.1 %collective-permute-start.5 = (bf16[24,2048]{1,0:T(8,128)(2,1)}, bf16[24,2048]{1,0:T(8,128)(2,1)S(1)}, u32[]{:S(2)}, u32[]{:S(2)}) collective-permute-start(bf16[24,2048]{1,0:T(8,128)(2,1)} %get-tuple-element.16), channel_id=1, source_target_pairs={{0,8},{8,16},{16,24},{24,0},{1,9},{9,17},{17,25},{25,1},{2,10},{10... | collective-permute-start | bytes 294920 | tf_op jit(solution)/shard_map/exchange_rows/ppermute | solution.py:225
  9.1 16.3 %collective-permute-start.1 = (bf16[24,2176]{1,0:T(8,128)(2,1)S(1)}, bf16[24,2176]{1,0:T(8,128)(2,1)S(1)}, u32[]{:S(2)}, u32[]{:S(2)}) collective-permute-start(bf16[24,2176]{1,0:T(8,128)(2,1)S(1)} %get-tuple-element.18), channel_id=1, source_target_pairs={{0,16},{8,24},{16,0},{24,8},{1,17},{9,25},{17,1},{25,9},{2,18},{10... | collective-permute-start | bytes 313352 | tf_op jit(solution)/shard_map/exchange_rows/ppermute | solution.py:225
  11.1 14.4 %collective-permute-start = (bf16[24,2176]{1,0:T(8,128)(2,1)S(1)}, bf16[24,2176]{1,0:T(8,128)(2,1)S(1)}, u32[]{:S(2)}, u32[]{:S(2)}) collective-permute-start(bf16[24,2176]{1,0:T(8,128)(2,1)S(1)} %get-tuple-element.18), channel_id=1, source_target_pairs={{0,8},{8,16},{16,24},{24,0},{1,9},{9,17},{17,25},{25,1},{2,10},{10... | collective-permute-start | bytes 313352 | tf_op jit(solution)/shard_map/exchange_rows/ppermute | solution.py:225
  13.9 11.6 %collective-permute-start.2 = (bf16[24,2176]{1,0:T(8,128)(2,1)S(1)}, bf16[24,2176]{1,0:T(8,128)(2,1)S(1)}, u32[]{:S(2)}, u32[]{:S(2)}) collective-permute-start(bf16[24,2176]{1,0:T(8,128)(2,1)S(1)} %get-tuple-element.18), channel_id=1, source_target_pairs={{0,24},{8,0},{16,8},{24,16},{1,25},{9,1},{17,9},{25,17},{2,26},{10... | collective-permute-start | bytes 313352 | tf_op jit(solution)/shard_map/exchange_rows/ppermute | solution.py:225
  22.3 17.7 %collective-permute-start.15 = (bf16[96,2048]{1,0:T(8,128)(2,1)S(1)}, bf16[96,2048]{1,0:T(8,128)(2,1)S(1)}, u32[]{:S(2)}, u32[]{:S(2)}) collective-permute-start(bf16[96,2048]{1,0:T(8,128)(2,1)S(1)} %pad_maximum_fusion.2.refs_1_), channel_id=1, source_target_pairs={{0,4},{1,5},{2,6},{3,7},{4,0},{5,1},{6,2},{7,3},{8,12},{9,13},{10,... | collective-permute-start | bytes 1179656 | tf_op jit(solution)/shard_map/exchange_rows/ppermute | solution.py:218
  23.9 16.7 %collective-permute-start.14 = (bf16[96,2048]{1,0:T(8,128)(2,1)S(1)}, bf16[96,2048]{1,0:T(8,128)(2,1)S(1)}, u32[]{:S(2)}, u32[]{:S(2)}) collective-permute-start(bf16[96,2048]{1,0:T(8,128)(2,1)S(1)} %pad_maximum_fusion.2.refs_1_), channel_id=1, source_target_pairs={{0,2},{1,3},{2,0},{3,1},{4,6},{5,7},{6,4},{7,5},{8,10},{9,11},{10,... | collective-permute-start | bytes 1179656 | tf_op jit(solution)/shard_map/exchange_rows/ppermute | solution.py:218
  25.5 18.6 %collective-permute-start.4 = (bf16[96,2176]{1,0:T(8,128)(2,1)S(1)}, bf16[96,2176]{1,0:T(8,128)(2,1)S(1)}, u32[]{:S(2)}, u32[]{:S(2)}) collective-permute-start(bf16[96,2176]{1,0:T(8,128)(2,1)S(1)} %pad_maximum_fusion.refs_0_), channel_id=1, source_target_pairs={{0,4},{1,5},{2,6},{3,7},{4,0},{5,1},{6,2},{7,3},{8,12},{9,13},{10,... | collective-permute-start | bytes 1253384 | tf_op jit(solution)/shard_map/exchange_rows/ppermute | solution.py:218
  26.1 16.4 %collective-permute-start.3 = (bf16[96,2176]{1,0:T(8,128)(2,1)S(1)}, bf16[96,2176]{1,0:T(8,128)(2,1)S(1)}, u32[]{:S(2)}, u32[]{:S(2)}) collective-permute-start(bf16[96,2176]{1,0:T(8,128)(2,1)S(1)} %pad_maximum_fusion.refs_0_), channel_id=1, source_target_pairs={{0,2},{1,3},{2,0},{3,1},{4,6},{5,7},{6,4},{7,5},{8,10},{9,11},{10,... | collective-permute-start | bytes 1253384 | tf_op jit(solution)/shard_map/exchange_rows/ppermute | solution.py:218
  39.7 16.4 %collective-permute-start.18 = (bf16[96,2048]{1,0:T(8,128)(2,1)S(1)}, bf16[96,2048]{1,0:T(8,128)(2,1)S(1)}, u32[]{:S(2)}, u32[]{:S(2)}) collective-permute-start(bf16[96,2048]{1,0:T(8,128)(2,1)S(1)} %slice_multiply_fusion), channel_id=1, source_target_pairs={{0,1},{1,0},{2,3},{3,2},{4,5},{5,4},{6,7},{7,6},{8,9},{9,8},{10,11... | collective-permute-start | bytes 1179656 | tf_op jit(solution)/shard_map/exchange_rows/ppermute | solution.py:218
  40.0 21.7 %collective-permute-start.10 = (bf16[96,2176]{1,0:T(8,128)(2,1)S(1)}, bf16[96,2176]{1,0:T(8,128)(2,1)S(1)}, u32[]{:S(2)}, u32[]{:S(2)}) collective-permute-start(bf16[96,2176]{1,0:T(8,128)(2,1)S(1)} %fusion), channel_id=1, source_target_pairs={{0,1},{1,0},{2,3},{3,2},{4,5},{5,4},{6,7},{7,6},{8,9},{9,8},{10,11... | collective-permute-start | bytes 1253384 | tf_op jit(solution)/shard_map/exchange_rows/ppermute | solution.py:218
  40.6 21.8 %collective-permute-start.20 = (bf16[96,2048]{1,0:T(8,128)(2,1)S(1)}, bf16[96,2048]{1,0:T(8,128)(2,1)S(1)}, u32[]{:S(2)}, u32[]{:S(2)}) collective-permute-start(bf16[96,2048]{1,0:T(8,128)(2,1)S(1)} %collective-permute-done.15), channel_id=1, source_target_pairs={{0,1},{1,0},{2,3},{3,2},{4,5},{5,4},{6,7},{7,6},{8,9},{9,8},{10,11... | collective-permute-start | bytes 1179656 | tf_op jit(solution)/shard_map/exchange_rows/ppermute | solution.py:218
  42.5 8.1 %collective-permute-start.17 = (bf16[96,1024]{1,0:T(8,128)(2,1)S(1)}, bf16[96,1024]{1,0:T(8,128)(2,1)S(1)}, u32[]{:S(2)}, u32[]{:S(2)}) collective-permute-start(bf16[96,1024]{1,0:T(8,128)(2,1)S(1)} %get-tuple-element.12), channel_id=1, source_target_pairs={{0,2},{1,3},{2,0},{3,1},{4,6},{5,7},{6,4},{7,5},{8,10},{9,11},{10,... | collective-permute-start | bytes 589832 | tf_op jit(solution)/shard_map/exchange_rows/ppermute | solution.py:218
  44.1 5.8 %collective-permute-start.16 = (bf16[96,1024]{1,0:T(8,128)(2,1)S(1)}, bf16[96,1024]{1,0:T(8,128)(2,1)S(1)}, u32[]{:S(2)}, u32[]{:S(2)}) collective-permute-start(bf16[96,1024]{1,0:T(8,128)(2,1)S(1)} %get-tuple-element.13), channel_id=1, source_target_pairs={{0,4},{1,5},{2,6},{3,7},{4,0},{5,1},{6,2},{7,3},{8,12},{9,13},{10,... | collective-permute-start | bytes 589832 | tf_op jit(solution)/shard_map/exchange_rows/ppermute | solution.py:218
  50.0 5.7 %collective-permute-start.8 = (bf16[96,1024]{1,0:T(8,128)(2,1)S(1)}, bf16[96,1024]{1,0:T(8,128)(2,1)S(1)}, u32[]{:S(2)}, u32[]{:S(2)}) collective-permute-start(bf16[96,1024]{1,0:T(8,128)(2,1)S(1)} %get-tuple-element.14), channel_id=1, source_target_pairs={{0,4},{1,5},{2,6},{3,7},{4,0},{5,1},{6,2},{7,3},{8,12},{9,13},{10,... | collective-permute-start | bytes 589832 | tf_op jit(solution)/shard_map/exchange_rows/ppermute | solution.py:218
  50.7 11.6 %collective-permute-start.19 = (bf16[96,2048]{1,0:T(8,128)(2,1)S(1)}, bf16[96,2048]{1,0:T(8,128)(2,1)S(1)}, u32[]{:S(2)}, u32[]{:S(2)}) collective-permute-start(bf16[96,2048]{1,0:T(8,128)(2,1)S(1)} %collective-permute-done.14), channel_id=1, source_target_pairs={{0,1},{1,0},{2,3},{3,2},{4,5},{5,4},{6,7},{7,6},{8,9},{9,8},{10,11... | collective-permute-start | bytes 1179656 | tf_op jit(solution)/shard_map/exchange_rows/ppermute | solution.py:218
  55.6 5.9 %collective-permute-start.9 = (bf16[96,1152]{1,0:T(8,128)(2,1)S(1)}, bf16[96,1152]{1,0:T(8,128)(2,1)S(1)}, u32[]{:S(2)}, u32[]{:S(2)}) collective-permute-start(bf16[96,1152]{1,0:T(8,128)(2,1)S(1)} %slice_multiply_fusion.1), channel_id=1, source_target_pairs={{0,2},{1,3},{2,0},{3,1},{4,6},{5,7},{6,4},{7,5},{8,10},{9,11},{10,... | collective-permute-start | bytes 663560 | tf_op jit(solution)/shard_map/exchange_rows/ppermute | solution.py:218
  56.2 7.2 %collective-permute-start.12 = (bf16[96,2176]{1,0:T(8,128)(2,1)S(1)}, bf16[96,2176]{1,0:T(8,128)(2,1)S(1)}, u32[]{:S(2)}, u32[]{:S(2)}) collective-permute-start(bf16[96,2176]{1,0:T(8,128)(2,1)S(1)} %collective-permute-done.4), channel_id=1, source_target_pairs={{0,1},{1,0},{2,3},{3,2},{4,5},{5,4},{6,7},{7,6},{8,9},{9,8},{10,11... | collective-permute-start | bytes 1253384 | tf_op jit(solution)/shard_map/exchange_rows/ppermute | solution.py:218
  61.6 1.8 %collective-permute-start.11 = (bf16[96,2176]{1,0:T(8,128)(2,1)S(1)}, bf16[96,2176]{1,0:T(8,128)(2,1)S(1)}, u32[]{:S(2)}, u32[]{:S(2)}) collective-permute-start(bf16[96,2176]{1,0:T(8,128)(2,1)S(1)} %collective-permute-done.3), channel_id=1, source_target_pairs={{0,1},{1,0},{2,3},{3,2},{4,5},{5,4},{6,7},{7,6},{8,9},{9,8},{10,11... | collective-permute-start | bytes 1253384 | tf_op jit(solution)/shard_map/exchange_rows/ppermute | solution.py:218
  61.7 2.2 %collective-permute-start.21 = (bf16[96,2048]{1,0:T(8,128)(2,1)S(1)}, bf16[96,2048]{1,0:T(8,128)(2,1)S(1)}, u32[]{:S(2)}, u32[]{:S(2)}) collective-permute-start(bf16[96,2048]{1,0:T(8,128)(2,1)S(1)} %pad_maximum_fusion.3), channel_id=1, source_target_pairs={{0,1},{1,0},{2,3},{3,2},{4,5},{5,4},{6,7},{7,6},{8,9},{9,8},{10,11... | collective-permute-start | bytes 1179656 | tf_op jit(solution)/shard_map/exchange_rows/ppermute | solution.py:218
  62.3 2.2 %collective-permute-start.13 = (bf16[96,2176]{1,0:T(8,128)(2,1)S(1)}, bf16[96,2176]{1,0:T(8,128)(2,1)S(1)}, u32[]{:S(2)}, u32[]{:S(2)}) collective-permute-start(bf16[96,2176]{1,0:T(8,128)(2,1)S(1)} %pad_maximum_fusion.1), channel_id=1, source_target_pairs={{0,1},{1,0},{2,3},{3,2},{4,5},{5,4},{6,7},{7,6},{8,9},{9,8},{10,11... | collective-permute-start | bytes 1253384 | tf_op jit(solution)/shard_map/exchange_rows/ppermute | solution.py:218

commit v7 on v6

--- a/solution.py
+++ b/solution.py
@@ -251,12 +251,11 @@
         base_weight, dual_start, token = load(mine, base_weight, dual_start)
     gathered = []
     with jax.named_scope("exchange_rows"):
-        for own in mine:
-            one, two = swap(own, 1), swap(own, 2)
-            middle = own.shape[1] // 2 // LANES * LANES
-            far = [swap(after(token, one[:, :middle]), 2), swap(after(token, two[:, middle:]), 1)]
-            pieces = [own, one, two, jnp.concatenate(far, axis=1)]
-            others = [swap(piece, 0) for piece in (after(token, own), *pieces[1:])]
+        near = [[own, swap(own, 1), swap(own, 2)] for own in mine]
+        far = [swap(after(token, near[0][1]), 2), swap(after(token, near[1][2]), 1)]
+        for blocks, last in zip(near, far):
+            pieces = [*blocks, last]
+            others = [swap(piece, 0) for piece in (after(token, blocks[0]), *pieces[1:])]
             gathered.append(jnp.concatenate(pieces + others, axis=0))
     with jax.named_scope("fused_iterations"):
         return fused(gathered, base_weight, keep_mask, dual_start, topk)

time: 101 us -> 102 us (level)
  local copies, waits for them, and re-layouts: 3.54 us -> 7.45 us
  waiting for transfers between devices: 24.3 us -> 21.3 us
    unnamed x22 -> x18, local copies, waits for them, and re-layouts: 3.38 us -> 7.29 us
    ppermute x16 -> x14, waiting for transfers between devices: 19.1 us -> 16.1 us  [swap(): return lax.ppermute(piece, 'exp', [(i, i ^ 1 << bit) for i in range(n)])]
    ppermute x16 -> x14, starting transfers between devices: 9.23 us -> 8.48 us  [swap(): return lax.ppermute(piece, 'exp', [(i, i ^ 1 << bit) for i in range(n)])]
  transfers between devices with their start and end apart: 22 -> 20, of which waited for: 8 -> 5; matrix products, arithmetic and copies ran while one was open for 5% -> 9% of each run, Pallas kernels for 12% -> 12%
where the time goes in v7:
time: 102 us; the launch traced here: 101 us
  Pallas kernels  48.3 us (47%)
  waiting for transfers between devices  21.3 us (21%)
  starting transfers between devices  20.3 us (20%)
  local copies, waits for them, and re-layouts  7.45 us (7%)
  other arithmetic  2.93 us (3%)
    pallas_call x1, Pallas kernels, fused(): pl.pallas_call(functools.partial(fused_kernel, chunk, topk, len(gathered)...  36.5 us
    ppermute x14, waiting for transfers between devices, swap(): return lax.ppermute(piece, 'exp', [(i, i ^ 1 << bit) for i in range(n)])  16.1 us
    ppermute x6, starting transfers between devices, column_rows(): lax.ppermute(own, 'tok', [(i, (i + shift) % n) for i in range(n)])  11.9 us
    pallas_call x1, Pallas kernels, load(): pl.pallas_call(functools.partial(load_kernel, len(marks)), in_specs=[anyw...  11.8 us
    ppermute x14, starting transfers between devices, swap(): return lax.ppermute(piece, 'exp', [(i, i ^ 1 << bit) for i in range(n)])  8.48 us
    unnamed x18, local copies, waits for them, and re-layouts  7.29 us
    ppermute x6, waiting for transfers between devices, column_rows(): lax.ppermute(own, 'tok', [(i, (i + shift) % n) for i in range(n)])  5.19 us
  transfers between devices with their start and end apart: 20, of which 5 were waited for; matrix products, arithmetic and copies ran while one was open for 9% of the time, Pallas kernels for 12%

profile of v7, /device:TPU:0, one launch (start us, length us, event | category | flops | bytes accessed | tf_op | source)
XLA Modules:
  0.0 101.1 jit_solution(2687107128076853836)
XLA Ops:
  0.6 1.6 %constant_dynamic-update-slice_fusion.21 = (bf16[768,2048]{1,0:T(8,128)(2,1)S(1)}, bf16[24,2048]{1,0:T(8,128)(2,1)}, bf16[24,2048]{1,0:T(8,128)(2,1)S(1)}) fusion(bf16[24,4096]{1,0:T(8,128)(2,1)} %param.5), kind=kLoop, calls=%fused_computation.26 | loop fusion | bytes 491520
  2.2 5.0 %collective-permute-start.7 = (bf16[24,2048]{1,0:T(8,128)(2,1)}, bf16[24,2048]{1,0:T(8,128)(2,1)S(1)}, u32[]{:S(2)}, u32[]{:S(2)}) collective-permute-start(bf16[24,2048]{1,0:T(8,128)(2,1)} %get-tuple-element.19), channel_id=1, source_target_pairs={{0,24},{8,0},{16,8},{24,16},{1,25},{9,1},{17,9},{25,17},{2,26},{10... | collective-permute-start | bytes 294920 | tf_op jit(solution)/shard_map/exchange_rows/ppermute | solution.py:225
  7.3 1.0 collective-permute-start.5
  9.1 2.0 %collective-permute-start.1 = (bf16[24,2176]{1,0:T(8,128)(2,1)S(1)}, bf16[24,2176]{1,0:T(8,128)(2,1)S(1)}, u32[]{:S(2)}, u32[]{:S(2)}) collective-permute-start(bf16[24,2176]{1,0:T(8,128)(2,1)S(1)} %get-tuple-element.21), channel_id=1, source_target_pairs={{0,16},{8,24},{16,0},{24,8},{1,17},{9,25},{17,1},{25,9},{2,18},{10... | collective-permute-start | bytes 313352 | tf_op jit(solution)/shard_map/exchange_rows/ppermute | solution.py:225
  11.1 1.5 %collective-permute-start = (bf16[24,2176]{1,0:T(8,128)(2,1)S(1)}, bf16[24,2176]{1,0:T(8,128)(2,1)S(1)}, u32[]{:S(2)}, u32[]{:S(2)}) collective-permute-start(bf16[24,2176]{1,0:T(8,128)(2,1)S(1)} %get-tuple-element.21), channel_id=1, source_target_pairs={{0,8},{8,16},{16,24},{24,0},{1,9},{9,17},{17,25},{25,1},{2,10},{10... | collective-permute-start | bytes 313352 | tf_op jit(solution)/shard_map/exchange_rows/ppermute | solution.py:225
  12.6 1.3 %copy.11.refs_4_ = s32[4,6,64]{2,1,0:T(8,128)} copy(s32[4,6,64]{2,0,1:T(4,128)} %param.8) | data formatting | bytes 12288 | tf_op args[3]
  13.9 2.4 %collective-permute-start.2 = (bf16[24,2176]{1,0:T(8,128)(2,1)S(1)}, bf16[24,2176]{1,0:T(8,128)(2,1)S(1)}, u32[]{:S(2)}, u32[]{:S(2)}) collective-permute-start(bf16[24,2176]{1,0:T(8,128)(2,1)S(1)} %get-tuple-element.21), channel_id=1, source_target_pairs={{0,24},{8,0},{16,8},{24,16},{1,25},{9,1},{17,9},{25,17},{2,26},{10... | collective-permute-start | bytes 313352 | tf_op jit(solution)/shard_map/exchange_rows/ppermute | solution.py:225
  16.2 5.2 %collective-permute-done.6 = bf16[24,2048]{1,0:T(8,128)(2,1)S(1)} collective-permute-done((bf16[24,2048]{1,0:T(8,128)(2,1)}, bf16[24,2048]{1,0:T(8,128)(2,1)S(1)}, u32[]{:S(2)}, u32[]{:S(2)}) %collective-permute-start.6) | collective-permute-done | bytes 98336 | tf_op jit(solution)/shard_map/exchange_rows/ppermute | solution.py:225
  21.4 0.9 pad_maximum_fusion.1.refs_1_
  22.3 1.6 %collective-permute-start.14 = (bf16[96,2048]{1,0:T(8,128)(2,1)S(1)}, bf16[96,2048]{1,0:T(8,128)(2,1)S(1)}, u32[]{:S(2)}, u32[]{:S(2)}) collective-permute-start(bf16[96,2048]{1,0:T(8,128)(2,1)S(1)} %pad_maximum_fusion.1.refs_1_), channel_id=1, source_target_pairs={{0,4},{1,5},{2,6},{3,7},{4,0},{5,1},{6,2},{7,3},{8,12},{9,13},{10,... | collective-permute-start | bytes 1179656 | tf_op jit(solution)/shard_map/exchange_rows/ppermute | solution.py:218
  23.9 1.5 %collective-permute-start.13 = (bf16[96,2048]{1,0:T(8,128)(2,1)S(1)}, bf16[96,2048]{1,0:T(8,128)(2,1)S(1)}, u32[]{:S(2)}, u32[]{:S(2)}) collective-permute-start(bf16[96,2048]{1,0:T(8,128)(2,1)S(1)} %pad_maximum_fusion.1.refs_1_), channel_id=1, source_target_pairs={{0,2},{1,3},{2,0},{3,1},{4,6},{5,7},{6,4},{7,5},{8,10},{9,11},{10,... | collective-permute-start | bytes 1179656 | tf_op jit(solution)/shard_map/exchange_rows/ppermute | solution.py:218
  27.0 11.8 %load_weights.1 = (bf16[4,384,4096]{2,1,0:T(8,128)(2,1)S(1)}, f32[4,384,4096]{2,1,0:T(8,128)S(1)}, bf16[96,2176]{1,0:T(8,128)(2,1)S(1)}) custom-call(bf16[96,2176]{1,0:T(8,128)(2,1)S(1)} %pad_maximum_fusion.refs_0_, bf16[96,2048]{1,0:T(8,128)(2,1)S(1)} %pad_maximum_fusion.1.refs_1_, bf16[4,384,4096]{2,1,0:T(8,128)(2,1)} %refs_2_.1, f32[4,384,4096]{2,1,0:T(8,128)} %refs_3_.1), custom_call_target="tpu_custom_call" | custom-call | bytes 37748736 | tf_op jit(solution)/shard_map/load_weights/pallas_call | solution.py:52
  38.9 1.1 %slice_multiply_fusion = (bf16[96,2048]{1,0:T(8,128)(2,1)S(1)}, bf16[96,2048]{1,0:T(8,128)(2,1)S(1)}, bf16[768,2048]{1,0:T(8,128)(2,1)S(1)}) fusion(bf16[96,2176]{1,0:T(8,128)(2,1)S(1)} %get-tuple-element.7, bf16[24,2048]{1,0:T(8,128)(2,1)S(1)} %collective-permute-done.7, bf16[24,2048]{1,0:T(8,128)(2,1)S(1)} %collective-permute-done.6, ...), kind=kLoop, calls=%fused_computation.2 | loop fusion | flops 2555904 | bytes 2359296 | tf_op jit(solution)/shard_map/exchange_rows/mul | solution.py:213
  40.0 1.3 %collective-permute-start.15 = (bf16[96,2048]{1,0:T(8,128)(2,1)S(1)}, bf16[96,2048]{1,0:T(8,128)(2,1)}, u32[]{:S(2)}, u32[]{:S(2)}) collective-permute-start(bf16[96,2048]{1,0:T(8,128)(2,1)S(1)} %get-tuple-element.13), channel_id=1, source_target_pairs={{0,2},{1,3},{2,0},{3,1},{4,6},{5,7},{6,4},{7,5},{8,10},{9,11},{10,... | collective-permute-start | bytes 1179656 | tf_op jit(solution)/shard_map/exchange_rows/ppermute | solution.py:218
  41.4 1.1 %collective-permute-done.3 = bf16[96,2176]{1,0:T(8,128)(2,1)S(1)} collective-permute-done((bf16[96,2176]{1,0:T(8,128)(2,1)S(1)}, bf16[96,2176]{1,0:T(8,128)(2,1)S(1)}, u32[]{:S(2)}, u32[]{:S(2)}) %collective-permute-start.3) | collective-permute-done | bytes 417824 | tf_op jit(solution)/shard_map/exchange_rows/ppermute | solution.py:218
  43.3 8.3 %collective-permute-done.15 = bf16[96,2048]{1,0:T(8,128)(2,1)} collective-permute-done((bf16[96,2048]{1,0:T(8,128)(2,1)S(1)}, bf16[96,2048]{1,0:T(8,128)(2,1)}, u32[]{:S(2)}, u32[]{:S(2)}) %collective-permute-start.15) | collective-permute-done | bytes 393248 | tf_op jit(solution)/shard_map/exchange_rows/ppermute | solution.py:218
  51.6 1.2 %collective-permute-start.8 = (bf16[96,2176]{1,0:T(8,128)(2,1)S(1)}, bf16[96,2176]{1,0:T(8,128)(2,1)S(1)}, u32[]{:S(2)}, u32[]{:S(2)}) collective-permute-start(bf16[96,2176]{1,0:T(8,128)(2,1)S(1)} %get-tuple-element.15), channel_id=1, source_target_pairs={{0,4},{1,5},{2,6},{3,7},{4,0},{5,1},{6,2},{7,3},{8,12},{9,13},{10,... | collective-permute-start | bytes 1253384 | tf_op jit(solution)/shard_map/exchange_rows/ppermute | solution.py:218
  52.9 1.0 %constant_dynamic-update-slice_fusion.15 = bf16[768,2048]{1,0:T(8,128)(2,1)S(1)} fusion(bf16[768,2048]{1,0:T(8,128)(2,1)S(1)} %get-tuple-element.17, bf16[96,2048]{1,0:T(8,128)(2,1)} %collective-permute-done.15), kind=kLoop, calls=%fused_computation.20 | loop fusion | bytes 786432
  54.0 1.0 %constant_dynamic-update-slice_fusion.14 = bf16[768,2048]{1,0:T(8,128)(2,1)S(1)} fusion(bf16[768,2048]{1,0:T(8,128)(2,1)S(1)} %constant_dynamic-update-slice_fusion.15, bf16[96,2048]{1,0:T(8,128)(2,1)} %collective-permute-done.16), kind=kLoop, calls=%fused_computation.19 | loop fusion | bytes 786432
  55.6 1.0 %constant_dynamic-update-slice_fusion.13 = bf16[768,2048]{1,0:T(8,128)(2,1)S(1)} fusion(bf16[768,2048]{1,0:T(8,128)(2,1)S(1)} %constant_dynamic-update-slice_fusion.14, bf16[96,2048]{1,0:T(8,128)(2,1)} %collective-permute-done.17), kind=kLoop, calls=%fused_computation.18 | loop fusion | bytes 786432
  56.7 1.0 %constant_dynamic-update-slice_fusion.12 = bf16[768,2048]{1,0:T(8,128)(2,1)S(1)} fusion(bf16[768,2048]{1,0:T(8,128)(2,1)S(1)} %constant_dynamic-update-slice_fusion.13, bf16[96,2048]{1,0:T(8,128)(2,1)} %collective-permute-done.18), kind=kLoop, calls=%fused_computation.17 | loop fusion | bytes 786432
  57.7 5.1 %collective-permute-done.8 = bf16[96,2176]{1,0:T(8,128)(2,1)S(1)} collective-permute-done((bf16[96,2176]{1,0:T(8,128)(2,1)S(1)}, bf16[96,2176]{1,0:T(8,128)(2,1)S(1)}, u32[]{:S(2)}, u32[]{:S(2)}) %collective-permute-start.8) | collective-permute-done | bytes 417824 | tf_op jit(solution)/shard_map/exchange_rows/ppermute | solution.py:218
  63.1 1.5 %collective-permute-done.12 = bf16[96,2176]{1,0:T(8,128)(2,1)S(1)} collective-permute-done((bf16[96,2176]{1,0:T(8,128)(2,1)S(1)}, bf16[96,2176]{1,0:T(8,128)(2,1)S(1)}, u32[]{:S(2)}, u32[]{:S(2)}) %collective-permute-start.12) | collective-permute-done | bytes 417824 | tf_op jit(solution)/shard_map/exchange_rows/ppermute | solution.py:218
  64.6 36.5 %fused_iterations.1 = (f32[4,384,4096]{2,1,0:T(8,128)}, f32[4,384,4096]{2,1,0:T(8,128)}, f32[4,384,4096]{2,1,0:T(8,128)S(1)}) custom-call(bf16[768,2176]{1,0:T(8,128)(2,1)S(1)} %constant_dynamic-update-slice_fusion.refs_0_, bf16[768,2048]{1,0:T(8,128)(2,1)S(1)} %constant_dynamic-update-slice_fusion.11.refs_1_, ...), custom_call_target="tpu_custom_call", output_to_operand_aliasing={{2}: (3, {})} | custom-call | flops 19327352832 | bytes 50331648 | tf_op jit(solution)/shard_map/fused_iterations/pallas_call | solution.py:164
  (46 shorter events, 4.4 us)
Async XLA Ops:
  2.2 11.6 %collective-permute-start.7 = (bf16[24,2048]{1,0:T(8,128)(2,1)}, bf16[24,2048]{1,0:T(8,128)(2,1)S(1)}, u32[]{:S(2)}, u32[]{:S(2)}) collective-permute-start(bf16[24,2048]{1,0:T(8,128)(2,1)} %get-tuple-element.19), channel_id=1, source_target_pairs={{0,24},{8,0},{16,8},{24,16},{1,25},{9,1},{17,9},{25,17},{2,26},{10... | collective-permute-start | bytes 294920 | tf_op jit(solution)/shard_map/exchange_rows/ppermute | solution.py:225
  7.3 14.1 %collective-permute-start.6 = (bf16[24,2048]{1,0:T(8,128)(2,1)}, bf16[24,2048]{1,0:T(8,128)(2,1)S(1)}, u32[]{:S(2)}, u32[]{:S(2)}) collective-permute-start(bf16[24,2048]{1,0:T(8,128)(2,1)} %get-tuple-element.19), channel_id=1, source_target_pairs={{0,16},{8,24},{16,0},{24,8},{1,17},{9,25},{17,1},{25,9},{2,18},{10... | collective-permute-start | bytes 294920 | tf_op jit(solution)/shard_map/exchange_rows/ppermute | solution.py:225
  7.3 14.1 %collective-permute-start.5 = (bf16[24,2048]{1,0:T(8,128)(2,1)}, bf16[24,2048]{1,0:T(8,128)(2,1)S(1)}, u32[]{:S(2)}, u32[]{:S(2)}) collective-permute-start(bf16[24,2048]{1,0:T(8,128)(2,1)} %get-tuple-element.19), channel_id=1, source_target_pairs={{0,8},{8,16},{16,24},{24,0},{1,9},{9,17},{17,25},{25,1},{2,10},{10... | collective-permute-start | bytes 294920 | tf_op jit(solution)/shard_map/exchange_rows/ppermute | solution.py:225
  9.1 16.3 %collective-permute-start.1 = (bf16[24,2176]{1,0:T(8,128)(2,1)S(1)}, bf16[24,2176]{1,0:T(8,128)(2,1)S(1)}, u32[]{:S(2)}, u32[]{:S(2)}) collective-permute-start(bf16[24,2176]{1,0:T(8,128)(2,1)S(1)} %get-tuple-element.21), channel_id=1, source_target_pairs={{0,16},{8,24},{16,0},{24,8},{1,17},{9,25},{17,1},{25,9},{2,18},{10... | collective-permute-start | bytes 313352 | tf_op jit(solution)/shard_map/exchange_rows/ppermute | solution.py:225
  11.1 14.4 %collective-permute-start = (bf16[24,2176]{1,0:T(8,128)(2,1)S(1)}, bf16[24,2176]{1,0:T(8,128)(2,1)S(1)}, u32[]{:S(2)}, u32[]{:S(2)}) collective-permute-start(bf16[24,2176]{1,0:T(8,128)(2,1)S(1)} %get-tuple-element.21), channel_id=1, source_target_pairs={{0,8},{8,16},{16,24},{24,0},{1,9},{9,17},{17,25},{25,1},{2,10},{10... | collective-permute-start | bytes 313352 | tf_op jit(solution)/shard_map/exchange_rows/ppermute | solution.py:225
  13.9 11.6 %collective-permute-start.2 = (bf16[24,2176]{1,0:T(8,128)(2,1)S(1)}, bf16[24,2176]{1,0:T(8,128)(2,1)S(1)}, u32[]{:S(2)}, u32[]{:S(2)}) collective-permute-start(bf16[24,2176]{1,0:T(8,128)(2,1)S(1)} %get-tuple-element.21), channel_id=1, source_target_pairs={{0,24},{8,0},{16,8},{24,16},{1,25},{9,1},{17,9},{25,17},{2,26},{10... | collective-permute-start | bytes 313352 | tf_op jit(solution)/shard_map/exchange_rows/ppermute | solution.py:225
  22.3 16.5 %collective-permute-start.14 = (bf16[96,2048]{1,0:T(8,128)(2,1)S(1)}, bf16[96,2048]{1,0:T(8,128)(2,1)S(1)}, u32[]{:S(2)}, u32[]{:S(2)}) collective-permute-start(bf16[96,2048]{1,0:T(8,128)(2,1)S(1)} %pad_maximum_fusion.1.refs_1_), channel_id=1, source_target_pairs={{0,4},{1,5},{2,6},{3,7},{4,0},{5,1},{6,2},{7,3},{8,12},{9,13},{10,... | collective-permute-start | bytes 1179656 | tf_op jit(solution)/shard_map/exchange_rows/ppermute | solution.py:218
  23.9 14.9 %collective-permute-start.13 = (bf16[96,2048]{1,0:T(8,128)(2,1)S(1)}, bf16[96,2048]{1,0:T(8,128)(2,1)S(1)}, u32[]{:S(2)}, u32[]{:S(2)}) collective-permute-start(bf16[96,2048]{1,0:T(8,128)(2,1)S(1)} %pad_maximum_fusion.1.refs_1_), channel_id=1, source_target_pairs={{0,2},{1,3},{2,0},{3,1},{4,6},{5,7},{6,4},{7,5},{8,10},{9,11},{10,... | collective-permute-start | bytes 1179656 | tf_op jit(solution)/shard_map/exchange_rows/ppermute | solution.py:218
  25.5 17.2 %collective-permute-start.4 = (bf16[96,2176]{1,0:T(8,128)(2,1)S(1)}, bf16[96,2176]{1,0:T(8,128)(2,1)S(1)}, u32[]{:S(2)}, u32[]{:S(2)}) collective-permute-start(bf16[96,2176]{1,0:T(8,128)(2,1)S(1)} %pad_maximum_fusion.refs_0_), channel_id=1, source_target_pairs={{0,4},{1,5},{2,6},{3,7},{4,0},{5,1},{6,2},{7,3},{8,12},{9,13},{10,... | collective-permute-start | bytes 1253384 | tf_op jit(solution)/shard_map/exchange_rows/ppermute | solution.py:218
  26.1 16.4 %collective-permute-start.3 = (bf16[96,2176]{1,0:T(8,128)(2,1)S(1)}, bf16[96,2176]{1,0:T(8,128)(2,1)S(1)}, u32[]{:S(2)}, u32[]{:S(2)}) collective-permute-start(bf16[96,2176]{1,0:T(8,128)(2,1)S(1)} %pad_maximum_fusion.refs_0_), channel_id=1, source_target_pairs={{0,2},{1,3},{2,0},{3,1},{4,6},{5,7},{6,4},{7,5},{8,10},{9,11},{10,... | collective-permute-start | bytes 1253384 | tf_op jit(solution)/shard_map/exchange_rows/ppermute | solution.py:218
  39.9 14.0 %collective-permute-start.16 = (bf16[96,2048]{1,0:T(8,128)(2,1)S(1)}, bf16[96,2048]{1,0:T(8,128)(2,1)}, u32[]{:S(2)}, u32[]{:S(2)}) collective-permute-start(bf16[96,2048]{1,0:T(8,128)(2,1)S(1)} %get-tuple-element.12), channel_id=1, source_target_pairs={{0,1},{1,0},{2,3},{3,2},{4,5},{5,4},{6,7},{7,6},{8,9},{9,8},{10,11... | collective-permute-start | bytes 1179656 | tf_op jit(solution)/shard_map/exchange_rows/ppermute | solution.py:218
  40.0 11.6 %collective-permute-start.15 = (bf16[96,2048]{1,0:T(8,128)(2,1)S(1)}, bf16[96,2048]{1,0:T(8,128)(2,1)}, u32[]{:S(2)}, u32[]{:S(2)}) collective-permute-start(bf16[96,2048]{1,0:T(8,128)(2,1)S(1)} %get-tuple-element.13), channel_id=1, source_target_pairs={{0,2},{1,3},{2,0},{3,1},{4,6},{5,7},{6,4},{7,5},{8,10},{9,11},{10,... | collective-permute-start | bytes 1179656 | tf_op jit(solution)/shard_map/exchange_rows/ppermute | solution.py:218
  41.3 15.3 %collective-permute-start.18 = (bf16[96,2048]{1,0:T(8,128)(2,1)S(1)}, bf16[96,2048]{1,0:T(8,128)(2,1)}, u32[]{:S(2)}, u32[]{:S(2)}) collective-permute-start(bf16[96,2048]{1,0:T(8,128)(2,1)S(1)} %collective-permute-done.14), channel_id=1, source_target_pairs={{0,1},{1,0},{2,3},{3,2},{4,5},{5,4},{6,7},{7,6},{8,9},{9,8},{10,11... | collective-permute-start | bytes 1179656 | tf_op jit(solution)/shard_map/exchange_rows/ppermute | solution.py:218
  42.5 12.5 %collective-permute-start.17 = (bf16[96,2048]{1,0:T(8,128)(2,1)S(1)}, bf16[96,2048]{1,0:T(8,128)(2,1)}, u32[]{:S(2)}, u32[]{:S(2)}) collective-permute-start(bf16[96,2048]{1,0:T(8,128)(2,1)S(1)} %collective-permute-done.13), channel_id=1, source_target_pairs={{0,1},{1,0},{2,3},{3,2},{4,5},{5,4},{6,7},{7,6},{8,9},{9,8},{10,11... | collective-permute-start | bytes 1179656 | tf_op jit(solution)/shard_map/exchange_rows/ppermute | solution.py:218
  42.7 20.2 %collective-permute-start.9 = (bf16[96,2176]{1,0:T(8,128)(2,1)S(1)}, bf16[96,2176]{1,0:T(8,128)(2,1)S(1)}, u32[]{:S(2)}, u32[]{:S(2)}) collective-permute-start(bf16[96,2176]{1,0:T(8,128)(2,1)S(1)} %get-tuple-element.14), channel_id=1, source_target_pairs={{0,1},{1,0},{2,3},{3,2},{4,5},{5,4},{6,7},{7,6},{8,9},{9,8},{10,11... | collective-permute-start | bytes 1253384 | tf_op jit(solution)/shard_map/exchange_rows/ppermute | solution.py:218
  51.6 11.2 %collective-permute-start.8 = (bf16[96,2176]{1,0:T(8,128)(2,1)S(1)}, bf16[96,2176]{1,0:T(8,128)(2,1)S(1)}, u32[]{:S(2)}, u32[]{:S(2)}) collective-permute-start(bf16[96,2176]{1,0:T(8,128)(2,1)S(1)} %get-tuple-element.15), channel_id=1, source_target_pairs={{0,4},{1,5},{2,6},{3,7},{4,0},{5,1},{6,2},{7,3},{8,12},{9,13},{10,... | collective-permute-start | bytes 1253384 | tf_op jit(solution)/shard_map/exchange_rows/ppermute | solution.py:218
  53.9 9.1 %collective-permute-start.11 = (bf16[96,2176]{1,0:T(8,128)(2,1)S(1)}, bf16[96,2176]{1,0:T(8,128)(2,1)S(1)}, u32[]{:S(2)}, u32[]{:S(2)}) collective-permute-start(bf16[96,2176]{1,0:T(8,128)(2,1)S(1)} %collective-permute-done.4), channel_id=1, source_target_pairs={{0,1},{1,0},{2,3},{3,2},{4,5},{5,4},{6,7},{7,6},{8,9},{9,8},{10,11... | collective-permute-start | bytes 1253384 | tf_op jit(solution)/shard_map/exchange_rows/ppermute | solution.py:218
  55.0 7.9 %collective-permute-start.10 = (bf16[96,2176]{1,0:T(8,128)(2,1)S(1)}, bf16[96,2176]{1,0:T(8,128)(2,1)S(1)}, u32[]{:S(2)}, u32[]{:S(2)}) collective-permute-start(bf16[96,2176]{1,0:T(8,128)(2,1)S(1)} %collective-permute-done.3), channel_id=1, source_target_pairs={{0,1},{1,0},{2,3},{3,2},{4,5},{5,4},{6,7},{7,6},{8,9},{9,8},{10,11... | collective-permute-start | bytes 1253384 | tf_op jit(solution)/shard_map/exchange_rows/ppermute | solution.py:218
  56.6 6.5 %collective-permute-start.19 = (bf16[96,2048]{1,0:T(8,128)(2,1)}, bf16[96,2048]{1,0:T(8,128)(2,1)S(1)}, u32[]{:S(2)}, u32[]{:S(2)}) collective-permute-start(bf16[96,2048]{1,0:T(8,128)(2,1)} %collective-permute-done.15), channel_id=1, source_target_pairs={{0,1},{1,0},{2,3},{3,2},{4,5},{5,4},{6,7},{7,6},{8,9},{9,8},{10,11... | collective-permute-start | bytes 1179656 | tf_op jit(solution)/shard_map/exchange_rows/ppermute | solution.py:218
  62.9 1.8 %collective-permute-start.12 = (bf16[96,2176]{1,0:T(8,128)(2,1)S(1)}, bf16[96,2176]{1,0:T(8,128)(2,1)S(1)}, u32[]{:S(2)}, u32[]{:S(2)}) collective-permute-start(bf16[96,2176]{1,0:T(8,128)(2,1)S(1)} %collective-permute-done.8), channel_id=1, source_target_pairs={{0,1},{1,0},{2,3},{3,2},{4,5},{5,4},{6,7},{7,6},{8,9},{9,8},{10,11... | collective-permute-start | bytes 1253384 | tf_op jit(solution)/shard_map/exchange_rows/ppermute | solution.py:218

commit v8 on v7

--- a/solution.py
+++ b/solution.py
@@ -253,10 +253,10 @@
     with jax.named_scope("exchange_rows"):
         near = [[own, swap(own, 1), swap(own, 2)] for own in mine]
         far = [swap(after(token, near[0][1]), 2), swap(after(token, near[1][2]), 1)]
-        for blocks, last in zip(near, far):
-            pieces = [*blocks, last]
-            others = [swap(piece, 0) for piece in (after(token, blocks[0]), *pieces[1:])]
-            gathered.append(jnp.concatenate(pieces + others, axis=0))
+        for h, ((own, *others), last) in enumerate(zip(near, far)):
+            pair = swap(jnp.concatenate([after(token, others[0]), others[1]], axis=0), 0)
+            theirs = [swap(own if h else after(token, own), 0), pair, swap(last, 0)]
+            gathered.append(jnp.concatenate([own, *others, last, *theirs], axis=0))
     with jax.named_scope("fused_iterations"):
         return fused(gathered, base_weight, keep_mask, dual_start, topk)
 

time: 102 us -> 96 us (0.941)
  waiting for transfers between devices: 21.3 us -> 18.1 us
  local copies, waits for them, and re-layouts: 7.45 us -> 5.5 us
    ppermute x14 -> x12, waiting for transfers between devices: 16.1 us -> 12.9 us  [swap(): return lax.ppermute(piece, 'exp', [(i, i ^ 1 << bit) for i in range(n)])]
    unnamed x18 -> x16, local copies, waits for them, and re-layouts: 7.29 us -> 5.34 us
    ppermute x14 -> x12, starting transfers between devices: 8.48 us -> 8.15 us  [swap(): return lax.ppermute(piece, 'exp', [(i, i ^ 1 << bit) for i in range(n)])]
  transfers between devices with their start and end apart: 20 -> 18, of which waited for: 5 -> 5; matrix products, arithmetic and copies ran while one was open for 9% -> 7% of each run, Pallas kernels for 12% -> 12%
where the time goes in v8:
time: 96 us; the launch traced here: 95.6 us
  Pallas kernels  48.3 us (50%)
  starting transfers between devices  20 us (21%)
  waiting for transfers between devices  18.1 us (19%)
  local copies, waits for them, and re-layouts  5.5 us (6%)
  other arithmetic  2.9 us (3%)
    pallas_call x1, Pallas kernels, fused(): pl.pallas_call(functools.partial(fused_kernel, chunk, topk, len(gathered)...  36.4 us
    ppermute x12, waiting for transfers between devices, swap(): return lax.ppermute(piece, 'exp', [(i, i ^ 1 << bit) for i in range(n)])  12.9 us
    ppermute x6, starting transfers between devices, column_rows(): lax.ppermute(own, 'tok', [(i, (i + shift) % n) for i in range(n)])  11.9 us
    pallas_call x1, Pallas kernels, load(): pl.pallas_call(functools.partial(load_kernel, len(marks)), in_specs=[anyw...  11.8 us
    ppermute x12, starting transfers between devices, swap(): return lax.ppermute(piece, 'exp', [(i, i ^ 1 << bit) for i in range(n)])  8.15 us
    unnamed x16, local copies, waits for them, and re-layouts  5.34 us
    ppermute x6, waiting for transfers between devices, column_rows(): lax.ppermute(own, 'tok', [(i, (i + shift) % n) for i in range(n)])  5.19 us
  transfers between devices with their start and end apart: 18, of which 5 were waited for; matrix products, arithmetic and copies ran while one was open for 7% of the time, Pallas kernels for 12%

profile of v8, /device:TPU:0, one launch (start us, length us, event | category | flops | bytes accessed | tf_op | source)
XLA Modules:
  0.0 95.6 jit_solution(17990441984195664731)
XLA Ops:
  0.6 1.6 %constant_dynamic-update-slice_fusion.19 = (bf16[768,2048]{1,0:T(8,128)(2,1)S(1)}, bf16[24,2048]{1,0:T(8,128)(2,1)}, bf16[24,2048]{1,0:T(8,128)(2,1)S(1)}) fusion(bf16[24,4096]{1,0:T(8,128)(2,1)} %param.5), kind=kLoop, calls=%fused_computation.26 | loop fusion | bytes 491520
  2.2 5.0 %collective-permute-start.7 = (bf16[24,2048]{1,0:T(8,128)(2,1)}, bf16[24,2048]{1,0:T(8,128)(2,1)S(1)}, u32[]{:S(2)}, u32[]{:S(2)}) collective-permute-start(bf16[24,2048]{1,0:T(8,128)(2,1)} %get-tuple-element.19), channel_id=1, source_target_pairs={{0,24},{8,0},{16,8},{24,16},{1,25},{9,1},{17,9},{25,17},{2,26},{10... | collective-permute-start | bytes 294920 | tf_op jit(solution)/shard_map/exchange_rows/ppermute | solution.py:225
  7.3 1.0 %collective-permute-start.5 = (bf16[24,2048]{1,0:T(8,128)(2,1)}, bf16[24,2048]{1,0:T(8,128)(2,1)S(1)}, u32[]{:S(2)}, u32[]{:S(2)}) collective-permute-start(bf16[24,2048]{1,0:T(8,128)(2,1)} %get-tuple-element.19), channel_id=1, source_target_pairs={{0,8},{8,16},{16,24},{24,0},{1,9},{9,17},{17,25},{25,1},{2,10},{10... | collective-permute-start | bytes 294920 | tf_op jit(solution)/shard_map/exchange_rows/ppermute | solution.py:225
  8.3 0.7 convert_element_type.5
  9.1 2.0 %collective-permute-start.1 = (bf16[24,2176]{1,0:T(8,128)(2,1)S(1)}, bf16[24,2176]{1,0:T(8,128)(2,1)S(1)}, u32[]{:S(2)}, u32[]{:S(2)}) collective-permute-start(bf16[24,2176]{1,0:T(8,128)(2,1)S(1)} %get-tuple-element.21), channel_id=1, source_target_pairs={{0,16},{8,24},{16,0},{24,8},{1,17},{9,25},{17,1},{25,9},{2,18},{10... | collective-permute-start | bytes 313352 | tf_op jit(solution)/shard_map/exchange_rows/ppermute | solution.py:225
  11.1 1.5 %collective-permute-start = (bf16[24,2176]{1,0:T(8,128)(2,1)S(1)}, bf16[24,2176]{1,0:T(8,128)(2,1)S(1)}, u32[]{:S(2)}, u32[]{:S(2)}) collective-permute-start(bf16[24,2176]{1,0:T(8,128)(2,1)S(1)} %get-tuple-element.21), channel_id=1, source_target_pairs={{0,8},{8,16},{16,24},{24,0},{1,9},{9,17},{17,25},{25,1},{2,10},{10... | collective-permute-start | bytes 313352 | tf_op jit(solution)/shard_map/exchange_rows/ppermute | solution.py:225
  12.6 1.3 %copy.11.refs_4_ = s32[4,6,64]{2,1,0:T(8,128)} copy(s32[4,6,64]{2,0,1:T(4,128)} %param.8) | data formatting | bytes 12288 | tf_op args[3]
  13.9 2.4 %collective-permute-start.2 = (bf16[24,2176]{1,0:T(8,128)(2,1)S(1)}, bf16[24,2176]{1,0:T(8,128)(2,1)S(1)}, u32[]{:S(2)}, u32[]{:S(2)}) collective-permute-start(bf16[24,2176]{1,0:T(8,128)(2,1)S(1)} %get-tuple-element.21), channel_id=1, source_target_pairs={{0,24},{8,0},{16,8},{24,16},{1,25},{9,1},{17,9},{25,17},{2,26},{10... | collective-permute-start | bytes 313352 | tf_op jit(solution)/shard_map/exchange_rows/ppermute | solution.py:225
  16.2 5.2 %collective-permute-done.6 = bf16[24,2048]{1,0:T(8,128)(2,1)S(1)} collective-permute-done((bf16[24,2048]{1,0:T(8,128)(2,1)}, bf16[24,2048]{1,0:T(8,128)(2,1)S(1)}, u32[]{:S(2)}, u32[]{:S(2)}) %collective-permute-start.6) | collective-permute-done | bytes 98336 | tf_op jit(solution)/shard_map/exchange_rows/ppermute | solution.py:225
  21.4 0.9 pad_maximum_fusion.3.refs_1_
  22.4 1.6 %collective-permute-start.13 = (bf16[96,2048]{1,0:T(8,128)(2,1)S(1)}, bf16[96,2048]{1,0:T(8,128)(2,1)S(1)}, u32[]{:S(2)}, u32[]{:S(2)}) collective-permute-start(bf16[96,2048]{1,0:T(8,128)(2,1)S(1)} %pad_maximum_fusion.3.refs_1_), channel_id=1, source_target_pairs={{0,4},{1,5},{2,6},{3,7},{4,0},{5,1},{6,2},{7,3},{8,12},{9,13},{10,... | collective-permute-start | bytes 1179656 | tf_op jit(solution)/shard_map/exchange_rows/ppermute | solution.py:218
  24.0 1.6 %collective-permute-start.12 = (bf16[96,2048]{1,0:T(8,128)(2,1)S(1)}, bf16[96,2048]{1,0:T(8,128)(2,1)S(1)}, u32[]{:S(2)}, u32[]{:S(2)}) collective-permute-start(bf16[96,2048]{1,0:T(8,128)(2,1)S(1)} %pad_maximum_fusion.3.refs_1_), channel_id=1, source_target_pairs={{0,2},{1,3},{2,0},{3,1},{4,6},{5,7},{6,4},{7,5},{8,10},{9,11},{10,... | collective-permute-start | bytes 1179656 | tf_op jit(solution)/shard_map/exchange_rows/ppermute | solution.py:218
  25.6 1.1 %collective-permute-start.4 = (bf16[96,2176]{1,0:T(8,128)(2,1)S(1)}, bf16[96,2176]{1,0:T(8,128)(2,1)S(1)}, u32[]{:S(2)}, u32[]{:S(2)}) collective-permute-start(bf16[96,2176]{1,0:T(8,128)(2,1)S(1)} %pad_maximum_fusion.2.refs_0_), channel_id=1, source_target_pairs={{0,4},{1,5},{2,6},{3,7},{4,0},{5,1},{6,2},{7,3},{8,12},{9,13},{10,... | collective-permute-start | bytes 1253384 | tf_op jit(solution)/shard_map/exchange_rows/ppermute | solution.py:218
  27.3 11.8 %load_weights.1 = (bf16[4,384,4096]{2,1,0:T(8,128)(2,1)S(1)}, f32[4,384,4096]{2,1,0:T(8,128)S(1)}, bf16[96,2176]{1,0:T(8,128)(2,1)S(1)}) custom-call(bf16[96,2176]{1,0:T(8,128)(2,1)S(1)} %pad_maximum_fusion.2.refs_0_, bf16[96,2048]{1,0:T(8,128)(2,1)S(1)} %pad_maximum_fusion.3.refs_1_, bf16[4,384,4096]{2,1,0:T(8,128)(2,1)} %refs_2_.1, f32[4,384,4096]{2,1,0:T(8,128)} %refs_3_.1), custom_call_target="tpu_custom_call" | custom-call | bytes 37748736 | tf_op jit(solution)/shard_map/load_weights/pallas_call | solution.py:52
  39.2 0.9 slice_multiply_fusion
  40.1 1.5 %collective-permute-start.14 = (bf16[96,2048]{1,0:T(8,128)(2,1)}, bf16[96,2048]{1,0:T(8,128)(2,1)}, u32[]{:S(2)}, u32[]{:S(2)}) collective-permute-start(bf16[96,2048]{1,0:T(8,128)(2,1)} %get-tuple-element.13), channel_id=1, source_target_pairs={{0,2},{1,3},{2,0},{3,1},{4,6},{5,7},{6,4},{7,5},{8,10},{9,11},{10,... | collective-permute-start | bytes 1179656 | tf_op jit(solution)/shard_map/exchange_rows/ppermute | solution.py:218
  41.7 3.3 %collective-permute-done.3 = bf16[96,2176]{1,0:T(8,128)(2,1)S(1)} collective-permute-done((bf16[96,2176]{1,0:T(8,128)(2,1)S(1)}, bf16[96,2176]{1,0:T(8,128)(2,1)S(1)}, u32[]{:S(2)}, u32[]{:S(2)}) %collective-permute-start.3) | collective-permute-done | bytes 417824 | tf_op jit(solution)/shard_map/exchange_rows/ppermute | solution.py:218
  45.3 1.1 %collective-permute-start.8 = (bf16[96,2176]{1,0:T(8,128)(2,1)S(1)}, bf16[96,2176]{1,0:T(8,128)(2,1)S(1)}, u32[]{:S(2)}, u32[]{:S(2)}) collective-permute-start(bf16[96,2176]{1,0:T(8,128)(2,1)S(1)} %get-tuple-element.15), channel_id=1, source_target_pairs={{0,4},{1,5},{2,6},{3,7},{4,0},{5,1},{6,2},{7,3},{8,12},{9,13},{10,... | collective-permute-start | bytes 1253384 | tf_op jit(solution)/shard_map/exchange_rows/ppermute | solution.py:218
  46.5 6.2 %collective-permute-done.14 = bf16[96,2048]{1,0:T(8,128)(2,1)} collective-permute-done((bf16[96,2048]{1,0:T(8,128)(2,1)}, bf16[96,2048]{1,0:T(8,128)(2,1)}, u32[]{:S(2)}, u32[]{:S(2)}) %collective-permute-start.14) | collective-permute-done | bytes 393248 | tf_op jit(solution)/shard_map/exchange_rows/ppermute | solution.py:218
  52.8 1.0 %constant_dynamic-update-slice_fusion.13 = bf16[768,2048]{1,0:T(8,128)(2,1)S(1)} fusion(bf16[768,2048]{1,0:T(8,128)(2,1)S(1)} %get-tuple-element.17, bf16[96,2048]{1,0:T(8,128)(2,1)} %collective-permute-done.14), kind=kLoop, calls=%fused_computation.20 | loop fusion | bytes 786432
  54.4 1.0 %constant_dynamic-update-slice_fusion.12 = bf16[768,2048]{1,0:T(8,128)(2,1)S(1)} fusion(bf16[768,2048]{1,0:T(8,128)(2,1)S(1)} %constant_dynamic-update-slice_fusion.13, bf16[96,2048]{1,0:T(8,128)(2,1)} %collective-permute-done.15), kind=kLoop, calls=%fused_computation.19 | loop fusion | bytes 786432
  55.4 1.9 %collective-permute-done.8 = bf16[96,2176]{1,0:T(8,128)(2,1)S(1)} collective-permute-done((bf16[96,2176]{1,0:T(8,128)(2,1)S(1)}, bf16[96,2176]{1,0:T(8,128)(2,1)S(1)}, u32[]{:S(2)}, u32[]{:S(2)}) %collective-permute-start.8) | collective-permute-done | bytes 417824 | tf_op jit(solution)/shard_map/exchange_rows/ppermute | solution.py:218
  57.7 1.4 %collective-permute-done.11 = bf16[96,2176]{1,0:T(8,128)(2,1)S(1)} collective-permute-done((bf16[96,2176]{1,0:T(8,128)(2,1)S(1)}, bf16[96,2176]{1,0:T(8,128)(2,1)S(1)}, u32[]{:S(2)}, u32[]{:S(2)}) %collective-permute-start.11) | collective-permute-done | bytes 417824 | tf_op jit(solution)/shard_map/exchange_rows/ppermute | solution.py:218
  59.2 36.4 %fused_iterations.1 = (f32[4,384,4096]{2,1,0:T(8,128)}, f32[4,384,4096]{2,1,0:T(8,128)}, f32[4,384,4096]{2,1,0:T(8,128)S(1)}) custom-call(bf16[768,2176]{1,0:T(8,128)(2,1)S(1)} %constant_dynamic-update-slice_fusion.refs_0_, bf16[768,2048]{1,0:T(8,128)(2,1)S(1)} %constant_dynamic-update-slice_fusion.10.refs_1_, ...), custom_call_target="tpu_custom_call", output_to_operand_aliasing={{2}: (3, {})} | custom-call | flops 19327352832 | bytes 50331648 | tf_op jit(solution)/shard_map/fused_iterations/pallas_call | solution.py:164
  (42 shorter events, 2.3 us)
Async XLA Ops:
  2.2 11.6 %collective-permute-start.7 = (bf16[24,2048]{1,0:T(8,128)(2,1)}, bf16[24,2048]{1,0:T(8,128)(2,1)S(1)}, u32[]{:S(2)}, u32[]{:S(2)}) collective-permute-start(bf16[24,2048]{1,0:T(8,128)(2,1)} %get-tuple-element.19), channel_id=1, source_target_pairs={{0,24},{8,0},{16,8},{24,16},{1,25},{9,1},{17,9},{25,17},{2,26},{10... | collective-permute-start | bytes 294920 | tf_op jit(solution)/shard_map/exchange_rows/ppermute | solution.py:225
  7.3 14.1 %collective-permute-start.6 = (bf16[24,2048]{1,0:T(8,128)(2,1)}, bf16[24,2048]{1,0:T(8,128)(2,1)S(1)}, u32[]{:S(2)}, u32[]{:S(2)}) collective-permute-start(bf16[24,2048]{1,0:T(8,128)(2,1)} %get-tuple-element.19), channel_id=1, source_target_pairs={{0,16},{8,24},{16,0},{24,8},{1,17},{9,25},{17,1},{25,9},{2,18},{10... | collective-permute-start | bytes 294920 | tf_op jit(solution)/shard_map/exchange_rows/ppermute | solution.py:225
  7.3 14.1 %collective-permute-start.5 = (bf16[24,2048]{1,0:T(8,128)(2,1)}, bf16[24,2048]{1,0:T(8,128)(2,1)S(1)}, u32[]{:S(2)}, u32[]{:S(2)}) collective-permute-start(bf16[24,2048]{1,0:T(8,128)(2,1)} %get-tuple-element.19), channel_id=1, source_target_pairs={{0,8},{8,16},{16,24},{24,0},{1,9},{9,17},{17,25},{25,1},{2,10},{10... | collective-permute-start | bytes 294920 | tf_op jit(solution)/shard_map/exchange_rows/ppermute | solution.py:225
  9.1 14.9 %collective-permute-start.1 = (bf16[24,2176]{1,0:T(8,128)(2,1)S(1)}, bf16[24,2176]{1,0:T(8,128)(2,1)S(1)}, u32[]{:S(2)}, u32[]{:S(2)}) collective-permute-start(bf16[24,2176]{1,0:T(8,128)(2,1)S(1)} %get-tuple-element.21), channel_id=1, source_target_pairs={{0,16},{8,24},{16,0},{24,8},{1,17},{9,25},{17,1},{25,9},{2,18},{10... | collective-permute-start | bytes 313352 | tf_op jit(solution)/shard_map/exchange_rows/ppermute | solution.py:225
  11.1 14.5 %collective-permute-start = (bf16[24,2176]{1,0:T(8,128)(2,1)S(1)}, bf16[24,2176]{1,0:T(8,128)(2,1)S(1)}, u32[]{:S(2)}, u32[]{:S(2)}) collective-permute-start(bf16[24,2176]{1,0:T(8,128)(2,1)S(1)} %get-tuple-element.21), channel_id=1, source_target_pairs={{0,8},{8,16},{16,24},{24,0},{1,9},{9,17},{17,25},{25,1},{2,10},{10... | collective-permute-start | bytes 313352 | tf_op jit(solution)/shard_map/exchange_rows/ppermute | solution.py:225
  13.9 11.7 %collective-permute-start.2 = (bf16[24,2176]{1,0:T(8,128)(2,1)S(1)}, bf16[24,2176]{1,0:T(8,128)(2,1)S(1)}, u32[]{:S(2)}, u32[]{:S(2)}) collective-permute-start(bf16[24,2176]{1,0:T(8,128)(2,1)S(1)} %get-tuple-element.21), channel_id=1, source_target_pairs={{0,24},{8,0},{16,8},{24,16},{1,25},{9,1},{17,9},{25,17},{2,26},{10... | collective-permute-start | bytes 313352 | tf_op jit(solution)/shard_map/exchange_rows/ppermute | solution.py:225
  22.3 31.5 %collective-permute-start.15 = (bf16[96,2048]{1,0:T(8,128)(2,1)S(1)}, bf16[96,2048]{1,0:T(8,128)(2,1)}, u32[]{:S(2)}, u32[]{:S(2)}) collective-permute-start(bf16[96,2048]{1,0:T(8,128)(2,1)S(1)} %pad_maximum_fusion.3.refs_1_), channel_id=1, source_target_pairs={{0,1},{1,0},{2,3},{3,2},{4,5},{5,4},{6,7},{7,6},{8,9},{9,8},{10,11... | collective-permute-start | bytes 1179656 | tf_op jit(solution)/shard_map/exchange_rows/ppermute | solution.py:218
  22.4 16.8 %collective-permute-start.13 = (bf16[96,2048]{1,0:T(8,128)(2,1)S(1)}, bf16[96,2048]{1,0:T(8,128)(2,1)S(1)}, u32[]{:S(2)}, u32[]{:S(2)}) collective-permute-start(bf16[96,2048]{1,0:T(8,128)(2,1)S(1)} %pad_maximum_fusion.3.refs_1_), channel_id=1, source_target_pairs={{0,4},{1,5},{2,6},{3,7},{4,0},{5,1},{6,2},{7,3},{8,12},{9,13},{10,... | collective-permute-start | bytes 1179656 | tf_op jit(solution)/shard_map/exchange_rows/ppermute | solution.py:218
  24.0 15.1 %collective-permute-start.12 = (bf16[96,2048]{1,0:T(8,128)(2,1)S(1)}, bf16[96,2048]{1,0:T(8,128)(2,1)S(1)}, u32[]{:S(2)}, u32[]{:S(2)}) collective-permute-start(bf16[96,2048]{1,0:T(8,128)(2,1)S(1)} %pad_maximum_fusion.3.refs_1_), channel_id=1, source_target_pairs={{0,2},{1,3},{2,0},{3,1},{4,6},{5,7},{6,4},{7,5},{8,10},{9,11},{10,... | collective-permute-start | bytes 1179656 | tf_op jit(solution)/shard_map/exchange_rows/ppermute | solution.py:218
  25.6 19.7 %collective-permute-start.4 = (bf16[96,2176]{1,0:T(8,128)(2,1)S(1)}, bf16[96,2176]{1,0:T(8,128)(2,1)S(1)}, u32[]{:S(2)}, u32[]{:S(2)}) collective-permute-start(bf16[96,2176]{1,0:T(8,128)(2,1)S(1)} %pad_maximum_fusion.2.refs_0_), channel_id=1, source_target_pairs={{0,4},{1,5},{2,6},{3,7},{4,0},{5,1},{6,2},{7,3},{8,12},{9,13},{10,... | collective-permute-start | bytes 1253384 | tf_op jit(solution)/shard_map/exchange_rows/ppermute | solution.py:218
  26.7 18.3 %collective-permute-start.3 = (bf16[96,2176]{1,0:T(8,128)(2,1)S(1)}, bf16[96,2176]{1,0:T(8,128)(2,1)S(1)}, u32[]{:S(2)}, u32[]{:S(2)}) collective-permute-start(bf16[96,2176]{1,0:T(8,128)(2,1)S(1)} %pad_maximum_fusion.2.refs_0_), channel_id=1, source_target_pairs={{0,2},{1,3},{2,0},{3,1},{4,6},{5,7},{6,4},{7,5},{8,10},{9,11},{10,... | collective-permute-start | bytes 1253384 | tf_op jit(solution)/shard_map/exchange_rows/ppermute | solution.py:218
  40.1 12.7 %collective-permute-start.14 = (bf16[96,2048]{1,0:T(8,128)(2,1)}, bf16[96,2048]{1,0:T(8,128)(2,1)}, u32[]{:S(2)}, u32[]{:S(2)}) collective-permute-start(bf16[96,2048]{1,0:T(8,128)(2,1)} %get-tuple-element.13), channel_id=1, source_target_pairs={{0,2},{1,3},{2,0},{3,1},{4,6},{5,7},{6,4},{7,5},{8,10},{9,11},{10,... | collective-permute-start | bytes 1179656 | tf_op jit(solution)/shard_map/exchange_rows/ppermute | solution.py:218
  41.6 15.8 %collective-permute-start.16 = (bf16[192,2048]{1,0:T(8,128)(2,1)S(1)}, bf16[192,2048]{1,0:T(8,128)(2,1)S(1)}, u32[]{:S(2)}, u32[]{:S(2)}) collective-permute-start(bf16[192,2048]{1,0:T(8,128)(2,1)S(1)} %pad_maximum_fusion.1), channel_id=1, source_target_pairs={{0,1},{1,0},{2,3},{3,2},{4,5},{5,4},{6,7},{7,6},{8,9},{9,8},{10,11... | collective-permute-start | bytes 2359304 | tf_op jit(solution)/shard_map/exchange_rows/ppermute | solution.py:218
  45.2 12.2 %collective-permute-start.9 = (bf16[96,2176]{1,0:T(8,128)(2,1)S(1)}, bf16[96,2176]{1,0:T(8,128)(2,1)S(1)}, u32[]{:S(2)}, u32[]{:S(2)}) collective-permute-start(bf16[96,2176]{1,0:T(8,128)(2,1)S(1)} %get-tuple-element.14), channel_id=1, source_target_pairs={{0,1},{1,0},{2,3},{3,2},{4,5},{5,4},{6,7},{7,6},{8,9},{9,8},{10,11... | collective-permute-start | bytes 1253384 | tf_op jit(solution)/shard_map/exchange_rows/ppermute | solution.py:218
  45.3 12.1 %collective-permute-start.8 = (bf16[96,2176]{1,0:T(8,128)(2,1)S(1)}, bf16[96,2176]{1,0:T(8,128)(2,1)S(1)}, u32[]{:S(2)}, u32[]{:S(2)}) collective-permute-start(bf16[96,2176]{1,0:T(8,128)(2,1)S(1)} %get-tuple-element.15), channel_id=1, source_target_pairs={{0,4},{1,5},{2,6},{3,7},{4,0},{5,1},{6,2},{7,3},{8,12},{9,13},{10,... | collective-permute-start | bytes 1253384 | tf_op jit(solution)/shard_map/exchange_rows/ppermute | solution.py:218
  52.8 4.8 %collective-permute-start.10 = (bf16[192,2176]{1,0:T(8,128)(2,1)S(1)}, bf16[192,2176]{1,0:T(8,128)(2,1)S(1)}, u32[]{:S(2)}, u32[]{:S(2)}) collective-permute-start(bf16[192,2176]{1,0:T(8,128)(2,1)S(1)} %pad_maximum_fusion), channel_id=1, source_target_pairs={{0,1},{1,0},{2,3},{3,2},{4,5},{5,4},{6,7},{7,6},{8,9},{9,8},{10,11... | collective-permute-start | bytes 2506760 | tf_op jit(solution)/shard_map/exchange_rows/ppermute | solution.py:218
  53.8 3.7 %collective-permute-start.17 = (bf16[96,2048]{1,0:T(8,128)(2,1)}, bf16[96,2048]{1,0:T(8,128)(2,1)S(1)}, u32[]{:S(2)}, u32[]{:S(2)}) collective-permute-start(bf16[96,2048]{1,0:T(8,128)(2,1)} %collective-permute-done.14), channel_id=1, source_target_pairs={{0,1},{1,0},{2,3},{3,2},{4,5},{5,4},{6,7},{7,6},{8,9},{9,8},{10,11... | collective-permute-start | bytes 1179656 | tf_op jit(solution)/shard_map/exchange_rows/ppermute | solution.py:218
  57.4 1.8 %collective-permute-start.11 = (bf16[96,2176]{1,0:T(8,128)(2,1)S(1)}, bf16[96,2176]{1,0:T(8,128)(2,1)S(1)}, u32[]{:S(2)}, u32[]{:S(2)}) collective-permute-start(bf16[96,2176]{1,0:T(8,128)(2,1)S(1)} %collective-permute-done.8), channel_id=1, source_target_pairs={{0,1},{1,0},{2,3},{3,2},{4,5},{5,4},{6,7},{7,6},{8,9},{9,8},{10,11... | collective-permute-start | bytes 1253384 | tf_op jit(solution)/shard_map/exchange_rows/ppermute | solution.py:218

commit v9 on v8

--- a/solution.py
+++ b/solution.py
@@ -151,7 +151,7 @@
 
 def fused(gathered, base_weight, keep_mask, dual_start, topk):
     local, tall, width = base_weight.shape
-    chunk = 512
+    chunk = 256
     tokens = gathered[0].shape[0]
     slots = min(-(-tokens // ROWS_BLOCK) * MOST, tokens)
     slots = -(-slots // LANES) * LANES

time: 96 us -> 97.2 us (1.012)
  Pallas kernels: 48.3 us -> 49.4 us
    pallas_call x1, Pallas kernels: 36.4 us -> 37.6 us  [fused(): pl.pallas_call(functools.partial(fused_kernel, chunk, topk, len(gathered)...]
where the time goes in v9:
time: 97.2 us; the launch traced here: 96.8 us
  Pallas kernels  49.4 us (51%)
  starting transfers between devices  20 us (21%)
  waiting for transfers between devices  18.1 us (19%)
  local copies, waits for them, and re-layouts  5.5 us (6%)
  other arithmetic  2.9 us (3%)
    pallas_call x1, Pallas kernels, fused(): pl.pallas_call(functools.partial(fused_kernel, chunk, topk, len(gathered)...  37.6 us
    ppermute x12, waiting for transfers between devices, swap(): return lax.ppermute(piece, 'exp', [(i, i ^ 1 << bit) for i in range(n)])  12.9 us
    ppermute x6, starting transfers between devices, column_rows(): lax.ppermute(own, 'tok', [(i, (i + shift) % n) for i in range(n)])  11.9 us
    pallas_call x1, Pallas kernels, load(): pl.pallas_call(functools.partial(load_kernel, len(marks)), in_specs=[anyw...  11.8 us
    ppermute x12, starting transfers between devices, swap(): return lax.ppermute(piece, 'exp', [(i, i ^ 1 << bit) for i in range(n)])  8.15 us
    unnamed x16, local copies, waits for them, and re-layouts  5.34 us
    ppermute x6, waiting for transfers between devices, column_rows(): lax.ppermute(own, 'tok', [(i, (i + shift) % n) for i in range(n)])  5.19 us
  transfers between devices with their start and end apart: 18, of which 5 were waited for; matrix products, arithmetic and copies ran while one was open for 7% of the time, Pallas kernels for 12%

profile of v9, /device:TPU:0, one launch (start us, length us, event | category | flops | bytes accessed | tf_op | source)
XLA Modules:
  0.0 96.8 jit_solution(10110916120950335854)
XLA Ops:
  0.6 1.6 %constant_dynamic-update-slice_fusion.19 = (bf16[768,2048]{1,0:T(8,128)(2,1)S(1)}, bf16[24,2048]{1,0:T(8,128)(2,1)}, bf16[24,2048]{1,0:T(8,128)(2,1)S(1)}) fusion(bf16[24,4096]{1,0:T(8,128)(2,1)} %param.5), kind=kLoop, calls=%fused_computation.26 | loop fusion | bytes 491520
  2.2 5.0 %collective-permute-start.7 = (bf16[24,2048]{1,0:T(8,128)(2,1)}, bf16[24,2048]{1,0:T(8,128)(2,1)S(1)}, u32[]{:S(2)}, u32[]{:S(2)}) collective-permute-start(bf16[24,2048]{1,0:T(8,128)(2,1)} %get-tuple-element.19), channel_id=1, source_target_pairs={{0,24},{8,0},{16,8},{24,16},{1,25},{9,1},{17,9},{25,17},{2,26},{10... | collective-permute-start | bytes 294920 | tf_op jit(solution)/shard_map/exchange_rows/ppermute | solution.py:225
  7.3 1.0 %collective-permute-start.5 = (bf16[24,2048]{1,0:T(8,128)(2,1)}, bf16[24,2048]{1,0:T(8,128)(2,1)S(1)}, u32[]{:S(2)}, u32[]{:S(2)}) collective-permute-start(bf16[24,2048]{1,0:T(8,128)(2,1)} %get-tuple-element.19), channel_id=1, source_target_pairs={{0,8},{8,16},{16,24},{24,0},{1,9},{9,17},{17,25},{25,1},{2,10},{10... | collective-permute-start | bytes 294920 | tf_op jit(solution)/shard_map/exchange_rows/ppermute | solution.py:225
  8.3 0.7 convert_element_type.5
  9.1 2.0 %collective-permute-start.1 = (bf16[24,2176]{1,0:T(8,128)(2,1)S(1)}, bf16[24,2176]{1,0:T(8,128)(2,1)S(1)}, u32[]{:S(2)}, u32[]{:S(2)}) collective-permute-start(bf16[24,2176]{1,0:T(8,128)(2,1)S(1)} %get-tuple-element.21), channel_id=1, source_target_pairs={{0,16},{8,24},{16,0},{24,8},{1,17},{9,25},{17,1},{25,9},{2,18},{10... | collective-permute-start | bytes 313352 | tf_op jit(solution)/shard_map/exchange_rows/ppermute | solution.py:225
  11.1 1.5 %collective-permute-start = (bf16[24,2176]{1,0:T(8,128)(2,1)S(1)}, bf16[24,2176]{1,0:T(8,128)(2,1)S(1)}, u32[]{:S(2)}, u32[]{:S(2)}) collective-permute-start(bf16[24,2176]{1,0:T(8,128)(2,1)S(1)} %get-tuple-element.21), channel_id=1, source_target_pairs={{0,8},{8,16},{16,24},{24,0},{1,9},{9,17},{17,25},{25,1},{2,10},{10... | collective-permute-start | bytes 313352 | tf_op jit(solution)/shard_map/exchange_rows/ppermute | solution.py:225
  12.6 1.3 %copy.11.refs_4_ = s32[4,6,64]{2,1,0:T(8,128)} copy(s32[4,6,64]{2,0,1:T(4,128)} %param.8) | data formatting | bytes 12288 | tf_op args[3]
  13.9 2.4 %collective-permute-start.2 = (bf16[24,2176]{1,0:T(8,128)(2,1)S(1)}, bf16[24,2176]{1,0:T(8,128)(2,1)S(1)}, u32[]{:S(2)}, u32[]{:S(2)}) collective-permute-start(bf16[24,2176]{1,0:T(8,128)(2,1)S(1)} %get-tuple-element.21), channel_id=1, source_target_pairs={{0,24},{8,0},{16,8},{24,16},{1,25},{9,1},{17,9},{25,17},{2,26},{10... | collective-permute-start | bytes 313352 | tf_op jit(solution)/shard_map/exchange_rows/ppermute | solution.py:225
  16.2 5.2 %collective-permute-done.6 = bf16[24,2048]{1,0:T(8,128)(2,1)S(1)} collective-permute-done((bf16[24,2048]{1,0:T(8,128)(2,1)}, bf16[24,2048]{1,0:T(8,128)(2,1)S(1)}, u32[]{:S(2)}, u32[]{:S(2)}) %collective-permute-start.6) | collective-permute-done | bytes 98336 | tf_op jit(solution)/shard_map/exchange_rows/ppermute | solution.py:225
  21.4 0.9 pad_maximum_fusion.3.refs_1_
  22.4 1.6 %collective-permute-start.13 = (bf16[96,2048]{1,0:T(8,128)(2,1)S(1)}, bf16[96,2048]{1,0:T(8,128)(2,1)S(1)}, u32[]{:S(2)}, u32[]{:S(2)}) collective-permute-start(bf16[96,2048]{1,0:T(8,128)(2,1)S(1)} %pad_maximum_fusion.3.refs_1_), channel_id=1, source_target_pairs={{0,4},{1,5},{2,6},{3,7},{4,0},{5,1},{6,2},{7,3},{8,12},{9,13},{10,... | collective-permute-start | bytes 1179656 | tf_op jit(solution)/shard_map/exchange_rows/ppermute | solution.py:218
  24.0 1.6 %collective-permute-start.12 = (bf16[96,2048]{1,0:T(8,128)(2,1)S(1)}, bf16[96,2048]{1,0:T(8,128)(2,1)S(1)}, u32[]{:S(2)}, u32[]{:S(2)}) collective-permute-start(bf16[96,2048]{1,0:T(8,128)(2,1)S(1)} %pad_maximum_fusion.3.refs_1_), channel_id=1, source_target_pairs={{0,2},{1,3},{2,0},{3,1},{4,6},{5,7},{6,4},{7,5},{8,10},{9,11},{10,... | collective-permute-start | bytes 1179656 | tf_op jit(solution)/shard_map/exchange_rows/ppermute | solution.py:218
  25.6 1.1 %collective-permute-start.4 = (bf16[96,2176]{1,0:T(8,128)(2,1)S(1)}, bf16[96,2176]{1,0:T(8,128)(2,1)S(1)}, u32[]{:S(2)}, u32[]{:S(2)}) collective-permute-start(bf16[96,2176]{1,0:T(8,128)(2,1)S(1)} %pad_maximum_fusion.2.refs_0_), channel_id=1, source_target_pairs={{0,4},{1,5},{2,6},{3,7},{4,0},{5,1},{6,2},{7,3},{8,12},{9,13},{10,... | collective-permute-start | bytes 1253384 | tf_op jit(solution)/shard_map/exchange_rows/ppermute | solution.py:218
  27.3 11.8 %load_weights.1 = (bf16[4,384,4096]{2,1,0:T(8,128)(2,1)S(1)}, f32[4,384,4096]{2,1,0:T(8,128)S(1)}, bf16[96,2176]{1,0:T(8,128)(2,1)S(1)}) custom-call(bf16[96,2176]{1,0:T(8,128)(2,1)S(1)} %pad_maximum_fusion.2.refs_0_, bf16[96,2048]{1,0:T(8,128)(2,1)S(1)} %pad_maximum_fusion.3.refs_1_, bf16[4,384,4096]{2,1,0:T(8,128)(2,1)} %refs_2_.1, f32[4,384,4096]{2,1,0:T(8,128)} %refs_3_.1), custom_call_target="tpu_custom_call" | custom-call | bytes 37748736 | tf_op jit(solution)/shard_map/load_weights/pallas_call | solution.py:52
  39.2 0.9 slice_multiply_fusion
  40.1 1.5 %collective-permute-start.14 = (bf16[96,2048]{1,0:T(8,128)(2,1)}, bf16[96,2048]{1,0:T(8,128)(2,1)}, u32[]{:S(2)}, u32[]{:S(2)}) collective-permute-start(bf16[96,2048]{1,0:T(8,128)(2,1)} %get-tuple-element.13), channel_id=1, source_target_pairs={{0,2},{1,3},{2,0},{3,1},{4,6},{5,7},{6,4},{7,5},{8,10},{9,11},{10,... | collective-permute-start | bytes 1179656 | tf_op jit(solution)/shard_map/exchange_rows/ppermute | solution.py:218
  41.7 3.3 %collective-permute-done.3 = bf16[96,2176]{1,0:T(8,128)(2,1)S(1)} collective-permute-done((bf16[96,2176]{1,0:T(8,128)(2,1)S(1)}, bf16[96,2176]{1,0:T(8,128)(2,1)S(1)}, u32[]{:S(2)}, u32[]{:S(2)}) %collective-permute-start.3) | collective-permute-done | bytes 417824 | tf_op jit(solution)/shard_map/exchange_rows/ppermute | solution.py:218
  45.3 1.1 %collective-permute-start.8 = (bf16[96,2176]{1,0:T(8,128)(2,1)S(1)}, bf16[96,2176]{1,0:T(8,128)(2,1)S(1)}, u32[]{:S(2)}, u32[]{:S(2)}) collective-permute-start(bf16[96,2176]{1,0:T(8,128)(2,1)S(1)} %get-tuple-element.15), channel_id=1, source_target_pairs={{0,4},{1,5},{2,6},{3,7},{4,0},{5,1},{6,2},{7,3},{8,12},{9,13},{10,... | collective-permute-start | bytes 1253384 | tf_op jit(solution)/shard_map/exchange_rows/ppermute | solution.py:218
  46.5 6.2 %collective-permute-done.14 = bf16[96,2048]{1,0:T(8,128)(2,1)} collective-permute-done((bf16[96,2048]{1,0:T(8,128)(2,1)}, bf16[96,2048]{1,0:T(8,128)(2,1)}, u32[]{:S(2)}, u32[]{:S(2)}) %collective-permute-start.14) | collective-permute-done | bytes 393248 | tf_op jit(solution)/shard_map/exchange_rows/ppermute | solution.py:218
  52.8 1.0 %constant_dynamic-update-slice_fusion.13 = bf16[768,2048]{1,0:T(8,128)(2,1)S(1)} fusion(bf16[768,2048]{1,0:T(8,128)(2,1)S(1)} %get-tuple-element.17, bf16[96,2048]{1,0:T(8,128)(2,1)} %collective-permute-done.14), kind=kLoop, calls=%fused_computation.20 | loop fusion | bytes 786432
  54.4 1.0 %constant_dynamic-update-slice_fusion.12 = bf16[768,2048]{1,0:T(8,128)(2,1)S(1)} fusion(bf16[768,2048]{1,0:T(8,128)(2,1)S(1)} %constant_dynamic-update-slice_fusion.13, bf16[96,2048]{1,0:T(8,128)(2,1)} %collective-permute-done.15), kind=kLoop, calls=%fused_computation.19 | loop fusion | bytes 786432
  55.4 1.9 %collective-permute-done.8 = bf16[96,2176]{1,0:T(8,128)(2,1)S(1)} collective-permute-done((bf16[96,2176]{1,0:T(8,128)(2,1)S(1)}, bf16[96,2176]{1,0:T(8,128)(2,1)S(1)}, u32[]{:S(2)}, u32[]{:S(2)}) %collective-permute-start.8) | collective-permute-done | bytes 417824 | tf_op jit(solution)/shard_map/exchange_rows/ppermute | solution.py:218
  57.7 1.4 %collective-permute-done.11 = bf16[96,2176]{1,0:T(8,128)(2,1)S(1)} collective-permute-done((bf16[96,2176]{1,0:T(8,128)(2,1)S(1)}, bf16[96,2176]{1,0:T(8,128)(2,1)S(1)}, u32[]{:S(2)}, u32[]{:S(2)}) %collective-permute-start.11) | collective-permute-done | bytes 417824 | tf_op jit(solution)/shard_map/exchange_rows/ppermute | solution.py:218
  59.2 37.6 %fused_iterations.1 = (f32[4,384,4096]{2,1,0:T(8,128)}, f32[4,384,4096]{2,1,0:T(8,128)}, f32[4,384,4096]{2,1,0:T(8,128)S(1)}) custom-call(bf16[768,2176]{1,0:T(8,128)(2,1)S(1)} %constant_dynamic-update-slice_fusion.refs_0_, bf16[768,2048]{1,0:T(8,128)(2,1)S(1)} %constant_dynamic-update-slice_fusion.10.refs_1_, ...), custom_call_target="tpu_custom_call", output_to_operand_aliasing={{2}: (3, {})} | custom-call | flops 19327352832 | bytes 50331648 | tf_op jit(solution)/shard_map/fused_iterations/pallas_call | solution.py:164
  (42 shorter events, 2.3 us)
Async XLA Ops:
  2.2 11.6 %collective-permute-start.7 = (bf16[24,2048]{1,0:T(8,128)(2,1)}, bf16[24,2048]{1,0:T(8,128)(2,1)S(1)}, u32[]{:S(2)}, u32[]{:S(2)}) collective-permute-start(bf16[24,2048]{1,0:T(8,128)(2,1)} %get-tuple-element.19), channel_id=1, source_target_pairs={{0,24},{8,0},{16,8},{24,16},{1,25},{9,1},{17,9},{25,17},{2,26},{10... | collective-permute-start | bytes 294920 | tf_op jit(solution)/shard_map/exchange_rows/ppermute | solution.py:225
  7.3 14.1 %collective-permute-start.6 = (bf16[24,2048]{1,0:T(8,128)(2,1)}, bf16[24,2048]{1,0:T(8,128)(2,1)S(1)}, u32[]{:S(2)}, u32[]{:S(2)}) collective-permute-start(bf16[24,2048]{1,0:T(8,128)(2,1)} %get-tuple-element.19), channel_id=1, source_target_pairs={{0,16},{8,24},{16,0},{24,8},{1,17},{9,25},{17,1},{25,9},{2,18},{10... | collective-permute-start | bytes 294920 | tf_op jit(solution)/shard_map/exchange_rows/ppermute | solution.py:225
  7.3 14.1 %collective-permute-start.5 = (bf16[24,2048]{1,0:T(8,128)(2,1)}, bf16[24,2048]{1,0:T(8,128)(2,1)S(1)}, u32[]{:S(2)}, u32[]{:S(2)}) collective-permute-start(bf16[24,2048]{1,0:T(8,128)(2,1)} %get-tuple-element.19), channel_id=1, source_target_pairs={{0,8},{8,16},{16,24},{24,0},{1,9},{9,17},{17,25},{25,1},{2,10},{10... | collective-permute-start | bytes 294920 | tf_op jit(solution)/shard_map/exchange_rows/ppermute | solution.py:225
  9.1 14.9 %collective-permute-start.1 = (bf16[24,2176]{1,0:T(8,128)(2,1)S(1)}, bf16[24,2176]{1,0:T(8,128)(2,1)S(1)}, u32[]{:S(2)}, u32[]{:S(2)}) collective-permute-start(bf16[24,2176]{1,0:T(8,128)(2,1)S(1)} %get-tuple-element.21), channel_id=1, source_target_pairs={{0,16},{8,24},{16,0},{24,8},{1,17},{9,25},{17,1},{25,9},{2,18},{10... | collective-permute-start | bytes 313352 | tf_op jit(solution)/shard_map/exchange_rows/ppermute | solution.py:225
  11.1 14.5 %collective-permute-start = (bf16[24,2176]{1,0:T(8,128)(2,1)S(1)}, bf16[24,2176]{1,0:T(8,128)(2,1)S(1)}, u32[]{:S(2)}, u32[]{:S(2)}) collective-permute-start(bf16[24,2176]{1,0:T(8,128)(2,1)S(1)} %get-tuple-element.21), channel_id=1, source_target_pairs={{0,8},{8,16},{16,24},{24,0},{1,9},{9,17},{17,25},{25,1},{2,10},{10... | collective-permute-start | bytes 313352 | tf_op jit(solution)/shard_map/exchange_rows/ppermute | solution.py:225
  13.9 11.7 %collective-permute-start.2 = (bf16[24,2176]{1,0:T(8,128)(2,1)S(1)}, bf16[24,2176]{1,0:T(8,128)(2,1)S(1)}, u32[]{:S(2)}, u32[]{:S(2)}) collective-permute-start(bf16[24,2176]{1,0:T(8,128)(2,1)S(1)} %get-tuple-element.21), channel_id=1, source_target_pairs={{0,24},{8,0},{16,8},{24,16},{1,25},{9,1},{17,9},{25,17},{2,26},{10... | collective-permute-start | bytes 313352 | tf_op jit(solution)/shard_map/exchange_rows/ppermute | solution.py:225
  22.3 31.5 %collective-permute-start.15 = (bf16[96,2048]{1,0:T(8,128)(2,1)S(1)}, bf16[96,2048]{1,0:T(8,128)(2,1)}, u32[]{:S(2)}, u32[]{:S(2)}) collective-permute-start(bf16[96,2048]{1,0:T(8,128)(2,1)S(1)} %pad_maximum_fusion.3.refs_1_), channel_id=1, source_target_pairs={{0,1},{1,0},{2,3},{3,2},{4,5},{5,4},{6,7},{7,6},{8,9},{9,8},{10,11... | collective-permute-start | bytes 1179656 | tf_op jit(solution)/shard_map/exchange_rows/ppermute | solution.py:218
  22.4 16.8 %collective-permute-start.13 = (bf16[96,2048]{1,0:T(8,128)(2,1)S(1)}, bf16[96,2048]{1,0:T(8,128)(2,1)S(1)}, u32[]{:S(2)}, u32[]{:S(2)}) collective-permute-start(bf16[96,2048]{1,0:T(8,128)(2,1)S(1)} %pad_maximum_fusion.3.refs_1_), channel_id=1, source_target_pairs={{0,4},{1,5},{2,6},{3,7},{4,0},{5,1},{6,2},{7,3},{8,12},{9,13},{10,... | collective-permute-start | bytes 1179656 | tf_op jit(solution)/shard_map/exchange_rows/ppermute | solution.py:218
  24.0 15.1 %collective-permute-start.12 = (bf16[96,2048]{1,0:T(8,128)(2,1)S(1)}, bf16[96,2048]{1,0:T(8,128)(2,1)S(1)}, u32[]{:S(2)}, u32[]{:S(2)}) collective-permute-start(bf16[96,2048]{1,0:T(8,128)(2,1)S(1)} %pad_maximum_fusion.3.refs_1_), channel_id=1, source_target_pairs={{0,2},{1,3},{2,0},{3,1},{4,6},{5,7},{6,4},{7,5},{8,10},{9,11},{10,... | collective-permute-start | bytes 1179656 | tf_op jit(solution)/shard_map/exchange_rows/ppermute | solution.py:218
  25.6 19.7 %collective-permute-start.4 = (bf16[96,2176]{1,0:T(8,128)(2,1)S(1)}, bf16[96,2176]{1,0:T(8,128)(2,1)S(1)}, u32[]{:S(2)}, u32[]{:S(2)}) collective-permute-start(bf16[96,2176]{1,0:T(8,128)(2,1)S(1)} %pad_maximum_fusion.2.refs_0_), channel_id=1, source_target_pairs={{0,4},{1,5},{2,6},{3,7},{4,0},{5,1},{6,2},{7,3},{8,12},{9,13},{10,... | collective-permute-start | bytes 1253384 | tf_op jit(solution)/shard_map/exchange_rows/ppermute | solution.py:218
  26.7 18.3 %collective-permute-start.3 = (bf16[96,2176]{1,0:T(8,128)(2,1)S(1)}, bf16[96,2176]{1,0:T(8,128)(2,1)S(1)}, u32[]{:S(2)}, u32[]{:S(2)}) collective-permute-start(bf16[96,2176]{1,0:T(8,128)(2,1)S(1)} %pad_maximum_fusion.2.refs_0_), channel_id=1, source_target_pairs={{0,2},{1,3},{2,0},{3,1},{4,6},{5,7},{6,4},{7,5},{8,10},{9,11},{10,... | collective-permute-start | bytes 1253384 | tf_op jit(solution)/shard_map/exchange_rows/ppermute | solution.py:218
  40.1 12.7 %collective-permute-start.14 = (bf16[96,2048]{1,0:T(8,128)(2,1)}, bf16[96,2048]{1,0:T(8,128)(2,1)}, u32[]{:S(2)}, u32[]{:S(2)}) collective-permute-start(bf16[96,2048]{1,0:T(8,128)(2,1)} %get-tuple-element.13), channel_id=1, source_target_pairs={{0,2},{1,3},{2,0},{3,1},{4,6},{5,7},{6,4},{7,5},{8,10},{9,11},{10,... | collective-permute-start | bytes 1179656 | tf_op jit(solution)/shard_map/exchange_rows/ppermute | solution.py:218
  41.6 15.8 %collective-permute-start.16 = (bf16[192,2048]{1,0:T(8,128)(2,1)S(1)}, bf16[192,2048]{1,0:T(8,128)(2,1)S(1)}, u32[]{:S(2)}, u32[]{:S(2)}) collective-permute-start(bf16[192,2048]{1,0:T(8,128)(2,1)S(1)} %pad_maximum_fusion.1), channel_id=1, source_target_pairs={{0,1},{1,0},{2,3},{3,2},{4,5},{5,4},{6,7},{7,6},{8,9},{9,8},{10,11... | collective-permute-start | bytes 2359304 | tf_op jit(solution)/shard_map/exchange_rows/ppermute | solution.py:218
  45.2 12.2 %collective-permute-start.9 = (bf16[96,2176]{1,0:T(8,128)(2,1)S(1)}, bf16[96,2176]{1,0:T(8,128)(2,1)S(1)}, u32[]{:S(2)}, u32[]{:S(2)}) collective-permute-start(bf16[96,2176]{1,0:T(8,128)(2,1)S(1)} %get-tuple-element.14), channel_id=1, source_target_pairs={{0,1},{1,0},{2,3},{3,2},{4,5},{5,4},{6,7},{7,6},{8,9},{9,8},{10,11... | collective-permute-start | bytes 1253384 | tf_op jit(solution)/shard_map/exchange_rows/ppermute | solution.py:218
  45.3 12.1 %collective-permute-start.8 = (bf16[96,2176]{1,0:T(8,128)(2,1)S(1)}, bf16[96,2176]{1,0:T(8,128)(2,1)S(1)}, u32[]{:S(2)}, u32[]{:S(2)}) collective-permute-start(bf16[96,2176]{1,0:T(8,128)(2,1)S(1)} %get-tuple-element.15), channel_id=1, source_target_pairs={{0,4},{1,5},{2,6},{3,7},{4,0},{5,1},{6,2},{7,3},{8,12},{9,13},{10,... | collective-permute-start | bytes 1253384 | tf_op jit(solution)/shard_map/exchange_rows/ppermute | solution.py:218
  52.8 4.8 %collective-permute-start.10 = (bf16[192,2176]{1,0:T(8,128)(2,1)S(1)}, bf16[192,2176]{1,0:T(8,128)(2,1)S(1)}, u32[]{:S(2)}, u32[]{:S(2)}) collective-permute-start(bf16[192,2176]{1,0:T(8,128)(2,1)S(1)} %pad_maximum_fusion), channel_id=1, source_target_pairs={{0,1},{1,0},{2,3},{3,2},{4,5},{5,4},{6,7},{7,6},{8,9},{9,8},{10,11... | collective-permute-start | bytes 2506760 | tf_op jit(solution)/shard_map/exchange_rows/ppermute | solution.py:218
  53.8 3.7 %collective-permute-start.17 = (bf16[96,2048]{1,0:T(8,128)(2,1)}, bf16[96,2048]{1,0:T(8,128)(2,1)S(1)}, u32[]{:S(2)}, u32[]{:S(2)}) collective-permute-start(bf16[96,2048]{1,0:T(8,128)(2,1)} %collective-permute-done.14), channel_id=1, source_target_pairs={{0,1},{1,0},{2,3},{3,2},{4,5},{5,4},{6,7},{7,6},{8,9},{9,8},{10,11... | collective-permute-start | bytes 1179656 | tf_op jit(solution)/shard_map/exchange_rows/ppermute | solution.py:218
  57.4 1.8 %collective-permute-start.11 = (bf16[96,2176]{1,0:T(8,128)(2,1)S(1)}, bf16[96,2176]{1,0:T(8,128)(2,1)S(1)}, u32[]{:S(2)}, u32[]{:S(2)}) collective-permute-start(bf16[96,2176]{1,0:T(8,128)(2,1)S(1)} %collective-permute-done.8), channel_id=1, source_target_pairs={{0,1},{1,0},{2,3},{3,2},{4,5},{5,4},{6,7},{7,6},{8,9},{9,8},{10,11... | collective-permute-start | bytes 1253384 | tf_op jit(solution)/shard_map/exchange_rows/ppermute | solution.py:218
